TPU v7x, 32 devices: a whole 2x2x4 slice. The times are simulated.
32 devices in a mesh: blk: 8 (over z, y), line: 4 (over x, core).
Axes of the slice: x: 2, y: 2, z: 4, core: 2. Of those that a mesh axis runs over, the one named last changes fastest.
Arguments:
- flow_state: float32 [8, 5, 512, 512], P('blk', None, 'line'), may hold values from -6 to 6
- block_owner: int32 [8], replicated, may hold values from 0 to 7, each once
- link_block: int32 [8, 2], replicated, may hold values from 0 to 7, as said below
- link_side: int32 [8, 2], replicated, may hold values from 0 to 1
- rows_live: int32 [8], replicated, may hold values from 256 to 512, as said below
- x_operator: float32 [512, 1024], replicated, may hold values from -0.25 to 0.25
- ghost_operator: float32 [6, 1024], replicated, may hold values from -1.25 to 1.25
- y_operator: float32 [512, 1024], replicated, may hold values from -0.25 to 0.25
- coefficients: float32 [7], replicated, may hold values from 0.2 to 1
Outputs:
- next_state: float32 [8, 5, 512, 512], P('blk', None, 'line')
Inputs may be any that keep to these rules, and one draw needn't show every extreme that they name: link_block and link_side join the blocks' faces in pairs: if face m of block b meets face s of block c, then face s of block c meets face m of block b; no block meets itself. `rows_live`: some block has all 512 lines.
All inputs are finite; a program needn't handle non-finite values.
Results may differ from a plain program's by a relative error of at most 0.0003.
Values sent between devices are 32-bit elements; how exact they have to be, the bound alone decides.
No kernel may reach another device: no remote copies, remote signals or barrier semaphores. Data moves between devices by JAX's collectives and lax.ppermute only.
A program may use at most 64 MiB of HBM per device.

v0:
```python
import jax
import jax.numpy as jnp
from jax import lax
from jax.sharding import PartitionSpec as P

GHOST = 3


highest = lax.Precision.HIGHEST
section_step = 0.3


def on_device(
    flow_state,
    block_owner,
    link_block,
    link_side,
    rows_live,
    x_operator,
    ghost_operator,
    y_operator,
    coefficients,
):
    values = flow_state[0]
    var_count, rows_here, x_length = values.shape
    my_slot = lax.axis_index("blk")
    line_pos = lax.axis_index("line")
    block_count = block_owner.shape[0]
    numbers = jnp.arange(block_count, dtype=jnp.int32)
    my_block = jnp.sum(numbers * (block_owner == my_slot).astype(jnp.int32))
    block_pick = (numbers == my_block).astype(jnp.int32)
    live_rows = jnp.sum(rows_live * block_pick)
    y_index = line_pos * rows_here + jnp.arange(rows_here, dtype=jnp.int32)
    live_mask = (y_index < live_rows).astype(jnp.float32)
    masked = values * live_mask[None, :, None]
    low_planes = jnp.swapaxes(masked[:, :, :GHOST], 1, 2)
    high_planes = jnp.swapaxes(masked[:, :, x_length - GHOST :], 1, 2)
    face_planes = jnp.stack([low_planes, high_planes], axis=1)[None]
    neighbours = jnp.sum(link_block * block_pick[:, None], axis=0)
    their_sides = jnp.sum(link_side * block_pick[:, None], axis=0)
    sources = jnp.sum(
        block_owner[None, :] * (numbers[None, :] == neighbours[:, None]).astype(jnp.int32), axis=1
    )
    shard_piece = lax.all_gather(face_planes, "blk", axis=0, tiled=True)
    row_ids = jnp.arange(shard_piece.shape[0], dtype=jnp.int32)
    select = (row_ids[None, :] == sources[:, None]).astype(jnp.float32)
    received = jnp.einsum("mn,nvsgy->mvsgy", select, shard_piece, precision=highest)
    flip_sign = jnp.array([-1.0, 1.0, 1.0, 1.0, 1.0], jnp.float32)[:, None, None]
    side_ghosts = []
    for my_side in range(2):
        far_side = their_sides[my_side]
        chosen = jnp.where(far_side == 0, received[my_side, :, 0], received[my_side, :, 1])
        side_ghosts.append(jnp.where(far_side == my_side, chosen[:, ::-1] * flip_sign, chosen))
    ghost_planes = jnp.concatenate(side_ghosts, axis=1)
    nu_values = coefficients[:var_count][:, None, None]
    x_parts = jnp.einsum("vyx,xk->vyk", masked, x_operator, precision=highest)
    x_parts = x_parts + jnp.einsum("vgy,gk->vyk", ghost_planes, ghost_operator, precision=highest)
    x_term = -masked[0][None] * x_parts[..., :x_length] + nu_values * x_parts[..., x_length:]
    columns = lax.all_to_all(masked, "line", split_axis=2, concat_axis=1, tiled=True)
    y_full = columns.shape[1]
    y_parts = jnp.einsum("vyx,yk->vxk", columns, y_operator, precision=highest)
    v_columns = jnp.swapaxes(columns[1], 0, 1)
    y_cols_term = -v_columns[None] * y_parts[..., :y_full] + nu_values * y_parts[..., y_full:]
    y_rows = lax.all_to_all(y_cols_term, "line", split_axis=2, concat_axis=1, tiled=True)
    y_term = jnp.swapaxes(y_rows, 1, 2)
    buoyancy = coefficients[var_count] * masked[3] + coefficients[var_count + 1] * masked[4]
    picker = (jnp.arange(var_count) == 1).astype(jnp.float32)[:, None, None]
    rhs_terms = x_term + y_term + picker * buoyancy[None]
    result = (masked + section_step * rhs_terms) * live_mask[None, :, None]
    return result[None]


def solution(mesh):
    return jax.shard_map(
        on_device,
        mesh=mesh,
        in_specs=(P("blk", None, "line", None), P(), P(), P(), P(), P(), P(), P(), P()),
        out_specs=P("blk", None, "line", None),
        check_vma=False,
    )
```

profile of v0, /device:TPU:0, one launch (start us, length us, event | category | flops | bytes accessed | tf_op | source)
XLA Modules:
  0.0 113.0 jit_solution(14717906404956709978)
XLA Ops:
  0.0 0.0 copy-start
  0.0 1.4 %fusion.31 = s32[]{:T(128)} fusion(s32[8]{0:T(128)} %param.11, s32[]{:T(128)S(6)} %axis_index.25), kind=kLoop, calls=%fused_computation.55 | loop fusion | flops 23 | bytes 40 | tf_op jit(solution)/shard_map/reduce_sum | solution.py:30
  1.4 1.9 %fusion.30 = s32[]{:T(128)} fusion(s32[8]{0:T(128)} %param.14, s32[]{:T(128)} %fusion.31), kind=kLoop, calls=%fused_computation.54 | loop fusion | flops 23 | bytes 40 | tf_op jit(solution)/shard_map/reduce_sum | solution.py:32
  3.4 0.6 compare_convert_fusion.1
  3.9 1.5 %bitcast_multiply_fusion = f32[5,128,512]{2,1,0:T(8,128)S(1)} fusion(f32[1,5,128,512]{3,2,1,0:T(8,128)} %param.10, f32[128]{0:T(128)S(1)} %compare_convert_fusion.1), kind=kLoop, calls=%fused_computation.17 | loop fusion | flops 327680 | bytes 2621952 | tf_op jit(solution)/shard_map/mul | solution.py:35
  5.4 1.8 %copy.61 = f32[5,128,512]{1,0,2:T(8,128)} copy(f32[5,128,512]{2,1,0:T(8,128)S(1)} %bitcast_multiply_fusion) | data formatting | bytes 2621440 | tf_op jit(solution)/shard_map/mul | solution.py:35
  7.2 4.4 %all-to-all-start = ((f32[5,128,512]{1,0,2:T(8,128)}), f32[5,128,512]{1,0,2:T(8,128)}, u32[]{:S(2)}, u32[]{:S(2)}) async-start(f32[5,128,512]{1,0,2:T(8,128)} %copy.61), calls=%async_computation | async-start | bytes 4194304 | tf_op jit(solution)/shard_map/all_to_all | solution.py:59
  11.6 0.0 copy-start.5
  11.7 0.0 copy-start.6
  11.7 0.0 copy-start.8
  11.7 0.0 copy-start.4
  11.7 0.0 copy-start.7
  11.7 0.7 compare_convert_fusion.2
  12.4 0.9 slice_bitcast_fusion.1
  13.3 0.0 copy-done.5
  13.3 0.0 copy-done.6
  13.3 0.1 multiply_reduce_fusion
  13.4 0.0 copy-done.8
  13.5 0.2 fusion.28
  13.6 0.6 fusion.36
  16.2 1.1 copy.56
  17.3 1.1 copy.57
  18.4 32.4 %all-gather = f32[40,2,3,128]{3,1,2,0:T(2,128)S(1)} all-gather(f32[5,2,3,128]{3,1,2,0:T(2,128)S(1)} %pad_maximum_fusion), channel_id=2, replica_groups=mesh['blk'=8,'line'=4] {'blk'}, dimensions={0}, use_global_device_ids=true | all-gather | bytes 138240 | tf_op jit(solution)/shard_map/all_gather | solution.py:44
  50.8 0.3 fusion.18
  51.2 0.0 copy-done.4
  51.2 0.6 fusion.35
  51.8 0.0 copy-done.7
  51.8 0.1 multiply_select_fusion.1
  51.9 0.0 all-to-all-done
  51.9 3.5 %copy.65 = f32[5,4,128,128]{2,1,3,0:T(4,128)} copy(f32[5,4,128,128]{2,0,3,1:T(8,128)} %bitcast.20) | data formatting | bytes 2621440 | tf_op jit(solution)/shard_map/all_to_all | solution.py:59
  55.4 2.7 %all_to_all.29 = f32[5,512,128]{1,2,0:T(8,128)} reshape(f32[5,4,128,128]{2,1,3,0:T(4,128)} %copy.65) | data formatting | bytes 2621440 | tf_op jit(solution)/shard_map/all_to_all | solution.py:59
  58.1 1.8 %copy.62 = f32[5,128,512]{1,2,0:T(8,128)S(1)} copy(f32[5,128,512]{1,0,2:T(8,128)} %all-to-all-done) | data formatting | bytes 2621440 | tf_op jit(solution)/shard_map/all_to_all | solution.py:59
  60.0 0.7 slice_negate_fusion
  60.7 1.8 %copy.63 = f32[1,4,128,128]{3,2,1,0:T(8,128)} copy(f32[1,4,128,128]{2,3,1,0:T(8,128)} %slice_negate_fusion) | data formatting | bytes 524288 | tf_op jit(solution)/shard_map/neg | solution.py:63
  62.5 1.8 %copy.64 = f32[128,512]{1,0:T(8,128)} copy(f32[128,512]{0,1:T(8,128)} %bitcast.69) | data formatting | bytes 524288 | tf_op jit(solution)/shard_map/neg | solution.py:63
  64.2 0.0 copy-done
  64.2 0.0 copy-start.2
  64.2 5.8 %fusion = f32[5,128,1024]{2,1,0:T(8,128)S(1)} fusion(f32[5,512,128]{1,2,0:T(8,128)} %all_to_all.29, f32[512,1024]{1,0:T(8,128)S(1)} %copy-done), kind=kOutput, calls=%fused_computation | convolution fusion | flops 4026531840 | bytes 6029312 | tf_op jit(solution)/shard_map/vyx,yk->vxk/dot_general | solution.py:61
  70.1 0.0 copy-done.2
  70.1 1.4 %fusion.7 = f32[5,128,512]{2,1,0:T(8,128)} fusion(f32[5,128,1024]{2,1,0:T(8,128)S(1)} %fusion, f32[128,512]{1,0:T(8,128)S(1)} %copy-done.2, f32[5]{0:T(128)S(1)} %bitcast.72), kind=kLoop, calls=%fused_computation.6 | loop fusion | flops 983040 | bytes 4194324 | tf_op jit(solution)/shard_map/add | solution.py:63
  71.5 2.8 %copy.66 = f32[5,128,512]{1,0,2:T(8,128)} copy(f32[5,128,512]{2,1,0:T(8,128)} %fusion.7) | data formatting | bytes 2621440 | tf_op jit(solution)/shard_map/add | solution.py:63
  74.3 4.6 %all-to-all-start.1 = ((f32[5,128,512]{1,0,2:T(8,128)}), f32[5,128,512]{1,0,2:T(8,128)}, u32[]{:S(2)}, u32[]{:S(2)}) async-start(f32[5,128,512]{1,0,2:T(8,128)} %copy.66), calls=%async_computation.1 | async-start | bytes 4194304 | tf_op jit(solution)/shard_map/all_to_all | solution.py:64
  78.9 0.0 copy-start.3
  79.0 2.1 %fusion.17 = (f32[128,512]{1,0:T(8,128)}, f32[128,512]{1,0:T(8,128)}) fusion(f32[5,128,512]{2,1,0:T(8,128)S(1)} %bitcast_multiply_fusion, f32[]{:T(128)} %bitcast.26, f32[]{:T(128)} %bitcast.25), kind=kLoop, calls=%fused_computation.27 | loop fusion | flops 262144 | bytes 1310728 | tf_op jit(solution)/shard_map/mul | solution.py:58
  81.1 0.0 copy-done.3
  81.1 0.0 copy-start.1
  81.1 2.3 %fusion.20 = f32[5,128,1024]{2,1,0:T(8,128)S(1)} fusion(f32[6,1024]{1,0:T(8,128)S(1)} %copy-done.3, f32[5,3,128]{2,1,0:T(4,128)S(1)} %get-tuple-element.17, f32[5,3,128]{2,1,0:T(4,128)S(1)} %get-tuple-element.16), kind=kOutput, calls=%fused_computation.30 | convolution fusion | flops 47189760 | bytes 2661376 | tf_op jit(solution)/shard_map/vgy,gk->vyk/dot_general | solution.py:57
  83.4 0.0 copy-done.1
  83.4 6.0 %fusion.4 = f32[5,128,1024]{2,1,0:T(8,128)} fusion(f32[5,128,1024]{2,1,0:T(8,128)S(1)} %fusion.20, f32[5,128,512]{2,1,0:T(8,128)S(1)} %bitcast_multiply_fusion, f32[512,1024]{1,0:T(8,128)S(1)} %copy-done.1), kind=kOutput, calls=%fused_computation.4 | convolution fusion | flops 4027187200 | bytes 8650752 | tf_op jit(solution)/shard_map/vyx,xk->vyk/dot_general | solution.py:56
  89.3 15.2 %all-to-all-done.1 = f32[5,128,512]{1,0,2:T(8,128)} async-done(((f32[5,128,512]{1,0,2:T(8,128)}), f32[5,128,512]{1,0,2:T(8,128)}, u32[]{:S(2)}, u32[]{:S(2)}) %all-to-all-start.1) | async-done | bytes 1310752 | tf_op jit(solution)/shard_map/all_to_all | solution.py:64
  104.5 2.4 %copy.83 = f32[5,128,4,128]{1,2,3,0:T(4,128)S(1)} copy(f32[5,128,4,128]{1,0,3,2:T(8,128)} %bitcast.22) | data formatting | bytes 2621440 | tf_op jit(solution)/shard_map/all_to_all | solution.py:64
  107.0 1.6 %all_to_all.33 = f32[5,512,128]{1,2,0:T(8,128)} reshape(f32[5,4,128,128]{2,1,3,0:T(4,128)S(1)} %bitcast.67) | data formatting | bytes 2621440 | tf_op jit(solution)/shard_map/all_to_all | solution.py:64
  108.5 4.5 %fusion.14 = f32[1,5,128,512]{3,2,1,0:T(8,128)} fusion(f32[5,128,1024]{2,1,0:T(8,128)} %fusion.4, f32[5,512,128]{1,2,0:T(8,128)} %all_to_all.33, f32[128,512]{1,0:T(8,128)} %get-tuple-element.8, f32[5]{0:T(128)S(1)} %compare_convert_fusion, f32[5]{0:T(128)S(1)} %bitcast.73, f32[128,512]{1,0:T(8,128)} %get-tuple-element.7, f32[128]{0:T(128)S(1)} %compare_convert_fusion.1, ...), kind=kLoop, calls=%fused_computation.15 | loop fusion | flops 3276800 | bytes 7078440 | tf_op jit(solution)/shard_map/broadcast_in_dim | solution.py:70
  (7 shorter events, 0.1 us)
Async XLA Ops:
  0.0 64.2 %copy-start = (f32[512,1024]{1,0:T(8,128)S(1)}, f32[512,1024]{1,0:T(8,128)}, u32[]{:S(2)}) copy-start(f32[512,1024]{1,0:T(8,128)} %param.17) | copy-start | bytes 6291460
  7.2 44.7 %all-to-all-start = ((f32[5,128,512]{1,0,2:T(8,128)}), f32[5,128,512]{1,0,2:T(8,128)}, u32[]{:S(2)}, u32[]{:S(2)}) async-start(f32[5,128,512]{1,0,2:T(8,128)} %copy.61), calls=%async_computation | async-start | bytes 4194304 | tf_op jit(solution)/shard_map/all_to_all | solution.py:59
  11.6 1.7 %copy-start.5 = (s32[8,2]{0,1:T(2,128)S(1)}, s32[8,2]{0,1:T(2,128)}, u32[]{:S(2)}) copy-start(s32[8,2]{0,1:T(2,128)} %param.12) | copy-start | bytes 196
  11.7 1.6 %copy-start.6 = (s32[8,2]{0,1:T(2,128)S(1)}, s32[8,2]{0,1:T(2,128)}, u32[]{:S(2)}) copy-start(s32[8,2]{0,1:T(2,128)} %param.13) | copy-start | bytes 196
  11.7 1.8 %copy-start.8 = (s32[8]{0:T(128)S(1)}, s32[8]{0:T(128)}, u32[]{:S(2)}) copy-start(s32[8]{0:T(128)} %param.11) | copy-start | bytes 100
  11.7 39.5 %copy-start.4 = (f32[7]{0:T(128)S(1)}, f32[7]{0:T(128)}, u32[]{:S(2)}) copy-start(f32[7]{0:T(128)} %param.18) | copy-start | bytes 88
  11.7 40.1 %copy-start.7 = (f32[5]{0:T(128)S(1)}, f32[5]{0:T(128)}, u32[]{:S(2)}) copy-start(f32[5]{0:T(128)} %constant.28.clone) | copy-start | bytes 64
  64.2 5.8 %copy-start.2 = (f32[128,512]{1,0:T(8,128)S(1)}, f32[128,512]{1,0:T(8,128)}, u32[]{:S(2)}) copy-start(f32[128,512]{1,0:T(8,128)} %copy.64) | copy-start | bytes 786436
  74.3 30.2 %all-to-all-start.1 = ((f32[5,128,512]{1,0,2:T(8,128)}), f32[5,128,512]{1,0,2:T(8,128)}, u32[]{:S(2)}, u32[]{:S(2)}) async-start(f32[5,128,512]{1,0,2:T(8,128)} %copy.66), calls=%async_computation.1 | async-start | bytes 4194304 | tf_op jit(solution)/shard_map/all_to_all | solution.py:64
  78.9 2.1 %copy-start.3 = (f32[6,1024]{1,0:T(8,128)S(1)}, f32[6,1024]{1,0:T(8,128)}, u32[]{:S(2)}) copy-start(f32[6,1024]{1,0:T(8,128)} %param.16) | copy-start | bytes 73732
  81.1 2.3 %copy-start.1 = (f32[512,1024]{1,0:T(8,128)S(1)}, f32[512,1024]{1,0:T(8,128)}, u32[]{:S(2)}) copy-start(f32[512,1024]{1,0:T(8,128)} %param.15) | copy-start | bytes 6291460
where the time goes:
time: 114 us; the launch traced here: 113 us
  blocking collectives  32.4 us (28%)
  local copies, waits for them, and re-layouts  24.7 us (22%)
  other arithmetic  15.3 us (13%)
  waiting for transfers between devices  15.2 us (13%)
  matrix products  14.3 us (13%)
  starting transfers between devices  9.07 us (8%)
  between operations  2.09 us (2%)
    all_gather x1, blocking collectives, on_device(): shard_piece = lax.all_gather(face_planes, 'blk', axis=0, tiled=True)  32.4 us
    all_to_all x1, waiting for transfers between devices, on_device(): lax.all_to_all(y_cols_term, 'line', split_axis=2, concat_axis=1, tiled=True)  15.2 us
    all_to_all x3, local copies, waits for them, and re-layouts, on_device(): lax.all_to_all(masked, 'line', split_axis=2, concat_axis=1, tiled=True)  8.05 us
    dot_general x1, matrix products, on_device(): x_parts = jnp.einsum('vyx,xk->vyk', masked, x_operator, precision=highest)  5.97 us
    dot_general x1, matrix products, on_device(): y_parts = jnp.einsum('vyx,yk->vxk', columns, y_operator, precision=highest)  5.81 us
    all_to_all x1, starting transfers between devices, on_device(): lax.all_to_all(y_cols_term, 'line', split_axis=2, concat_axis=1, tiled=True)  4.63 us
    broadcast_in_dim x1, other arithmetic, on_device(): return result[None]  4.48 us
    all_to_all x1, starting transfers between devices, on_device(): lax.all_to_all(masked, 'line', split_axis=2, concat_axis=1, tiled=True)  4.44 us
  transfers between devices with their start and end apart: 2, of which 1 were waited for; matrix products, arithmetic and copies ran while one was open for 14% of the time, Pallas kernels for 0%

commit v1 on v0

v1 whole, which is shorter than its diff:
```python
import functools

import jax
import jax.numpy as jnp
from jax import lax
from jax.experimental import pallas as pl
from jax.experimental.pallas import tpu as pltpu
from jax.sharding import PartitionSpec as P

GHOST = 3
SECTION_STEP = 0.3
FACE_ROWS = 16
TILE = 256
LANES = 128
FIRST, SECOND = (1, 3), (3, 4)
RAW = tuple(range(FIRST[0], SECOND[1]))
SENT = (0, 4)

SMEM = pltpu.MemorySpace.SMEM
VMEM = pltpu.MemorySpace.VMEM
HBM = pltpu.MemorySpace.HBM


def split_bf16(x):
    hi = x.astype(jnp.bfloat16)
    lo = (x - hi.astype(jnp.float32)).astype(jnp.bfloat16)
    return hi, lo


def dot(a, b):
    return jnp.dot(a, b, preferred_element_type=jnp.float32)


def three_parts(pieces):
    split = [split_bf16(piece) for piece in pieces]
    hi = [s[0] for s in split]
    lo = [s[1] for s in split]
    return jnp.concatenate(hi + hi + lo, axis=0)


def find_block(owner_ref, my_slot):
    return lax.fori_loop(
        0, owner_ref.shape[0], lambda i, found: jnp.where(owner_ref[i] == my_slot, i, found), 0
    )


def faces_kernel(owner_ref, rows_ref, low_ref, high_ref, out_ref):
    nvar, rows, lanes = low_ref.shape[1:]
    live_rows = rows_ref[find_block(owner_ref, lax.axis_index("blk"))]
    y_index = lax.axis_index("line") * rows + lax.broadcasted_iota(jnp.int32, (GHOST, rows), 1)
    live = y_index < live_rows
    for v in range(nvar):
        low = jnp.transpose(low_ref[0, v])[:GHOST]
        high = jnp.transpose(high_ref[0, v])[lanes - GHOST :]
        out_ref[0, 0, GHOST * v : GHOST * (v + 1), :] = jnp.where(live, low, 0.0)
        out_ref[0, 1, GHOST * v : GHOST * (v + 1), :] = jnp.where(live, high, 0.0)
    for m in range(2):
        out_ref[0, m, GHOST * nvar :, :] = jnp.zeros((FACE_ROWS - GHOST * nvar, rows), jnp.float32)


def part_kernel(low, q_ref, out_ref, sem):
    copy = pltpu.make_async_copy(q_ref.at[:, low : low + out_ref.shape[1]], out_ref, sem)
    copy.start()
    copy.wait()


def weights_kernel(
    lines,
    owner_ref,
    rows_ref,
    coef_ref,
    yop_ref,
    wown_ref,
    wnear_ref,
    wdirect_ref,
    wpassed_ref,
    wsend_ref,
    nu_ref,
    columns_ref,
    turned_ref,
    theirs_ref,
    pieces_hi_ref,
    pieces_lo_ref,
    sems,
):
    y_length = yop_ref.shape[0]
    rows = y_length // lines
    line_pos = lax.axis_index("line")
    other = jnp.bitwise_xor(line_pos, 1)
    shifts = range(2, lines, 2)
    targets = [lax.rem(line_pos + s, lines) for s in shifts]

    def column(d, line):
        return pl.ds(pl.multiple_of(d * y_length + (line * rows) // LANES * LANES, LANES), LANES)

    copies = []
    for d in range(2):
        source = yop_ref.at[:, column(d, line_pos)]
        copies.append(pltpu.make_async_copy(source, columns_ref.at[d], sems.at[d]))
    for j, target in enumerate(targets):
        for d in range(2):
            for i, line in enumerate((line_pos, other)):
                source = yop_ref.at[pl.ds(pl.multiple_of(line * rows, 8), rows), column(d, target)]
                goal = theirs_ref.at[j, d, i * rows : (i + 1) * rows]
                copies.append(pltpu.make_async_copy(source, goal, sems.at[len(copies)]))
    for copy in copies:
        copy.start()

    live_rows = rows_ref[find_block(owner_ref, lax.axis_index("blk"))]
    for v in range(nu_ref.shape[0]):
        nu_ref[v] = jnp.full(nu_ref.shape[1:], coef_ref[v], jnp.float32)
    for copy in copies:
        copy.wait()

    shape = (rows, y_length)
    live_in = lax.broadcasted_iota(jnp.int32, shape, 1) < live_rows
    live_out = line_pos * rows + lax.broadcasted_iota(jnp.int32, shape, 0) < live_rows
    offset = pl.multiple_of(lax.rem(line_pos * rows, LANES), 8)
    for d in range(2):
        turned_ref[d] = jnp.transpose(columns_ref[d])
        mine = turned_ref[d, pl.ds(offset, rows), :]
        hi, lo = split_bf16(jnp.where(live_in & live_out, SECTION_STEP * mine, 0.0))
        for p in range(lines):
            pieces_hi_ref[p, d * rows : (d + 1) * rows] = hi[:, p * rows : (p + 1) * rows]
            pieces_lo_ref[p, d * rows : (d + 1) * rows] = lo[:, p * rows : (p + 1) * rows]

    def gather(ref, places):
        hi = [pieces_hi_ref[p] for p in places]
        lo = [pieces_lo_ref[p] for p in places]
        ref[...] = jnp.concatenate(hi + lo + hi, axis=1)

    gather(wown_ref, [line_pos])
    gather(wnear_ref, [other])
    gather(wdirect_ref, [lax.rem(line_pos + lines - s, lines) for s in shifts])
    gather(wpassed_ref, [lax.rem(other + lines - s, lines) for s in shifts])

    shape = (rows, rows)
    ins = [line * rows + lax.broadcasted_iota(jnp.int32, shape, 1) for line in (line_pos, other)]
    live_in = jnp.concatenate(ins, axis=1) < live_rows
    for j, target in enumerate(targets):
        live_out = target * rows + lax.broadcasted_iota(jnp.int32, live_in.shape, 0) < live_rows
        offset = pl.multiple_of(lax.rem(target * rows, LANES), 8)
        for d in range(2):
            turned_ref[d, :, : 2 * rows] = jnp.transpose(theirs_ref[j, d])
            mine = turned_ref[d, pl.ds(offset, rows), : 2 * rows]
            hi, lo = split_bf16(jnp.where(live_in & live_out, SECTION_STEP * mine, 0.0))
            wsend_ref[j, d * rows : (d + 1) * rows] = jnp.concatenate([hi, lo, hi], axis=1)


def own_kernel(
    owner_ref,
    rows_ref,
    coef_ref,
    wown_ref,
    q_ref,
    tile_ref,
    dx_ref,
    dxx_ref,
    out_ref,
    hi_ref,
    lo_ref,
):
    nvar, rows, _ = q_ref.shape[1:]
    live_rows = rows_ref[find_block(owner_ref, lax.axis_index("blk"))]

    @pl.when(pl.program_id(0) == 0)
    def _():
        for v in range(nvar):
            hi, lo = split_bf16(q_ref[0, v])
            hi_ref[v * rows : (v + 1) * rows] = hi
            lo_ref[v * rows : (v + 1) * rows] = lo

    def derivative(op_ref):
        hi, lo = split_bf16(op_ref[...])
        return dot(hi_ref[...], hi) + dot(lo_ref[...], hi) + dot(hi_ref[...], lo)

    dx = derivative(dx_ref)
    dxx = derivative(dxx_ref)
    u, w = tile_ref[0, 0], tile_ref[0, 1]
    live = lax.axis_index("line") * rows + lax.broadcasted_iota(jnp.int32, u.shape, 0) < live_rows
    for v in range(nvar):
        here = slice(v * rows, (v + 1) * rows)
        dy = dot(wown_ref[...], three_parts([tile_ref[0, v]]))
        rhs = coef_ref[v] * dxx[here] - u * dx[here]
        if v == 1:
            rhs = rhs + coef_ref[nvar] * tile_ref[0, 3] + coef_ref[nvar + 1] * tile_ref[0, 4]
        value = jnp.where(live, tile_ref[0, v] + SECTION_STEP * rhs, 0.0)
        out_ref[0, v] = value + coef_ref[v] * dy[rows:] - w * dy[:rows]


def near_kernel(
    face_count,
    owner_ref,
    link_ref,
    side_ref,
    rows_ref,
    gop_ref,
    wnear_ref,
    nu_ref,
    q_ref,
    base_ref,
    near_raw_ref,
    *refs,
):
    near_sent, refs = refs[0], refs[1:]
    faces, (out_ref, left_ref, done_ref, sems) = refs[:face_count], refs[face_count:]
    near = {v: near_sent.at[0, i] for i, v in enumerate(SENT)}
    near.update({v: near_raw_ref.at[0, i] for i, v in enumerate(RAW)})
    nvar, rows, x_length = q_ref.shape[1:]
    my_slot = lax.axis_index("blk")
    my_block = find_block(owner_ref, my_slot)
    sides = [side_ref[m, my_block] for m in range(2)]
    live_rows = rows_ref[my_block]
    y_index = lax.axis_index("line") * rows + lax.broadcasted_iota(jnp.int32, (FACE_ROWS, rows), 1)
    scale = jnp.where(y_index < live_rows, SECTION_STEP, 0.0)

    planes = []
    for m in range(2):
        place = jnp.bitwise_xor(owner_ref[link_ref[m, my_block]], my_slot)
        plane, first = faces[0][0, sides[m]], 1
        for ref in faces[1:]:
            count = ref.shape[0]
            at = jnp.clip(place - first, 0, count - 1)
            plane = jnp.where(place >= first, ref[at, sides[m]], plane)
            first += count
        planes.append(plane * scale)

    def ghost_rows(g):
        parts = []
        for m in range(2):
            straight = g[GHOST * m : GHOST * (m + 1)]
            turned = jnp.concatenate([straight[2:3], straight[1:2], straight[0:1]], axis=0)
            parts.append(jnp.where(sides[m] == m, turned, straight))
        hi, lo = split_bf16(jnp.concatenate(parts, axis=0))
        pad = jnp.zeros((LANES - 6 * GHOST, hi.shape[1]), jnp.float32)
        stacked = [hi.astype(jnp.float32), hi.astype(jnp.float32), lo.astype(jnp.float32)]
        return jnp.concatenate(stacked + [pad], axis=0).astype(jnp.bfloat16)

    operator = ghost_rows(gop_ref[...])
    pad = jnp.zeros((LANES - 6 * GHOST, rows), jnp.float32)
    copies = []
    for v in RAW + SENT:
        parts = []
        for m in range(2):
            part = planes[m][GHOST * v : GHOST * (v + 1)]
            if v == 0:
                part = jnp.where(sides[m] == m, -part, part)
            parts.append(part)
        hi, lo = split_bf16(jnp.concatenate(parts, axis=0))
        stacked = [hi.astype(jnp.float32), lo.astype(jnp.float32), hi.astype(jnp.float32)]
        ghost = jnp.transpose(jnp.concatenate(stacked + [pad], axis=0)).astype(jnp.bfloat16)
        dx = dot(ghost, operator)
        dy = dot(wnear_ref[...], three_parts([near[v][...]]))
        second = nu_ref[v, 0:1] * (dx[:, x_length:] + dy[rows:])
        value = base_ref[0, v] + second - q_ref[0, 0] * dx[:, :x_length] - q_ref[0, 1] * dy[:rows]
        if v in SENT:
            left_ref[0, SENT.index(v)] = value
            continue
        i = RAW.index(v)
        done_ref[i] = value
        copies.append(pltpu.make_async_copy(done_ref.at[i], out_ref.at[0, v], sems.at[i]))
        copies[-1].start()
    for copy in copies:
        copy.wait()


def send_kernel(wsend_ref, nu_ref, q_ref, *refs):
    count = wsend_ref.shape[0]
    near, refs = refs[0], refs[1:]
    far_v, out = refs[:count], refs[count:]
    rows = q_ref.shape[2]
    for j in range(count):
        for i, v in enumerate(SENT):
            dy = dot(wsend_ref[j], three_parts([q_ref[0, v], near[0, i]]))
            out[j][0, i] = nu_ref[v, 0:1] * dy[rows:] - far_v[j][0, 0] * dy[:rows]


def raw_kernel(count, wdirect_ref, wpassed_ref, nu_ref, q_ref, base_ref, *refs):
    out_ref = refs[-1]
    rows = q_ref.shape[2]
    first, second = [(refs[k : k + count], refs[k + count : k + 2 * count]) for k in (0, 2 * count)]
    for (low, high), (direct, passed) in ((FIRST, first), (SECOND, second)):
        for v in range(low, high):
            dy = dot(wdirect_ref[...], three_parts([piece[0, v - low] for piece in direct]))
            dy = dy + dot(wpassed_ref[...], three_parts([piece[0, v - low] for piece in passed]))
            out_ref[0, v] = base_ref[0, v] + nu_ref[v, 0:1] * dy[rows:] - q_ref[0, 1] * dy[:rows]
    for v in SENT:
        out_ref[0, v] = base_ref[0, v]


def last_kernel(left_ref, *refs):
    results, (_, out_ref, done_ref, sems) = refs[:-4], refs[-4:]
    copies = []
    for i, v in enumerate(SENT):
        done_ref[i] = left_ref[0, i] + sum(piece[0, i] for piece in results)
        copies.append(pltpu.make_async_copy(done_ref.at[i], out_ref.at[0, v], sems.at[i]))
        copies[-1].start()
    for copy in copies:
        copy.wait()


def smem():
    return pl.BlockSpec(memory_space=SMEM)


def kept():
    return pl.BlockSpec(memory_space=VMEM)


def held(array):
    return pltpu.with_memory_space_constraint(array, VMEM)


def on_device(
    slots,
    lines,
    flow_state,
    block_owner,
    link_block,
    link_side,
    rows_live,
    x_operator,
    ghost_operator,
    y_operator,
    coefficients,
):
    _, nvar, rows, x_length = flow_state.shape
    y_length = lines * rows
    limit = pltpu.CompilerParams(vmem_limit_bytes=16 * 1024 * 1024)
    small = pl.CostEstimate(flops=1, bytes_accessed=1, transcendentals=0)
    state_shape = jax.ShapeDtypeStruct(flow_state.shape, jnp.float32)
    sibling = [(i, i ^ 1) for i in range(lines)]
    shifts = range(2, lines, 2)

    def across(array):
        return [lax.ppermute(array, "line", [(i, (i + s) % lines) for i in range(lines)]) for s in shifts]

    low, high = FIRST
    part = pl.pallas_call(
        functools.partial(part_kernel, low),
        in_specs=[pl.BlockSpec(memory_space=pl.ANY)],
        out_specs=pl.BlockSpec(memory_space=VMEM),
        out_shape=jax.ShapeDtypeStruct((1, high - low, rows, x_length), jnp.float32),
        scratch_shapes=[pltpu.SemaphoreType.DMA],
        compiler_params=limit,
        cost_estimate=small,
        name="part",
    )(pltpu.with_memory_space_constraint(flow_state, HBM))
    part, flow_state = lax.optimization_barrier((part, flow_state))
    direct_first = across(part)
    second = flow_state[:, SECOND[0] : SECOND[1]]
    direct_second = across(second)
    near_sent = lax.ppermute(
        jnp.concatenate([flow_state[:, v : v + 1] for v in SENT], axis=1), "line", sibling
    )

    last = x_length // LANES - 1
    faces = pl.pallas_call(
        faces_kernel,
        grid=(1,),
        in_specs=[
            smem(),
            smem(),
            pl.BlockSpec((1, nvar, rows, LANES), lambda i: (0, 0, 0, 0)),
            pl.BlockSpec((1, nvar, rows, LANES), lambda i: (0, 0, 0, last)),
        ],
        out_specs=pl.BlockSpec((1, 2, FACE_ROWS, rows), lambda i: (0, 0, 0, 0)),
        out_shape=jax.ShapeDtypeStruct((1, 2, FACE_ROWS, rows), jnp.float32),
        compiler_params=limit,
        cost_estimate=small,
        name="faces",
    )(block_owner, rows_live, flow_state, flow_state)

    w_near = jax.ShapeDtypeStruct((2 * rows, 3 * rows), jnp.bfloat16)
    w_far = jax.ShapeDtypeStruct((2 * rows, 3 * len(shifts) * rows), jnp.bfloat16)
    w_send = jax.ShapeDtypeStruct((len(shifts), 2 * rows, 6 * rows), jnp.bfloat16)
    nu = jax.ShapeDtypeStruct((nvar, 8, x_length), jnp.float32)
    w_own, w_near, w_direct, w_passed, w_send, nu = pl.pallas_call(
        functools.partial(weights_kernel, lines),
        in_specs=[smem()] * 3 + [pl.BlockSpec(memory_space=pl.ANY)],
        out_specs=[kept()] * 6,
        out_shape=[w_near, w_near, w_far, w_far, w_send, nu],
        scratch_shapes=[
            pltpu.VMEM((2, y_length, LANES), jnp.float32),
            pltpu.VMEM((2, LANES, y_length), jnp.float32),
            pltpu.VMEM((len(shifts), 2, 2 * rows, LANES), jnp.float32),
            pltpu.VMEM((lines, 2 * rows, rows), jnp.bfloat16),
            pltpu.VMEM((lines, 2 * rows, rows), jnp.bfloat16),
            pltpu.SemaphoreType.DMA((2 + 4 * len(shifts),)),
        ],
        compiler_params=limit,
        cost_estimate=small,
        name="weights",
    )(block_owner, rows_live, coefficients, pltpu.with_memory_space_constraint(y_operator, HBM))

    tiles = x_length // TILE
    def own_terms(w_own):
        return pl.pallas_call(
            own_kernel,
            grid=(tiles,),
            in_specs=[smem()] * 3
            + [
                pl.BlockSpec(w_own.shape, lambda n: (0, 0)),
                pl.BlockSpec((1, nvar, rows, x_length), lambda n: (0, 0, 0, 0)),
                pl.BlockSpec((1, nvar, rows, TILE), lambda n: (0, 0, 0, n)),
                pl.BlockSpec((x_length, TILE), lambda n: (0, n)),
                pl.BlockSpec((x_length, TILE), lambda n: (0, n + tiles)),
            ],
            out_specs=pl.BlockSpec((1, nvar, rows, TILE), lambda n: (0, 0, 0, n)),
            out_shape=state_shape,
            scratch_shapes=[
                pltpu.VMEM((nvar * rows, x_length), jnp.bfloat16),
                pltpu.VMEM((nvar * rows, x_length), jnp.bfloat16),
            ],
            compiler_params=limit,
            cost_estimate=small,
            name="own_terms",
        )(
            block_owner,
            rows_live,
            coefficients,
            w_own,
            flow_state,
            flow_state,
            *[pltpu.with_memory_space_constraint(x_operator, HBM)] * 2,
        )

    far_v = [direct_first[shifts.index(lines - s)] for s in shifts]
    sent = jax.ShapeDtypeStruct((1, len(SENT), rows, x_length), jnp.float32)
    send = pl.pallas_call(
        send_kernel,
        in_specs=[kept()] * (4 + len(shifts)),
        out_specs=[kept()] * len(shifts),
        out_shape=[sent] * len(shifts),
        compiler_params=limit,
        cost_estimate=small,
        name="send_terms",
    )
    arrived = [faces]
    held_faces, step = faces, 1
    while step < slots:
        there = lax.ppermute(held_faces, "blk", [(i, i ^ step) for i in range(slots)])
        if step == 1:
            there, w_own, own = lax.optimization_barrier((there, w_own, flow_state))
            near_raw = lax.ppermute(own[:, RAW[0] : RAW[-1] + 1], "line", sibling)
        elif step == 2:
            state = own_terms(w_own)
            w_send, *_ = lax.optimization_barrier((w_send, state, there))
            results = send(*map(held, (w_send, nu, flow_state, near_sent, *far_v)))
            direct_first, *_ = lax.optimization_barrier((direct_first, *results))
            direct_second, *_ = lax.optimization_barrier((direct_second, *results))
        arrived.append(there)
        step *= 2
        if step < slots:
            held_faces = jnp.concatenate([held_faces, there], axis=0)

    results = [
        lax.ppermute(result, "line", [(i, (i + s) % lines) for i in range(lines)])
        for s, result in zip(shifts, results)
    ]

    passed_first = [lax.ppermute(piece, "line", sibling) for piece in direct_first]
    passed_second = [lax.ppermute(piece, "line", sibling) for piece in direct_second]
    pieces = [*direct_first, *passed_first, *direct_second, *passed_second]
    state = pl.pallas_call(
        functools.partial(raw_kernel, len(shifts)),
        in_specs=[kept()] * (5 + len(pieces)),
        out_specs=kept(),
        out_shape=state_shape,
        compiler_params=limit,
        cost_estimate=small,
        name="raw_terms",
    )(*map(held, (w_direct, w_passed, nu, flow_state, state, *pieces)))

    anywhere = pl.BlockSpec(memory_space=pl.ANY)
    result, left = pl.pallas_call(
        functools.partial(near_kernel, len(arrived)),
        in_specs=[smem()] * 4 + [kept()] * (7 + len(arrived)),
        out_specs=[anywhere, kept()],
        out_shape=[state_shape, sent],
        scratch_shapes=[
            pltpu.VMEM((len(RAW), rows, x_length), jnp.float32),
            pltpu.SemaphoreType.DMA((len(RAW),)),
        ],
        compiler_params=limit,
        cost_estimate=small,
        name="near_terms",
    )(
        block_owner,
        link_block.T,
        link_side.T,
        rows_live,
        *map(held, (ghost_operator, w_near, nu, flow_state, state, near_raw, near_sent, *arrived)),
    )

    operands = [*map(held, (left, *results))]
    return pl.pallas_call(
        last_kernel,
        in_specs=[kept()] * len(operands) + [anywhere],
        out_specs=anywhere,
        out_shape=state_shape,
        input_output_aliases={len(operands): 0},
        scratch_shapes=[pltpu.VMEM(sent.shape[1:], jnp.float32), pltpu.SemaphoreType.DMA((len(SENT),))],
        compiler_params=limit,
        cost_estimate=small,
        name="last_terms",
    )(*operands, result)


def solution(mesh):
    return jax.shard_map(
        functools.partial(on_device, mesh.shape["blk"], mesh.shape["line"]),
        mesh=mesh,
        in_specs=(P("blk", None, "line", None), P(), P(), P(), P(), P(), P(), P(), P()),
        out_specs=P("blk", None, "line", None),
        check_vma=False,
    )
```

time: 114 us -> 34 us (0.30)
  blocking collectives: 32.4 us -> 0 us
  local copies, waits for them, and re-layouts: 24.7 us -> 0.14 us
  other arithmetic: 15.3 us -> 0.04 us
  matrix products: 14.3 us -> 0 us
  Pallas kernels: 0 us -> 14 us
  waiting for transfers between devices: 15.2 us -> 7.29 us
  starting transfers between devices: 9.07 us -> 12.1 us
  between operations: 2.09 us -> 0.18 us
    all_gather x1 -> x0, blocking collectives: 32.4 us -> none  [on_device(): shard_piece = lax.all_gather(face_planes, 'blk', axis=0, tiled=True)]
    all_to_all x2 -> x0, waiting for transfers between devices: 15.2 us -> none  [the longest x1 15.2 us: on_device(): lax.all_to_all(y_cols_term, 'line', split_axis=2, concat_axis=1, tiled=True)]
    dot_general x4 -> x0, matrix products: 14.3 us -> none  [the longest x1 5.97 us: on_device(): x_parts = jnp.einsum('vyx,xk->vyk', masked, x_operator, precision=highest)]
    pallas_call x0 -> x8, Pallas kernels: none -> 14 us  [the longest x1 5.02 us: own_terms(): pl.pallas_call(own_kernel, grid=(tiles,), in_specs=[smem()] * 3 + [pl.Blo...]
    ppermute x0 -> x10, starting transfers between devices: none -> 12.1 us  [the longest x3 6.05 us: on_device(): lax.ppermute(held_faces, 'blk', [(i, i ^ step) for i in range(slots)])]
    all_to_all x5 -> x0, local copies, waits for them, and re-layouts: 12.1 us -> none  [the longest x3 8.05 us: on_device(): lax.all_to_all(masked, 'line', split_axis=2, concat_axis=1, tiled=True)]
    all_to_all x2 -> x0, starting transfers between devices: 9.07 us -> none  [the longest x1 4.63 us: on_device(): lax.all_to_all(y_cols_term, 'line', split_axis=2, concat_axis=1, tiled=True)]
    ppermute x0 -> x10, waiting for transfers between devices: none -> 7.29 us  [the longest x3 3.04 us: on_device(): lax.ppermute(held_faces, 'blk', [(i, i ^ step) for i in range(slots)])]
  transfers between devices with their start and end apart: 2 -> 10, of which waited for: 1 -> 4; matrix products, arithmetic and copies ran while one was open for 14% -> 0% of each run, Pallas kernels for 0% -> 36%
where the time goes in v1:
time: 34 us; the launch traced here: 33.8 us
  Pallas kernels  14 us (41%)
  starting transfers between devices  12.1 us (36%)
  waiting for transfers between devices  7.29 us (21%)
    ppermute x3, starting transfers between devices, on_device(): lax.ppermute(held_faces, 'blk', [(i, i ^ step) for i in range(slots)])  6.05 us
    pallas_call x1, Pallas kernels, own_terms(): pl.pallas_call(own_kernel, grid=(tiles,), in_specs=[smem()] * 3 + [pl.Blo...  5.02 us
    ppermute x2, starting transfers between devices, across(): lax.ppermute(array, 'line', [(i, (i + s) % lines) for i in range(lines)])  3.54 us
    ppermute x3, waiting for transfers between devices, on_device(): lax.ppermute(held_faces, 'blk', [(i, i ^ step) for i in range(slots)])  3.04 us
    ppermute x2, waiting for transfers between devices, across(): lax.ppermute(array, 'line', [(i, (i + s) % lines) for i in range(lines)])  3 us
    pallas_call x1, Pallas kernels, on_device(): pl.pallas_call(functools.partial(near_kernel, len(arrived)), in_specs=[sm...  2.35 us
    pallas_call x1, Pallas kernels, on_device(): pl.pallas_call(functools.partial(weights_kernel, lines), in_specs=[smem()...  2.19 us
    ppermute x1, starting transfers between devices, on_device(): lax.ppermute(result, 'line', [(i, (i + s) % lines) for i in range(lines)])  2.13 us
  transfers between devices with their start and end apart: 10, of which 4 were waited for; matrix products, arithmetic and copies ran while one was open for 0% of the time, Pallas kernels for 36%

profile of v1, /device:TPU:0, one launch (start us, length us, event | category | flops | bytes accessed | tf_op | source)
XLA Modules:
  0.0 33.8 jit_solution(16691988363531383332)
XLA Ops:
  0.0 0.0 copy-start
  0.0 1.2 %part.1 = f32[1,2,128,512]{3,2,1,0:T(8,128)S(1)} custom-call(f32[1,5,128,512]{3,2,1,0:T(8,128)} %q_ref.5), custom_call_target="tpu_custom_call" | custom-call | flops 1 | bytes 1 | tf_op jit(solution)/shard_map/part/pallas_call | solution.py:339
  1.2 0.0 copy-start.2
  1.2 0.0 copy-start.3
  1.2 3.0 %collective-permute-start.1 = (f32[1,2,128,512]{3,2,1,0:T(8,128)S(1)}, f32[1,2,128,512]{3,2,1,0:T(8,128)S(1)}, u32[]{:S(2)}, u32[]{:S(2)}) collective-permute-start(f32[1,2,128,512]{3,2,1,0:T(8,128)S(1)} %part.1), channel_id=1, source_target_pairs={{0,2},{1,3},{2,0},{3,1},{4,6},{5,7},{6,4},{7,5},{8,10},{9,11},{10,... | collective-permute-start | bytes 1572872 | tf_op jit(solution)/shard_map/ppermute | solution.py:336
  4.2 0.0 copy-done
  4.2 0.1 fusion
  4.3 0.0 copy-start.4
  4.3 0.1 collective-permute-start.3
  4.4 0.0 copy-done.2
  4.4 0.0 copy-done.3
  4.4 0.8 %faces.1.refs_1_ = f32[1,2,16,128]{3,2,1,0:T(8,128)S(1)} custom-call(s32[8]{0:T(128)S(1)} %copy-done.2, s32[8]{0:T(128)S(1)} %copy-done.3, f32[1,5,128,512]{3,2,1,0:T(8,128)S(1)} %copy-done, f32[1,5,128,512]{3,2,1,0:T(8,128)S(1)} %copy-done), custom_call_target="tpu_custom_call" | custom-call | flops 1 | bytes 1 | tf_op jit(solution)/shard_map/faces/pallas_call | solution.py:358
  5.3 1.6 %collective-permute-start = (f32[1,2,16,128]{3,2,1,0:T(8,128)S(1)}, f32[1,2,16,128]{3,2,1,0:T(8,128)S(1)}, u32[]{:S(2)}, u32[]{:S(2)}) collective-permute-start(f32[1,2,16,128]{3,2,1,0:T(8,128)S(1)} %faces.1.refs_1_), channel_id=1, source_target_pairs={{0,4},{4,0},{8,12},{12,8},{16,20},{20,16},{24,28},{28,24},{1,5},{5... | collective-permute-start | bytes 49160 | tf_op jit(solution)/shard_map/ppermute | solution.py:442
  6.8 0.0 copy-done.4
  6.8 2.2 %weights.1 = (bf16[256,384]{1,0:T(8,128)(2,1)S(1)}, bf16[256,384]{1,0:T(8,128)(2,1)S(1)}, bf16[256,384]{1,0:T(8,128)(2,1)S(1)}, bf16[256,384]{1,0:T(8,128)(2,1)S...) custom-call(s32[8]{0:T(128)S(1)} %copy-done.2, s32[8]{0:T(128)S(1)} %copy-done.3, f32[7]{0:T(128)S(1)} %copy-done.4, ...), custom_call_target="tpu_custom_call" | custom-call | flops 1 | bytes 1 | tf_op jit(solution)/shard_map/weights/pallas_call | solution.py:378
  9.0 0.0 collective-permute-done.refs_2_
  9.1 0.1 slice.15
  9.1 0.3 collective-permute-start.7
  9.4 1.6 %collective-permute-start.2 = (f32[2,2,16,128]{3,2,1,0:T(8,128)S(1)}, f32[2,2,16,128]{3,2,1,0:T(8,128)S(1)}, u32[]{:S(2)}, u32[]{:S(2)}) collective-permute-start(f32[2,2,16,128]{3,2,1,0:T(8,128)S(1)} %pad_maximum_fusion.2), channel_id=1, source_target_pairs={{0,8},{4,12},{8,0},{12,4},{16,24},{20,28},{24,16},{28,20},{1,9},{5... | collective-permute-start | bytes 98312 | tf_op jit(solution)/shard_map/ppermute | solution.py:442
  11.0 0.5 %collective-permute-start.5 = (f32[1,1,128,512]{3,2,1,0:T(8,128)S(1)}, f32[1,1,128,512]{3,2,1,0:T(8,128)S(1)}, u32[]{:S(2)}, u32[]{:S(2)}) collective-permute-start(f32[1,1,128,512]{3,2,1,0:T(8,128)S(1)} %get-tuple-element.37), channel_id=1, source_target_pairs={{0,2},{1,3},{2,0},{3,1},{4,6},{5,7},{6,4},{7,5},{8,10},{9,11},{10,... | collective-permute-start | bytes 786440 | tf_op jit(solution)/shard_map/ppermute | solution.py:336
  11.5 5.0 %own_terms.1.base_ref = f32[1,5,128,512]{3,2,1,0:T(8,128)S(1)} custom-call(s32[8]{0:T(128)S(1)} %copy-done.2, s32[8]{0:T(128)S(1)} %copy-done.3, f32[7]{0:T(128)S(1)} %copy-done.4, bf16[256,384]{1,0:T(8,128)(2,1)S(1)} %get-tuple-element.27.wown_ref, f32[1,5,128,512]{3,2,1,0:T(8,128)S(1)} %copy-done, f32[1,5,128,512]{3,2,1,0:T(8,128)S(1)} %copy-done, ...), custom_call_target="tpu_custom_call" | custom-call | flops 1 | bytes 1 | tf_op jit(solution)/shard_map/own_terms/pallas_call | solution.py:398
  16.5 0.0 collective-permute-done.2.refs_3_
  16.5 0.4 %collective-permute-done.1.refs_1_.refs_0_ = f32[1,2,128,512]{3,2,1,0:T(8,128)S(1)} collective-permute-done((f32[1,2,128,512]{3,2,1,0:T(8,128)S(1)}, f32[1,2,128,512]{3,2,1,0:T(8,128)S(1)}, u32[]{:S(2)}, u32[]{:S(2)}) %collective-permute-start.1) | collective-permute-done | bytes 524320 | tf_op jit(solution)/shard_map/ppermute | solution.py:336
  16.9 0.0 collective-permute-done.3.refs_0_
  16.9 0.6 %send_terms.1 = f32[1,2,128,512]{3,2,1,0:T(8,128)S(1)} custom-call(bf16[1,256,768]{2,1,0:T(8,128)(2,1)S(1)} %get-tuple-element.31.wsend_ref, f32[5,8,512]{2,1,0:T(8,128)S(1)} %get-tuple-element.22.nu_ref, f32[1,5,128,512]{3,2,1,0:T(8,128)S(1)} %copy-done, f32[1,2,128,512]{3,2,1,0:T(8,128)S(1)} %collective-permute-done.3.refs_0_, ...), custom_call_target="tpu_custom_call" | custom-call | flops 1 | bytes 1 | tf_op jit(solution)/shard_map/send_terms/pallas_call | solution.py:449
  17.6 0.1 collective-permute-start.4
  17.6 2.1 %collective-permute-start.9 = (f32[1,2,128,512]{3,2,1,0:T(8,128)S(1)}, f32[1,2,128,512]{3,2,1,0:T(8,128)S(1)}, u32[]{:S(2)}, u32[]{:S(2)}) collective-permute-start(f32[1,2,128,512]{3,2,1,0:T(8,128)S(1)} %send_terms.1), channel_id=1, source_target_pairs={{0,2},{1,3},{2,0},{3,1},{4,6},{5,7},{6,4},{7,5},{8,10},{9,11},{10,... | collective-permute-start | bytes 1572872 | tf_op jit(solution)/shard_map/ppermute | solution.py:458
  19.8 2.6 %collective-permute-done.5.refs_2_ = f32[1,1,128,512]{3,2,1,0:T(8,128)S(1)} collective-permute-done((f32[1,1,128,512]{3,2,1,0:T(8,128)S(1)}, f32[1,1,128,512]{3,2,1,0:T(8,128)S(1)}, u32[]{:S(2)}, u32[]{:S(2)}) %collective-permute-start.5) | collective-permute-done | bytes 262176 | tf_op jit(solution)/shard_map/ppermute | solution.py:336
  22.4 0.0 collective-permute-start.6
  22.4 2.9 %collective-permute-start.8 = (f32[4,2,16,128]{3,2,1,0:T(8,128)S(1)}, f32[4,2,16,128]{3,2,1,0:T(8,128)S(1)}, u32[]{:S(2)}, u32[]{:S(2)}) collective-permute-start(f32[4,2,16,128]{3,2,1,0:T(8,128)S(1)} %pad_maximum_fusion.1), channel_id=1, source_target_pairs={{0,16},{4,20},{8,24},{12,28},{16,0},{20,4},{24,8},{28,12},{1,17},{... | collective-permute-start | bytes 196616 | tf_op jit(solution)/shard_map/ppermute | solution.py:442
  25.3 0.0 collective-permute-done.6.refs_3_
  25.3 0.0 collective-permute-done.4.refs_1_
  25.3 0.0 copy-start.1
  25.3 0.0 copy-start.5
  25.3 0.0 copy-start.6
  25.3 1.0 %raw_terms.1.base_ref = f32[1,5,128,512]{3,2,1,0:T(8,128)S(1)} custom-call(bf16[256,384]{1,0:T(8,128)(2,1)S(1)} %get-tuple-element.24.wdirect_ref, bf16[256,384]{1,0:T(8,128)(2,1)S(1)} %get-tuple-element.25.wpassed_ref, f32[5,8,512]{2,1,0:T(8,128)S(1)} %get-tuple-element.22.nu_ref, f32[1,5,128,512]{3,2,1,0:T(8,128)S(1)} %copy-done, ...), custom_call_target="tpu_custom_call" | custom-call | flops 1 | bytes 1 | tf_op jit(solution)/shard_map/raw_terms/pallas_call | solution.py:465
  26.3 3.0 %collective-permute-done.8.refs_4_ = f32[4,2,16,128]{3,2,1,0:T(8,128)S(1)} collective-permute-done((f32[4,2,16,128]{3,2,1,0:T(8,128)S(1)}, f32[4,2,16,128]{3,2,1,0:T(8,128)S(1)}, u32[]{:S(2)}, u32[]{:S(2)}) %collective-permute-start.8) | collective-permute-done | bytes 65568 | tf_op jit(solution)/shard_map/ppermute | solution.py:442
  29.4 0.0 collective-permute-done.7.near_raw_ref
  29.4 0.0 copy-done.1
  29.4 0.0 copy-done.5
  29.4 0.0 copy-done.6
  29.4 2.3 %near_terms.1 = (f32[1,5,128,512]{3,2,1,0:T(8,128)}, f32[1,2,128,512]{3,2,1,0:T(8,128)S(1)}) custom-call(s32[8]{0:T(128)S(1)} %copy-done.2, s32[2,8]{1,0:T(2,128)S(1)} %bitcast.2, s32[2,8]{1,0:T(2,128)S(1)} %bitcast.3, s32[8]{0:T(128)S(1)} %copy-done.3, f32[6,1024]{1,0:T(8,128)S(1)} %copy-done.1, bf16[256,384]{1,0:T(8,128)(2,1)S(1)} %get-tuple-element.21.wnear_ref, ...), custom_call_target="tpu_custom_call" | custom-call | flops 1 | bytes 1 | tf_op jit(solution)/shard_map/near_terms/pallas_call | solution.py:476
  31.7 1.2 %collective-permute-done.9.refs_0_ = f32[1,2,128,512]{3,2,1,0:T(8,128)S(1)} collective-permute-done((f32[1,2,128,512]{3,2,1,0:T(8,128)S(1)}, f32[1,2,128,512]{3,2,1,0:T(8,128)S(1)}, u32[]{:S(2)}, u32[]{:S(2)}) %collective-permute-start.9) | collective-permute-done | bytes 524320 | tf_op jit(solution)/shard_map/ppermute | solution.py:458
  33.0 0.8 %last_terms.1 = f32[1,5,128,512]{3,2,1,0:T(8,128)} custom-call(f32[1,2,128,512]{3,2,1,0:T(8,128)S(1)} %get-tuple-element.35.left_ref, f32[1,2,128,512]{3,2,1,0:T(8,128)S(1)} %collective-permute-done.9.refs_0_, f32[1,5,128,512]{3,2,1,0:T(8,128)} %get-tuple-element.36.refs_1_), custom_call_target="tpu_custom_call", output_to_operand_aliasing={{}: (2, {})} | custom-call | flops 1 | bytes 1 | tf_op jit(solution)/shard_map/last_terms/pallas_call | solution.py:497
  (3 shorter events, 0.0 us)
Async XLA Ops:
  0.0 4.2 %copy-start = (f32[1,5,128,512]{3,2,1,0:T(8,128)S(1)}, f32[1,5,128,512]{3,2,1,0:T(8,128)}, u32[]{:S(2)}) copy-start(f32[1,5,128,512]{3,2,1,0:T(8,128)} %q_ref.5) | copy-start | bytes 3932164
  1.2 3.2 %copy-start.2 = (s32[8]{0:T(128)S(1)}, s32[8]{0:T(128)}, u32[]{:S(2)}) copy-start(s32[8]{0:T(128)} %owner_ref.7) | copy-start | bytes 100
  1.2 3.2 %copy-start.3 = (s32[8]{0:T(128)S(1)}, s32[8]{0:T(128)}, u32[]{:S(2)}) copy-start(s32[8]{0:T(128)} %rows_ref.7) | copy-start | bytes 100
  1.2 15.8 %collective-permute-start.1 = (f32[1,2,128,512]{3,2,1,0:T(8,128)S(1)}, f32[1,2,128,512]{3,2,1,0:T(8,128)S(1)}, u32[]{:S(2)}, u32[]{:S(2)}) collective-permute-start(f32[1,2,128,512]{3,2,1,0:T(8,128)S(1)} %part.1), channel_id=1, source_target_pairs={{0,2},{1,3},{2,0},{3,1},{4,6},{5,7},{6,4},{7,5},{8,10},{9,11},{10,... | collective-permute-start | bytes 1572872 | tf_op jit(solution)/shard_map/ppermute | solution.py:336
  4.3 2.5 %copy-start.4 = (f32[7]{0:T(128)S(1)}, f32[7]{0:T(128)}, u32[]{:S(2)}) copy-start(f32[7]{0:T(128)} %coef_ref.3) | copy-start | bytes 88
  4.3 12.6 %collective-permute-start.3 = (f32[1,2,128,512]{3,2,1,0:T(8,128)S(1)}, f32[1,2,128,512]{3,2,1,0:T(8,128)S(1)}, u32[]{:S(2)}, u32[]{:S(2)}) collective-permute-start(f32[1,2,128,512]{3,2,1,0:T(8,128)S(1)} %pad_maximum_fusion), channel_id=1, source_target_pairs={{0,1},{1,0},{2,3},{3,2},{4,5},{5,4},{6,7},{7,6},{8,9},{9,8},{10,11... | collective-permute-start | bytes 1572872 | tf_op jit(solution)/shard_map/ppermute | solution.py:353
  5.3 3.8 %collective-permute-start = (f32[1,2,16,128]{3,2,1,0:T(8,128)S(1)}, f32[1,2,16,128]{3,2,1,0:T(8,128)S(1)}, u32[]{:S(2)}, u32[]{:S(2)}) collective-permute-start(f32[1,2,16,128]{3,2,1,0:T(8,128)S(1)} %faces.1.refs_1_), channel_id=1, source_target_pairs={{0,4},{4,0},{8,12},{12,8},{16,20},{20,16},{24,28},{28,24},{1,5},{5... | collective-permute-start | bytes 49160 | tf_op jit(solution)/shard_map/ppermute | solution.py:442
  9.1 20.2 %collective-permute-start.7 = (f32[1,3,128,512]{3,2,1,0:T(8,128)S(1)}, f32[1,3,128,512]{3,2,1,0:T(8,128)S(1)}, u32[]{:S(2)}, u32[]{:S(2)}) collective-permute-start(f32[1,3,128,512]{3,2,1,0:T(8,128)S(1)} %slice.15), channel_id=1, source_target_pairs={{0,1},{1,0},{2,3},{3,2},{4,5},{5,4},{6,7},{7,6},{8,9},{9,8},{10,11... | collective-permute-start | bytes 2359304 | tf_op jit(solution)/shard_map/ppermute | solution.py:445
  9.4 7.1 %collective-permute-start.2 = (f32[2,2,16,128]{3,2,1,0:T(8,128)S(1)}, f32[2,2,16,128]{3,2,1,0:T(8,128)S(1)}, u32[]{:S(2)}, u32[]{:S(2)}) collective-permute-start(f32[2,2,16,128]{3,2,1,0:T(8,128)S(1)} %pad_maximum_fusion.2), channel_id=1, source_target_pairs={{0,8},{4,12},{8,0},{12,4},{16,24},{20,28},{24,16},{28,20},{1,9},{5... | collective-permute-start | bytes 98312 | tf_op jit(solution)/shard_map/ppermute | solution.py:442
  11.0 11.4 %collective-permute-start.5 = (f32[1,1,128,512]{3,2,1,0:T(8,128)S(1)}, f32[1,1,128,512]{3,2,1,0:T(8,128)S(1)}, u32[]{:S(2)}, u32[]{:S(2)}) collective-permute-start(f32[1,1,128,512]{3,2,1,0:T(8,128)S(1)} %get-tuple-element.37), channel_id=1, source_target_pairs={{0,2},{1,3},{2,0},{3,1},{4,6},{5,7},{6,4},{7,5},{8,10},{9,11},{10,... | collective-permute-start | bytes 786440 | tf_op jit(solution)/shard_map/ppermute | solution.py:336
  17.6 7.7 %collective-permute-start.4 = (f32[1,2,128,512]{3,2,1,0:T(8,128)S(1)}, f32[1,2,128,512]{3,2,1,0:T(8,128)S(1)}, u32[]{:S(2)}, u32[]{:S(2)}) collective-permute-start(f32[1,2,128,512]{3,2,1,0:T(8,128)S(1)} %collective-permute-done.1.refs_1_.refs_0_), channel_id=1, source_target_pairs={{0,1},{1,0},{2,3},{3,2},{4,5},{5,4},{6,7},{7,6},{8,9},{9,8},{10,11... | collective-permute-start | bytes 1572872 | tf_op jit(solution)/shard_map/ppermute | solution.py:462
  17.6 15.3 %collective-permute-start.9 = (f32[1,2,128,512]{3,2,1,0:T(8,128)S(1)}, f32[1,2,128,512]{3,2,1,0:T(8,128)S(1)}, u32[]{:S(2)}, u32[]{:S(2)}) collective-permute-start(f32[1,2,128,512]{3,2,1,0:T(8,128)S(1)} %send_terms.1), channel_id=1, source_target_pairs={{0,2},{1,3},{2,0},{3,1},{4,6},{5,7},{6,4},{7,5},{8,10},{9,11},{10,... | collective-permute-start | bytes 1572872 | tf_op jit(solution)/shard_map/ppermute | solution.py:458
  22.4 2.9 %collective-permute-start.6 = (f32[1,1,128,512]{3,2,1,0:T(8,128)S(1)}, f32[1,1,128,512]{3,2,1,0:T(8,128)S(1)}, u32[]{:S(2)}, u32[]{:S(2)}) collective-permute-start(f32[1,1,128,512]{3,2,1,0:T(8,128)S(1)} %collective-permute-done.5.refs_2_), channel_id=1, source_target_pairs={{0,1},{1,0},{2,3},{3,2},{4,5},{5,4},{6,7},{7,6},{8,9},{9,8},{10,11... | collective-permute-start | bytes 786440 | tf_op jit(solution)/shard_map/ppermute | solution.py:463
  22.4 7.0 %collective-permute-start.8 = (f32[4,2,16,128]{3,2,1,0:T(8,128)S(1)}, f32[4,2,16,128]{3,2,1,0:T(8,128)S(1)}, u32[]{:S(2)}, u32[]{:S(2)}) collective-permute-start(f32[4,2,16,128]{3,2,1,0:T(8,128)S(1)} %pad_maximum_fusion.1), channel_id=1, source_target_pairs={{0,16},{4,20},{8,24},{12,28},{16,0},{20,4},{24,8},{28,12},{1,17},{... | collective-permute-start | bytes 196616 | tf_op jit(solution)/shard_map/ppermute | solution.py:442
  25.3 4.1 %copy-start.1 = (f32[6,1024]{1,0:T(8,128)S(1)}, f32[6,1024]{1,0:T(8,128)}, u32[]{:S(2)}) copy-start(f32[6,1024]{1,0:T(8,128)} %gop_ref.1) | copy-start | bytes 73732
  25.3 4.1 %copy-start.5 = (s32[8,2]{0,1:T(2,128)S(1)}, s32[8,2]{0,1:T(2,128)}, u32[]{:S(2)}) copy-start(s32[8,2]{0,1:T(2,128)} %param.11) | copy-start | bytes 196
  25.3 4.1 %copy-start.6 = (s32[8,2]{0,1:T(2,128)S(1)}, s32[8,2]{0,1:T(2,128)}, u32[]{:S(2)}) copy-start(s32[8,2]{0,1:T(2,128)} %param.12) | copy-start | bytes 196

commit v2 on v1

--- a/solution.py
+++ b/solution.py
@@ -12,6 +12,7 @@
 FACE_ROWS = 16
 TILE = 256
 LANES = 128
+PIECES = 4
 FIRST, SECOND = (1, 3), (3, 4)
 RAW = tuple(range(FIRST[0], SECOND[1]))
 SENT = (0, 4)
@@ -58,10 +59,18 @@
         out_ref[0, m, GHOST * nvar :, :] = jnp.zeros((FACE_ROWS - GHOST * nvar, rows), jnp.float32)
 
 
-def part_kernel(low, q_ref, out_ref, sem):
-    copy = pltpu.make_async_copy(q_ref.at[:, low : low + out_ref.shape[1]], out_ref, sem)
-    copy.start()
-    copy.wait()
+def part_kernel(low, q_ref, out_ref, sems):
+    size = out_ref.shape[2] // PIECES
+    copies = []
+    for i in range(out_ref.shape[1]):
+        for j in range(PIECES):
+            here = pl.ds(j * size, size)
+            source, goal = q_ref.at[0, low + i, here], out_ref.at[0, i, here]
+            copies.append(pltpu.make_async_copy(source, goal, sems.at[len(copies)]))
+    for copy in copies:
+        copy.start()
+    for copy in copies:
+        copy.wait()
 
 
 def weights_kernel(
@@ -291,10 +300,14 @@
 def last_kernel(left_ref, *refs):
     results, (_, out_ref, done_ref, sems) = refs[:-4], refs[-4:]
     copies = []
+    size = left_ref.shape[2] // PIECES
     for i, v in enumerate(SENT):
-        done_ref[i] = left_ref[0, i] + sum(piece[0, i] for piece in results)
-        copies.append(pltpu.make_async_copy(done_ref.at[i], out_ref.at[0, v], sems.at[i]))
-        copies[-1].start()
+        for j in range(PIECES):
+            here = pl.ds(j * size, size)
+            done_ref[i, here] = left_ref[0, i, here] + sum(piece[0, i, here] for piece in results)
+            source, goal = done_ref.at[i, here], out_ref.at[0, v, here]
+            copies.append(pltpu.make_async_copy(source, goal, sems.at[len(copies)]))
+            copies[-1].start()
     for copy in copies:
         copy.wait()
 
@@ -341,7 +354,7 @@
         in_specs=[pl.BlockSpec(memory_space=pl.ANY)],
         out_specs=pl.BlockSpec(memory_space=VMEM),
         out_shape=jax.ShapeDtypeStruct((1, high - low, rows, x_length), jnp.float32),
-        scratch_shapes=[pltpu.SemaphoreType.DMA],
+        scratch_shapes=[pltpu.SemaphoreType.DMA(((high - low) * PIECES,))],
         compiler_params=limit,
         cost_estimate=small,
         name="part",
@@ -500,7 +513,7 @@
         out_specs=anywhere,
         out_shape=state_shape,
         input_output_aliases={len(operands): 0},
-        scratch_shapes=[pltpu.VMEM(sent.shape[1:], jnp.float32), pltpu.SemaphoreType.DMA((len(SENT),))],
+        scratch_shapes=[pltpu.VMEM(sent.shape[1:], jnp.float32), pltpu.SemaphoreType.DMA((len(SENT) * PIECES,))],
         compiler_params=limit,
         cost_estimate=small,
         name="last_terms",

time: 34 us -> 34.1 us (level)
  transfers between devices with their start and end apart: 10 -> 10, of which waited for: 4 -> 4; matrix products, arithmetic and copies ran while one was open for 0% -> 0% of each run, Pallas kernels for 36% -> 35%
where the time goes in v2:
time: 34.1 us; the launch traced here: 33.9 us
  Pallas kernels  14.1 us (41%)
  starting transfers between devices  12.1 us (35%)
  waiting for transfers between devices  7.31 us (21%)
    ppermute x3, starting transfers between devices, on_device(): lax.ppermute(held_faces, 'blk', [(i, i ^ step) for i in range(slots)])  6.04 us
    pallas_call x1, Pallas kernels, own_terms(): pl.pallas_call(own_kernel, grid=(tiles,), in_specs=[smem()] * 3 + [pl.Blo...  5.02 us
    ppermute x2, starting transfers between devices, across(): lax.ppermute(array, 'line', [(i, (i + s) % lines) for i in range(lines)])  3.54 us
    ppermute x3, waiting for transfers between devices, on_device(): lax.ppermute(held_faces, 'blk', [(i, i ^ step) for i in range(slots)])  3.05 us
    ppermute x2, waiting for transfers between devices, across(): lax.ppermute(array, 'line', [(i, (i + s) % lines) for i in range(lines)])  3.01 us
    pallas_call x1, Pallas kernels, on_device(): pl.pallas_call(functools.partial(near_kernel, len(arrived)), in_specs=[sm...  2.34 us
    pallas_call x1, Pallas kernels, on_device(): pl.pallas_call(functools.partial(weights_kernel, lines), in_specs=[smem()...  2.19 us
    ppermute x1, starting transfers between devices, on_device(): lax.ppermute(result, 'line', [(i, (i + s) % lines) for i in range(lines)])  2.12 us
  transfers between devices with their start and end apart: 10, of which 4 were waited for; matrix products, arithmetic and copies ran while one was open for 0% of the time, Pallas kernels for 35%

profile of v2, /device:TPU:0, one launch (start us, length us, event | category | flops | bytes accessed | tf_op | source)
XLA Modules:
  0.0 33.9 jit_solution(47373549718920390)
XLA Ops:
  0.0 0.0 copy-start
  0.0 1.2 %part.1 = f32[1,2,128,512]{3,2,1,0:T(8,128)S(1)} custom-call(f32[1,5,128,512]{3,2,1,0:T(8,128)} %q_ref.5), custom_call_target="tpu_custom_call" | custom-call | flops 1 | bytes 1 | tf_op jit(solution)/shard_map/part/pallas_call | solution.py:352
  1.2 0.0 copy-start.2
  1.3 0.0 copy-start.3
  1.3 3.0 %collective-permute-start.1 = (f32[1,2,128,512]{3,2,1,0:T(8,128)S(1)}, f32[1,2,128,512]{3,2,1,0:T(8,128)S(1)}, u32[]{:S(2)}, u32[]{:S(2)}) collective-permute-start(f32[1,2,128,512]{3,2,1,0:T(8,128)S(1)} %part.1), channel_id=1, source_target_pairs={{0,2},{1,3},{2,0},{3,1},{4,6},{5,7},{6,4},{7,5},{8,10},{9,11},{10,... | collective-permute-start | bytes 1572872 | tf_op jit(solution)/shard_map/ppermute | solution.py:349
  4.3 0.0 copy-done
  4.3 0.1 fusion
  4.4 0.0 copy-start.4
  4.4 0.1 collective-permute-start.3
  4.5 0.0 copy-done.2
  4.5 0.0 copy-done.3
  4.5 0.8 %faces.1.refs_1_ = f32[1,2,16,128]{3,2,1,0:T(8,128)S(1)} custom-call(s32[8]{0:T(128)S(1)} %copy-done.2, s32[8]{0:T(128)S(1)} %copy-done.3, f32[1,5,128,512]{3,2,1,0:T(8,128)S(1)} %copy-done, f32[1,5,128,512]{3,2,1,0:T(8,128)S(1)} %copy-done), custom_call_target="tpu_custom_call" | custom-call | flops 1 | bytes 1 | tf_op jit(solution)/shard_map/faces/pallas_call | solution.py:371
  5.3 1.6 %collective-permute-start = (f32[1,2,16,128]{3,2,1,0:T(8,128)S(1)}, f32[1,2,16,128]{3,2,1,0:T(8,128)S(1)}, u32[]{:S(2)}, u32[]{:S(2)}) collective-permute-start(f32[1,2,16,128]{3,2,1,0:T(8,128)S(1)} %faces.1.refs_1_), channel_id=1, source_target_pairs={{0,4},{4,0},{8,12},{12,8},{16,20},{20,16},{24,28},{28,24},{1,5},{5... | collective-permute-start | bytes 49160 | tf_op jit(solution)/shard_map/ppermute | solution.py:455
  6.9 0.0 copy-done.4
  6.9 2.2 %weights.1 = (bf16[256,384]{1,0:T(8,128)(2,1)S(1)}, bf16[256,384]{1,0:T(8,128)(2,1)S(1)}, bf16[256,384]{1,0:T(8,128)(2,1)S(1)}, bf16[256,384]{1,0:T(8,128)(2,1)S...) custom-call(s32[8]{0:T(128)S(1)} %copy-done.2, s32[8]{0:T(128)S(1)} %copy-done.3, f32[7]{0:T(128)S(1)} %copy-done.4, ...), custom_call_target="tpu_custom_call" | custom-call | flops 1 | bytes 1 | tf_op jit(solution)/shard_map/weights/pallas_call | solution.py:391
  9.1 0.0 collective-permute-done.refs_2_
  9.1 0.1 slice.15
  9.2 0.3 collective-permute-start.7
  9.5 1.6 %collective-permute-start.2 = (f32[2,2,16,128]{3,2,1,0:T(8,128)S(1)}, f32[2,2,16,128]{3,2,1,0:T(8,128)S(1)}, u32[]{:S(2)}, u32[]{:S(2)}) collective-permute-start(f32[2,2,16,128]{3,2,1,0:T(8,128)S(1)} %pad_maximum_fusion.2), channel_id=1, source_target_pairs={{0,8},{4,12},{8,0},{12,4},{16,24},{20,28},{24,16},{28,20},{1,9},{5... | collective-permute-start | bytes 98312 | tf_op jit(solution)/shard_map/ppermute | solution.py:455
  11.0 0.5 %collective-permute-start.5 = (f32[1,1,128,512]{3,2,1,0:T(8,128)S(1)}, f32[1,1,128,512]{3,2,1,0:T(8,128)S(1)}, u32[]{:S(2)}, u32[]{:S(2)}) collective-permute-start(f32[1,1,128,512]{3,2,1,0:T(8,128)S(1)} %get-tuple-element.37), channel_id=1, source_target_pairs={{0,2},{1,3},{2,0},{3,1},{4,6},{5,7},{6,4},{7,5},{8,10},{9,11},{10,... | collective-permute-start | bytes 786440 | tf_op jit(solution)/shard_map/ppermute | solution.py:349
  11.6 5.0 %own_terms.1.base_ref = f32[1,5,128,512]{3,2,1,0:T(8,128)S(1)} custom-call(s32[8]{0:T(128)S(1)} %copy-done.2, s32[8]{0:T(128)S(1)} %copy-done.3, f32[7]{0:T(128)S(1)} %copy-done.4, bf16[256,384]{1,0:T(8,128)(2,1)S(1)} %get-tuple-element.27.wown_ref, f32[1,5,128,512]{3,2,1,0:T(8,128)S(1)} %copy-done, f32[1,5,128,512]{3,2,1,0:T(8,128)S(1)} %copy-done, ...), custom_call_target="tpu_custom_call" | custom-call | flops 1 | bytes 1 | tf_op jit(solution)/shard_map/own_terms/pallas_call | solution.py:411
  16.6 0.0 collective-permute-done.2.refs_3_
  16.6 0.4 %collective-permute-done.1.refs_1_.refs_0_ = f32[1,2,128,512]{3,2,1,0:T(8,128)S(1)} collective-permute-done((f32[1,2,128,512]{3,2,1,0:T(8,128)S(1)}, f32[1,2,128,512]{3,2,1,0:T(8,128)S(1)}, u32[]{:S(2)}, u32[]{:S(2)}) %collective-permute-start.1) | collective-permute-done | bytes 524320 | tf_op jit(solution)/shard_map/ppermute | solution.py:349
  17.0 0.0 collective-permute-done.3.refs_0_
  17.0 0.6 %send_terms.1 = f32[1,2,128,512]{3,2,1,0:T(8,128)S(1)} custom-call(bf16[1,256,768]{2,1,0:T(8,128)(2,1)S(1)} %get-tuple-element.31.wsend_ref, f32[5,8,512]{2,1,0:T(8,128)S(1)} %get-tuple-element.22.nu_ref, f32[1,5,128,512]{3,2,1,0:T(8,128)S(1)} %copy-done, f32[1,2,128,512]{3,2,1,0:T(8,128)S(1)} %collective-permute-done.3.refs_0_, ...), custom_call_target="tpu_custom_call" | custom-call | flops 1 | bytes 1 | tf_op jit(solution)/shard_map/send_terms/pallas_call | solution.py:462
  17.6 0.1 collective-permute-start.4
  17.7 2.1 %collective-permute-start.9 = (f32[1,2,128,512]{3,2,1,0:T(8,128)S(1)}, f32[1,2,128,512]{3,2,1,0:T(8,128)S(1)}, u32[]{:S(2)}, u32[]{:S(2)}) collective-permute-start(f32[1,2,128,512]{3,2,1,0:T(8,128)S(1)} %send_terms.1), channel_id=1, source_target_pairs={{0,2},{1,3},{2,0},{3,1},{4,6},{5,7},{6,4},{7,5},{8,10},{9,11},{10,... | collective-permute-start | bytes 1572872 | tf_op jit(solution)/shard_map/ppermute | solution.py:471
  19.8 2.6 %collective-permute-done.5.refs_2_ = f32[1,1,128,512]{3,2,1,0:T(8,128)S(1)} collective-permute-done((f32[1,1,128,512]{3,2,1,0:T(8,128)S(1)}, f32[1,1,128,512]{3,2,1,0:T(8,128)S(1)}, u32[]{:S(2)}, u32[]{:S(2)}) %collective-permute-start.5) | collective-permute-done | bytes 262176 | tf_op jit(solution)/shard_map/ppermute | solution.py:349
  22.4 0.0 collective-permute-start.6
  22.4 2.9 %collective-permute-start.8 = (f32[4,2,16,128]{3,2,1,0:T(8,128)S(1)}, f32[4,2,16,128]{3,2,1,0:T(8,128)S(1)}, u32[]{:S(2)}, u32[]{:S(2)}) collective-permute-start(f32[4,2,16,128]{3,2,1,0:T(8,128)S(1)} %pad_maximum_fusion.1), channel_id=1, source_target_pairs={{0,16},{4,20},{8,24},{12,28},{16,0},{20,4},{24,8},{28,12},{1,17},{... | collective-permute-start | bytes 196616 | tf_op jit(solution)/shard_map/ppermute | solution.py:455
  25.3 0.0 collective-permute-done.6.refs_3_
  25.3 0.0 collective-permute-done.4.refs_1_
  25.3 0.0 copy-start.1
  25.3 0.0 copy-start.5
  25.4 0.0 copy-start.6
  25.4 1.0 %raw_terms.1.base_ref = f32[1,5,128,512]{3,2,1,0:T(8,128)S(1)} custom-call(bf16[256,384]{1,0:T(8,128)(2,1)S(1)} %get-tuple-element.24.wdirect_ref, bf16[256,384]{1,0:T(8,128)(2,1)S(1)} %get-tuple-element.25.wpassed_ref, f32[5,8,512]{2,1,0:T(8,128)S(1)} %get-tuple-element.22.nu_ref, f32[1,5,128,512]{3,2,1,0:T(8,128)S(1)} %copy-done, ...), custom_call_target="tpu_custom_call" | custom-call | flops 1 | bytes 1 | tf_op jit(solution)/shard_map/raw_terms/pallas_call | solution.py:478
  26.4 3.0 %collective-permute-done.8.refs_4_ = f32[4,2,16,128]{3,2,1,0:T(8,128)S(1)} collective-permute-done((f32[4,2,16,128]{3,2,1,0:T(8,128)S(1)}, f32[4,2,16,128]{3,2,1,0:T(8,128)S(1)}, u32[]{:S(2)}, u32[]{:S(2)}) %collective-permute-start.8) | collective-permute-done | bytes 65568 | tf_op jit(solution)/shard_map/ppermute | solution.py:455
  29.4 0.0 collective-permute-done.7.near_raw_ref
  29.4 0.0 copy-done.1
  29.4 0.0 copy-done.5
  29.4 0.0 copy-done.6
  29.4 2.3 %near_terms.1 = (f32[1,5,128,512]{3,2,1,0:T(8,128)}, f32[1,2,128,512]{3,2,1,0:T(8,128)S(1)}) custom-call(s32[8]{0:T(128)S(1)} %copy-done.2, s32[2,8]{1,0:T(2,128)S(1)} %bitcast.2, s32[2,8]{1,0:T(2,128)S(1)} %bitcast.3, s32[8]{0:T(128)S(1)} %copy-done.3, f32[6,1024]{1,0:T(8,128)S(1)} %copy-done.1, bf16[256,384]{1,0:T(8,128)(2,1)S(1)} %get-tuple-element.21.wnear_ref, ...), custom_call_target="tpu_custom_call" | custom-call | flops 1 | bytes 1 | tf_op jit(solution)/shard_map/near_terms/pallas_call | solution.py:489
  31.8 1.2 %collective-permute-done.9.refs_0_ = f32[1,2,128,512]{3,2,1,0:T(8,128)S(1)} collective-permute-done((f32[1,2,128,512]{3,2,1,0:T(8,128)S(1)}, f32[1,2,128,512]{3,2,1,0:T(8,128)S(1)}, u32[]{:S(2)}, u32[]{:S(2)}) %collective-permute-start.9) | collective-permute-done | bytes 524320 | tf_op jit(solution)/shard_map/ppermute | solution.py:471
  33.0 0.9 %last_terms.1 = f32[1,5,128,512]{3,2,1,0:T(8,128)} custom-call(f32[1,2,128,512]{3,2,1,0:T(8,128)S(1)} %get-tuple-element.35.left_ref, f32[1,2,128,512]{3,2,1,0:T(8,128)S(1)} %collective-permute-done.9.refs_0_, f32[1,5,128,512]{3,2,1,0:T(8,128)} %get-tuple-element.36.refs_1_), custom_call_target="tpu_custom_call", output_to_operand_aliasing={{}: (2, {})} | custom-call | flops 1 | bytes 1 | tf_op jit(solution)/shard_map/last_terms/pallas_call | solution.py:510
  (3 shorter events, 0.0 us)
Async XLA Ops:
  0.0 4.3 %copy-start = (f32[1,5,128,512]{3,2,1,0:T(8,128)S(1)}, f32[1,5,128,512]{3,2,1,0:T(8,128)}, u32[]{:S(2)}) copy-start(f32[1,5,128,512]{3,2,1,0:T(8,128)} %q_ref.5) | copy-start | bytes 3932164
  1.2 3.2 %copy-start.2 = (s32[8]{0:T(128)S(1)}, s32[8]{0:T(128)}, u32[]{:S(2)}) copy-start(s32[8]{0:T(128)} %owner_ref.7) | copy-start | bytes 100
  1.3 3.2 %copy-start.3 = (s32[8]{0:T(128)S(1)}, s32[8]{0:T(128)}, u32[]{:S(2)}) copy-start(s32[8]{0:T(128)} %rows_ref.7) | copy-start | bytes 100
  1.3 15.8 %collective-permute-start.1 = (f32[1,2,128,512]{3,2,1,0:T(8,128)S(1)}, f32[1,2,128,512]{3,2,1,0:T(8,128)S(1)}, u32[]{:S(2)}, u32[]{:S(2)}) collective-permute-start(f32[1,2,128,512]{3,2,1,0:T(8,128)S(1)} %part.1), channel_id=1, source_target_pairs={{0,2},{1,3},{2,0},{3,1},{4,6},{5,7},{6,4},{7,5},{8,10},{9,11},{10,... | collective-permute-start | bytes 1572872 | tf_op jit(solution)/shard_map/ppermute | solution.py:349
  4.4 2.5 %copy-start.4 = (f32[7]{0:T(128)S(1)}, f32[7]{0:T(128)}, u32[]{:S(2)}) copy-start(f32[7]{0:T(128)} %coef_ref.3) | copy-start | bytes 88
  4.4 12.6 %collective-permute-start.3 = (f32[1,2,128,512]{3,2,1,0:T(8,128)S(1)}, f32[1,2,128,512]{3,2,1,0:T(8,128)S(1)}, u32[]{:S(2)}, u32[]{:S(2)}) collective-permute-start(f32[1,2,128,512]{3,2,1,0:T(8,128)S(1)} %pad_maximum_fusion), channel_id=1, source_target_pairs={{0,1},{1,0},{2,3},{3,2},{4,5},{5,4},{6,7},{7,6},{8,9},{9,8},{10,11... | collective-permute-start | bytes 1572872 | tf_op jit(solution)/shard_map/ppermute | solution.py:366
  5.3 3.8 %collective-permute-start = (f32[1,2,16,128]{3,2,1,0:T(8,128)S(1)}, f32[1,2,16,128]{3,2,1,0:T(8,128)S(1)}, u32[]{:S(2)}, u32[]{:S(2)}) collective-permute-start(f32[1,2,16,128]{3,2,1,0:T(8,128)S(1)} %faces.1.refs_1_), channel_id=1, source_target_pairs={{0,4},{4,0},{8,12},{12,8},{16,20},{20,16},{24,28},{28,24},{1,5},{5... | collective-permute-start | bytes 49160 | tf_op jit(solution)/shard_map/ppermute | solution.py:455
  9.2 20.2 %collective-permute-start.7 = (f32[1,3,128,512]{3,2,1,0:T(8,128)S(1)}, f32[1,3,128,512]{3,2,1,0:T(8,128)S(1)}, u32[]{:S(2)}, u32[]{:S(2)}) collective-permute-start(f32[1,3,128,512]{3,2,1,0:T(8,128)S(1)} %slice.15), channel_id=1, source_target_pairs={{0,1},{1,0},{2,3},{3,2},{4,5},{5,4},{6,7},{7,6},{8,9},{9,8},{10,11... | collective-permute-start | bytes 2359304 | tf_op jit(solution)/shard_map/ppermute | solution.py:458
  9.5 7.1 %collective-permute-start.2 = (f32[2,2,16,128]{3,2,1,0:T(8,128)S(1)}, f32[2,2,16,128]{3,2,1,0:T(8,128)S(1)}, u32[]{:S(2)}, u32[]{:S(2)}) collective-permute-start(f32[2,2,16,128]{3,2,1,0:T(8,128)S(1)} %pad_maximum_fusion.2), channel_id=1, source_target_pairs={{0,8},{4,12},{8,0},{12,4},{16,24},{20,28},{24,16},{28,20},{1,9},{5... | collective-permute-start | bytes 98312 | tf_op jit(solution)/shard_map/ppermute | solution.py:455
  11.0 11.4 %collective-permute-start.5 = (f32[1,1,128,512]{3,2,1,0:T(8,128)S(1)}, f32[1,1,128,512]{3,2,1,0:T(8,128)S(1)}, u32[]{:S(2)}, u32[]{:S(2)}) collective-permute-start(f32[1,1,128,512]{3,2,1,0:T(8,128)S(1)} %get-tuple-element.37), channel_id=1, source_target_pairs={{0,2},{1,3},{2,0},{3,1},{4,6},{5,7},{6,4},{7,5},{8,10},{9,11},{10,... | collective-permute-start | bytes 786440 | tf_op jit(solution)/shard_map/ppermute | solution.py:349
  17.6 7.7 %collective-permute-start.4 = (f32[1,2,128,512]{3,2,1,0:T(8,128)S(1)}, f32[1,2,128,512]{3,2,1,0:T(8,128)S(1)}, u32[]{:S(2)}, u32[]{:S(2)}) collective-permute-start(f32[1,2,128,512]{3,2,1,0:T(8,128)S(1)} %collective-permute-done.1.refs_1_.refs_0_), channel_id=1, source_target_pairs={{0,1},{1,0},{2,3},{3,2},{4,5},{5,4},{6,7},{7,6},{8,9},{9,8},{10,11... | collective-permute-start | bytes 1572872 | tf_op jit(solution)/shard_map/ppermute | solution.py:475
  17.7 15.3 %collective-permute-start.9 = (f32[1,2,128,512]{3,2,1,0:T(8,128)S(1)}, f32[1,2,128,512]{3,2,1,0:T(8,128)S(1)}, u32[]{:S(2)}, u32[]{:S(2)}) collective-permute-start(f32[1,2,128,512]{3,2,1,0:T(8,128)S(1)} %send_terms.1), channel_id=1, source_target_pairs={{0,2},{1,3},{2,0},{3,1},{4,6},{5,7},{6,4},{7,5},{8,10},{9,11},{10,... | collective-permute-start | bytes 1572872 | tf_op jit(solution)/shard_map/ppermute | solution.py:471
  22.4 2.9 %collective-permute-start.6 = (f32[1,1,128,512]{3,2,1,0:T(8,128)S(1)}, f32[1,1,128,512]{3,2,1,0:T(8,128)S(1)}, u32[]{:S(2)}, u32[]{:S(2)}) collective-permute-start(f32[1,1,128,512]{3,2,1,0:T(8,128)S(1)} %collective-permute-done.5.refs_2_), channel_id=1, source_target_pairs={{0,1},{1,0},{2,3},{3,2},{4,5},{5,4},{6,7},{7,6},{8,9},{9,8},{10,11... | collective-permute-start | bytes 786440 | tf_op jit(solution)/shard_map/ppermute | solution.py:476
  22.4 7.0 %collective-permute-start.8 = (f32[4,2,16,128]{3,2,1,0:T(8,128)S(1)}, f32[4,2,16,128]{3,2,1,0:T(8,128)S(1)}, u32[]{:S(2)}, u32[]{:S(2)}) collective-permute-start(f32[4,2,16,128]{3,2,1,0:T(8,128)S(1)} %pad_maximum_fusion.1), channel_id=1, source_target_pairs={{0,16},{4,20},{8,24},{12,28},{16,0},{20,4},{24,8},{28,12},{1,17},{... | collective-permute-start | bytes 196616 | tf_op jit(solution)/shard_map/ppermute | solution.py:455
  25.3 4.1 %copy-start.1 = (f32[6,1024]{1,0:T(8,128)S(1)}, f32[6,1024]{1,0:T(8,128)}, u32[]{:S(2)}) copy-start(f32[6,1024]{1,0:T(8,128)} %gop_ref.1) | copy-start | bytes 73732
  25.3 4.1 %copy-start.5 = (s32[8,2]{0,1:T(2,128)S(1)}, s32[8,2]{0,1:T(2,128)}, u32[]{:S(2)}) copy-start(s32[8,2]{0,1:T(2,128)} %param.11) | copy-start | bytes 196
  25.4 4.1 %copy-start.6 = (s32[8,2]{0,1:T(2,128)S(1)}, s32[8,2]{0,1:T(2,128)}, u32[]{:S(2)}) copy-start(s32[8,2]{0,1:T(2,128)} %param.12) | copy-start | bytes 196

commit v3 on v1

--- a/solution.py
+++ b/solution.py
@@ -44,18 +44,22 @@
     )
 
 
-def faces_kernel(owner_ref, rows_ref, low_ref, high_ref, out_ref):
-    nvar, rows, lanes = low_ref.shape[1:]
+def faces_kernel(owner_ref, rows_ref, part_ref, q_ref, held_ref, out_ref, sems):
+    nvar, rows, x_length = held_ref.shape[1:]
+    copies = [pltpu.make_async_copy(q_ref.at[0, v], held_ref.at[0, v], sems.at[v]) for v in range(nvar)]
+    for copy in copies:
+        copy.start()
     live_rows = rows_ref[find_block(owner_ref, lax.axis_index("blk"))]
     y_index = lax.axis_index("line") * rows + lax.broadcasted_iota(jnp.int32, (GHOST, rows), 1)
     live = y_index < live_rows
+    for m in range(2):
+        out_ref[0, m, GHOST * nvar :, :] = jnp.zeros((FACE_ROWS - GHOST * nvar, rows), jnp.float32)
     for v in range(nvar):
-        low = jnp.transpose(low_ref[0, v])[:GHOST]
-        high = jnp.transpose(high_ref[0, v])[lanes - GHOST :]
+        copies[v].wait()
+        low = jnp.transpose(held_ref[0, v, :, :LANES])[:GHOST]
+        high = jnp.transpose(held_ref[0, v, :, x_length - LANES :])[LANES - GHOST :]
         out_ref[0, 0, GHOST * v : GHOST * (v + 1), :] = jnp.where(live, low, 0.0)
         out_ref[0, 1, GHOST * v : GHOST * (v + 1), :] = jnp.where(live, high, 0.0)
-    for m in range(2):
-        out_ref[0, m, GHOST * nvar :, :] = jnp.zeros((FACE_ROWS - GHOST * nvar, rows), jnp.float32)
 
 
 def part_kernel(low, q_ref, out_ref, sem):
@@ -346,30 +350,24 @@
         cost_estimate=small,
         name="part",
     )(pltpu.with_memory_space_constraint(flow_state, HBM))
-    part, flow_state = lax.optimization_barrier((part, flow_state))
     direct_first = across(part)
+
+    in_hbm = pltpu.with_memory_space_constraint(flow_state, HBM)
+    flow_state, faces = pl.pallas_call(
+        faces_kernel,
+        in_specs=[smem(), smem(), kept(), pl.BlockSpec(memory_space=pl.ANY)],
+        out_specs=[kept(), kept()],
+        out_shape=[state_shape, jax.ShapeDtypeStruct((1, 2, FACE_ROWS, rows), jnp.float32)],
+        scratch_shapes=[pltpu.SemaphoreType.DMA((nvar,))],
+        compiler_params=limit,
+        cost_estimate=small,
+        name="faces",
+    )(block_owner, rows_live, held(part), in_hbm)
     second = flow_state[:, SECOND[0] : SECOND[1]]
     direct_second = across(second)
     near_sent = lax.ppermute(
         jnp.concatenate([flow_state[:, v : v + 1] for v in SENT], axis=1), "line", sibling
     )
-
-    last = x_length // LANES - 1
-    faces = pl.pallas_call(
-        faces_kernel,
-        grid=(1,),
-        in_specs=[
-            smem(),
-            smem(),
-            pl.BlockSpec((1, nvar, rows, LANES), lambda i: (0, 0, 0, 0)),
-            pl.BlockSpec((1, nvar, rows, LANES), lambda i: (0, 0, 0, last)),
-        ],
-        out_specs=pl.BlockSpec((1, 2, FACE_ROWS, rows), lambda i: (0, 0, 0, 0)),
-        out_shape=jax.ShapeDtypeStruct((1, 2, FACE_ROWS, rows), jnp.float32),
-        compiler_params=limit,
-        cost_estimate=small,
-        name="faces",
-    )(block_owner, rows_live, flow_state, flow_state)
 
     w_near = jax.ShapeDtypeStruct((2 * rows, 3 * rows), jnp.bfloat16)
     w_far = jax.ShapeDtypeStruct((2 * rows, 3 * len(shifts) * rows), jnp.bfloat16)
@@ -459,6 +457,7 @@
         for s, result in zip(shifts, results)
     ]
 
+    direct_second, *_ = lax.optimization_barrier((direct_second, *arrived))
     passed_first = [lax.ppermute(piece, "line", sibling) for piece in direct_first]
     passed_second = [lax.ppermute(piece, "line", sibling) for piece in direct_second]
     pieces = [*direct_first, *passed_first, *direct_second, *passed_second]

time: 34 us -> 33.9 us (level)
  Pallas kernels: 14 us -> 15.1 us
  starting transfers between devices: 12.1 us -> 11.2 us
    ppermute x2, waiting for transfers between devices: 3 us -> 0.01 us  [across(): lax.ppermute(array, 'line', [(i, (i + s) % lines) for i in range(lines)])]
    ppermute x2, waiting for transfers between devices: 0.01 us -> 1.54 us  [on_device(): lax.ppermute(piece, 'line', sibling)]
    pallas_call x1, Pallas kernels: 0.85 us -> 2.04 us  [on_device(): pl.pallas_call(faces_kernel, in_specs=[smem(), smem(), kept(), pl.BlockSp...]
    ppermute x3, waiting for transfers between devices: 3.04 us -> 4 us  [on_device(): lax.ppermute(held_faces, 'blk', [(i, i ^ step) for i in range(slots)])]
    ppermute x1, starting transfers between devices: 2.13 us -> 1.56 us  [on_device(): lax.ppermute(result, 'line', [(i, (i + s) % lines) for i in range(lines)])]
  transfers between devices with their start and end apart: 10 -> 10, of which waited for: 4 -> 3; matrix products, arithmetic and copies ran while one was open for 0% -> 0% of each run, Pallas kernels for 36% -> 39%
where the time goes in v3:
time: 33.9 us; the launch traced here: 33.7 us
  Pallas kernels  15.1 us (45%)
  starting transfers between devices  11.2 us (33%)
  waiting for transfers between devices  6.99 us (21%)
    ppermute x3, starting transfers between devices, on_device(): lax.ppermute(held_faces, 'blk', [(i, i ^ step) for i in range(slots)])  5.75 us
    pallas_call x1, Pallas kernels, own_terms(): pl.pallas_call(own_kernel, grid=(tiles,), in_specs=[smem()] * 3 + [pl.Blo...  5.02 us
    ppermute x3, waiting for transfers between devices, on_device(): lax.ppermute(held_faces, 'blk', [(i, i ^ step) for i in range(slots)])  4 us
    ppermute x2, starting transfers between devices, across(): lax.ppermute(array, 'line', [(i, (i + s) % lines) for i in range(lines)])  3.54 us
    pallas_call x1, Pallas kernels, on_device(): pl.pallas_call(functools.partial(near_kernel, len(arrived)), in_specs=[sm...  2.35 us
    pallas_call x1, Pallas kernels, on_device(): pl.pallas_call(functools.partial(weights_kernel, lines), in_specs=[smem()...  2.19 us
    pallas_call x1, Pallas kernels, on_device(): pl.pallas_call(faces_kernel, in_specs=[smem(), smem(), kept(), pl.BlockSp...  2.04 us
    ppermute x1, starting transfers between devices, on_device(): lax.ppermute(result, 'line', [(i, (i + s) % lines) for i in range(lines)])  1.56 us
  transfers between devices with their start and end apart: 10, of which 3 were waited for; matrix products, arithmetic and copies ran while one was open for 0% of the time, Pallas kernels for 39%

profile of v3, /device:TPU:0, one launch (start us, length us, event | category | flops | bytes accessed | tf_op | source)
XLA Modules:
  0.0 33.7 jit_solution(5023712167268845936)
XLA Ops:
  0.0 0.0 copy-start.1
  0.0 0.0 copy-start.2
  0.0 1.1 %part.1.part_ref = f32[1,2,128,512]{3,2,1,0:T(8,128)S(1)} custom-call(f32[1,5,128,512]{3,2,1,0:T(8,128)} %q_ref.3), custom_call_target="tpu_custom_call" | custom-call | flops 1 | bytes 1 | tf_op jit(solution)/shard_map/part/pallas_call | solution.py:343
  1.1 3.0 %collective-permute-start.1 = (f32[1,2,128,512]{3,2,1,0:T(8,128)S(1)}, f32[1,2,128,512]{3,2,1,0:T(8,128)S(1)}, u32[]{:S(2)}, u32[]{:S(2)}) collective-permute-start(f32[1,2,128,512]{3,2,1,0:T(8,128)S(1)} %part.1.part_ref), channel_id=1, source_target_pairs={{0,2},{1,3},{2,0},{3,1},{4,6},{5,7},{6,4},{7,5},{8,10},{9,11},{10,... | collective-permute-start | bytes 1572872 | tf_op jit(solution)/shard_map/ppermute | solution.py:340
  4.1 0.0 copy-done.1
  4.1 0.0 copy-done.2
  4.1 2.0 %faces.1 = (f32[1,5,128,512]{3,2,1,0:T(8,128)S(1)}, f32[1,2,16,128]{3,2,1,0:T(8,128)S(1)}) custom-call(s32[8]{0:T(128)S(1)} %copy-done.1, s32[8]{0:T(128)S(1)} %copy-done.2, f32[1,2,128,512]{3,2,1,0:T(8,128)S(1)} %part.1.part_ref, f32[1,5,128,512]{3,2,1,0:T(8,128)} %q_ref.3), custom_call_target="tpu_custom_call" | custom-call | flops 1 | bytes 1 | tf_op jit(solution)/shard_map/faces/pallas_call | solution.py:356
  6.2 0.0 copy-start.3
  6.2 0.1 fusion
  6.3 0.1 collective-permute-start.3
  6.3 1.6 %collective-permute-start = (f32[1,2,16,128]{3,2,1,0:T(8,128)S(1)}, f32[1,2,16,128]{3,2,1,0:T(8,128)S(1)}, u32[]{:S(2)}, u32[]{:S(2)}) collective-permute-start(f32[1,2,16,128]{3,2,1,0:T(8,128)S(1)} %get-tuple-element.27.refs_1_), channel_id=1, source_target_pairs={{0,4},{4,0},{8,12},{12,8},{16,20},{20,16},{24,28},{28,24},{1,5},{5... | collective-permute-start | bytes 49160 | tf_op jit(solution)/shard_map/ppermute | solution.py:440
  7.9 0.0 copy-done.3
  7.9 2.2 %weights.1 = (bf16[256,384]{1,0:T(8,128)(2,1)S(1)}, bf16[256,384]{1,0:T(8,128)(2,1)S(1)}, bf16[256,384]{1,0:T(8,128)(2,1)S(1)}, bf16[256,384]{1,0:T(8,128)(2,1)S...) custom-call(s32[8]{0:T(128)S(1)} %copy-done.1, s32[8]{0:T(128)S(1)} %copy-done.2, f32[7]{0:T(128)S(1)} %copy-done.3, ...), custom_call_target="tpu_custom_call" | custom-call | flops 1 | bytes 1 | tf_op jit(solution)/shard_map/weights/pallas_call | solution.py:376
  10.1 0.0 collective-permute-done.refs_2_
  10.2 0.1 slice.15
  10.2 0.2 collective-permute-start.8
  10.4 1.6 %collective-permute-start.2 = (f32[2,2,16,128]{3,2,1,0:T(8,128)S(1)}, f32[2,2,16,128]{3,2,1,0:T(8,128)S(1)}, u32[]{:S(2)}, u32[]{:S(2)}) collective-permute-start(f32[2,2,16,128]{3,2,1,0:T(8,128)S(1)} %pad_maximum_fusion.2), channel_id=1, source_target_pairs={{0,8},{4,12},{8,0},{12,4},{16,24},{20,28},{24,16},{28,20},{1,9},{5... | collective-permute-start | bytes 98312 | tf_op jit(solution)/shard_map/ppermute | solution.py:440
  12.0 0.5 %collective-permute-start.5 = (f32[1,1,128,512]{3,2,1,0:T(8,128)S(1)}, f32[1,1,128,512]{3,2,1,0:T(8,128)S(1)}, u32[]{:S(2)}, u32[]{:S(2)}) collective-permute-start(f32[1,1,128,512]{3,2,1,0:T(8,128)S(1)} %get-tuple-element.39), channel_id=1, source_target_pairs={{0,2},{1,3},{2,0},{3,1},{4,6},{5,7},{6,4},{7,5},{8,10},{9,11},{10,... | collective-permute-start | bytes 786440 | tf_op jit(solution)/shard_map/ppermute | solution.py:340
  12.6 5.0 %own_terms.1.base_ref = f32[1,5,128,512]{3,2,1,0:T(8,128)S(1)} custom-call(s32[8]{0:T(128)S(1)} %copy-done.1, s32[8]{0:T(128)S(1)} %copy-done.2, f32[7]{0:T(128)S(1)} %copy-done.3, bf16[256,384]{1,0:T(8,128)(2,1)S(1)} %get-tuple-element.29.wown_ref, f32[1,5,128,512]{3,2,1,0:T(8,128)S(1)} %get-tuple-element.36.q_ref.tile_ref, ...), custom_call_target="tpu_custom_call" | custom-call | flops 1 | bytes 1 | tf_op jit(solution)/shard_map/own_terms/pallas_call | solution.py:396
  17.6 0.0 collective-permute-done.2.refs_3_
  17.6 0.0 collective-permute-done.1.refs_1_.refs_0_
  17.6 0.0 collective-permute-done.3.refs_0_
  17.6 0.6 %send_terms.1 = f32[1,2,128,512]{3,2,1,0:T(8,128)S(1)} custom-call(bf16[1,256,768]{2,1,0:T(8,128)(2,1)S(1)} %get-tuple-element.32.wsend_ref, f32[5,8,512]{2,1,0:T(8,128)S(1)} %get-tuple-element.23.nu_ref, f32[1,5,128,512]{3,2,1,0:T(8,128)S(1)} %get-tuple-element.36.q_ref.tile_ref, f32[1,2,128,512]{3,2,1,0:T(8,128)S(1)} %collective-permute-done.3.refs_0_, ...), custom_call_target="tpu_custom_call" | custom-call | flops 1 | bytes 1 | tf_op jit(solution)/shard_map/send_terms/pallas_call | solution.py:447
  18.2 0.1 collective-permute-start.4
  18.3 1.6 %collective-permute-start.9 = (f32[1,2,128,512]{3,2,1,0:T(8,128)S(1)}, f32[1,2,128,512]{3,2,1,0:T(8,128)S(1)}, u32[]{:S(2)}, u32[]{:S(2)}) collective-permute-start(f32[1,2,128,512]{3,2,1,0:T(8,128)S(1)} %send_terms.1), channel_id=1, source_target_pairs={{0,2},{1,3},{2,0},{3,1},{4,6},{5,7},{6,4},{7,5},{8,10},{9,11},{10,... | collective-permute-start | bytes 1572872 | tf_op jit(solution)/shard_map/ppermute | solution.py:456
  19.9 2.6 %collective-permute-start.6 = (f32[4,2,16,128]{3,2,1,0:T(8,128)S(1)}, f32[4,2,16,128]{3,2,1,0:T(8,128)S(1)}, u32[]{:S(2)}, u32[]{:S(2)}) collective-permute-start(f32[4,2,16,128]{3,2,1,0:T(8,128)S(1)} %pad_maximum_fusion.1), channel_id=1, source_target_pairs={{0,16},{4,20},{8,24},{12,28},{16,0},{20,4},{24,8},{28,12},{1,17},{... | collective-permute-start | bytes 196616 | tf_op jit(solution)/shard_map/ppermute | solution.py:440
  22.5 0.0 collective-permute-done.5.refs_2_
  22.5 4.0 %collective-permute-done.6.refs_4_ = f32[4,2,16,128]{3,2,1,0:T(8,128)S(1)} collective-permute-done((f32[4,2,16,128]{3,2,1,0:T(8,128)S(1)}, f32[4,2,16,128]{3,2,1,0:T(8,128)S(1)}, u32[]{:S(2)}, u32[]{:S(2)}) %collective-permute-start.6) | collective-permute-done | bytes 65568 | tf_op jit(solution)/shard_map/ppermute | solution.py:440
  26.4 0.0 collective-permute-start.7
  26.4 1.5 %collective-permute-done.7.refs_3_ = f32[1,1,128,512]{3,2,1,0:T(8,128)S(1)} collective-permute-done((f32[1,1,128,512]{3,2,1,0:T(8,128)S(1)}, f32[1,1,128,512]{3,2,1,0:T(8,128)S(1)}, u32[]{:S(2)}, u32[]{:S(2)}) %collective-permute-start.7) | collective-permute-done | bytes 262176 | tf_op jit(solution)/shard_map/ppermute | solution.py:462
  28.0 0.0 collective-permute-done.4.refs_1_
  28.0 0.0 copy-start
  28.0 0.0 copy-start.4
  28.0 0.0 copy-start.5
  28.0 1.0 %raw_terms.1.base_ref = f32[1,5,128,512]{3,2,1,0:T(8,128)S(1)} custom-call(bf16[256,384]{1,0:T(8,128)(2,1)S(1)} %get-tuple-element.25.wdirect_ref, bf16[256,384]{1,0:T(8,128)(2,1)S(1)} %get-tuple-element.26.wpassed_ref, f32[5,8,512]{2,1,0:T(8,128)S(1)} %get-tuple-element.23.nu_ref, f32[1,5,128,512]{3,2,1,0:T(8,128)S(1)} %get-tuple-element.36.q_ref.tile_ref, ...), custom_call_target="tpu_custom_call" | custom-call | flops 1 | bytes 1 | tf_op jit(solution)/shard_map/raw_terms/pallas_call | solution.py:464
  29.0 0.0 collective-permute-done.8.near_raw_ref
  29.0 0.0 copy-done
  29.0 0.0 copy-done.4
  29.1 0.0 copy-done.5
  29.1 2.3 %near_terms.1 = (f32[1,5,128,512]{3,2,1,0:T(8,128)}, f32[1,2,128,512]{3,2,1,0:T(8,128)S(1)}) custom-call(s32[8]{0:T(128)S(1)} %copy-done.1, s32[2,8]{1,0:T(2,128)S(1)} %bitcast.2, s32[2,8]{1,0:T(2,128)S(1)} %bitcast.3, s32[8]{0:T(128)S(1)} %copy-done.2, f32[6,1024]{1,0:T(8,128)S(1)} %copy-done, bf16[256,384]{1,0:T(8,128)(2,1)S(1)} %get-tuple-element.22.wnear_ref, ...), custom_call_target="tpu_custom_call" | custom-call | flops 1 | bytes 1 | tf_op jit(solution)/shard_map/near_terms/pallas_call | solution.py:475
  31.4 1.4 %collective-permute-done.9.refs_0_ = f32[1,2,128,512]{3,2,1,0:T(8,128)S(1)} collective-permute-done((f32[1,2,128,512]{3,2,1,0:T(8,128)S(1)}, f32[1,2,128,512]{3,2,1,0:T(8,128)S(1)}, u32[]{:S(2)}, u32[]{:S(2)}) %collective-permute-start.9) | collective-permute-done | bytes 524320 | tf_op jit(solution)/shard_map/ppermute | solution.py:456
  32.9 0.8 %last_terms.1 = f32[1,5,128,512]{3,2,1,0:T(8,128)} custom-call(f32[1,2,128,512]{3,2,1,0:T(8,128)S(1)} %get-tuple-element.37.left_ref, f32[1,2,128,512]{3,2,1,0:T(8,128)S(1)} %collective-permute-done.9.refs_0_, f32[1,5,128,512]{3,2,1,0:T(8,128)} %get-tuple-element.38.refs_1_), custom_call_target="tpu_custom_call", output_to_operand_aliasing={{}: (2, {})} | custom-call | flops 1 | bytes 1 | tf_op jit(solution)/shard_map/last_terms/pallas_call | solution.py:496
  (3 shorter events, 0.0 us)
Async XLA Ops:
  0.0 4.1 %copy-start.1 = (s32[8]{0:T(128)S(1)}, s32[8]{0:T(128)}, u32[]{:S(2)}) copy-start(s32[8]{0:T(128)} %owner_ref.7) | copy-start | bytes 100
  0.0 4.1 %copy-start.2 = (s32[8]{0:T(128)S(1)}, s32[8]{0:T(128)}, u32[]{:S(2)}) copy-start(s32[8]{0:T(128)} %rows_ref.7) | copy-start | bytes 100
  1.1 16.5 %collective-permute-start.1 = (f32[1,2,128,512]{3,2,1,0:T(8,128)S(1)}, f32[1,2,128,512]{3,2,1,0:T(8,128)S(1)}, u32[]{:S(2)}, u32[]{:S(2)}) collective-permute-start(f32[1,2,128,512]{3,2,1,0:T(8,128)S(1)} %part.1.part_ref), channel_id=1, source_target_pairs={{0,2},{1,3},{2,0},{3,1},{4,6},{5,7},{6,4},{7,5},{8,10},{9,11},{10,... | collective-permute-start | bytes 1572872 | tf_op jit(solution)/shard_map/ppermute | solution.py:340
  6.2 1.8 %copy-start.3 = (f32[7]{0:T(128)S(1)}, f32[7]{0:T(128)}, u32[]{:S(2)}) copy-start(f32[7]{0:T(128)} %coef_ref.3) | copy-start | bytes 88
  6.3 11.3 %collective-permute-start.3 = (f32[1,2,128,512]{3,2,1,0:T(8,128)S(1)}, f32[1,2,128,512]{3,2,1,0:T(8,128)S(1)}, u32[]{:S(2)}, u32[]{:S(2)}) collective-permute-start(f32[1,2,128,512]{3,2,1,0:T(8,128)S(1)} %pad_maximum_fusion), channel_id=1, source_target_pairs={{0,1},{1,0},{2,3},{3,2},{4,5},{5,4},{6,7},{7,6},{8,9},{9,8},{10,11... | collective-permute-start | bytes 1572872 | tf_op jit(solution)/shard_map/ppermute | solution.py:368
  6.3 3.8 %collective-permute-start = (f32[1,2,16,128]{3,2,1,0:T(8,128)S(1)}, f32[1,2,16,128]{3,2,1,0:T(8,128)S(1)}, u32[]{:S(2)}, u32[]{:S(2)}) collective-permute-start(f32[1,2,16,128]{3,2,1,0:T(8,128)S(1)} %get-tuple-element.27.refs_1_), channel_id=1, source_target_pairs={{0,4},{4,0},{8,12},{12,8},{16,20},{20,16},{24,28},{28,24},{1,5},{5... | collective-permute-start | bytes 49160 | tf_op jit(solution)/shard_map/ppermute | solution.py:440
  10.2 18.8 %collective-permute-start.8 = (f32[1,3,128,512]{3,2,1,0:T(8,128)S(1)}, f32[1,3,128,512]{3,2,1,0:T(8,128)S(1)}, u32[]{:S(2)}, u32[]{:S(2)}) collective-permute-start(f32[1,3,128,512]{3,2,1,0:T(8,128)S(1)} %slice.15), channel_id=1, source_target_pairs={{0,1},{1,0},{2,3},{3,2},{4,5},{5,4},{6,7},{7,6},{8,9},{9,8},{10,11... | collective-permute-start | bytes 2359304 | tf_op jit(solution)/shard_map/ppermute | solution.py:443
  10.4 7.1 %collective-permute-start.2 = (f32[2,2,16,128]{3,2,1,0:T(8,128)S(1)}, f32[2,2,16,128]{3,2,1,0:T(8,128)S(1)}, u32[]{:S(2)}, u32[]{:S(2)}) collective-permute-start(f32[2,2,16,128]{3,2,1,0:T(8,128)S(1)} %pad_maximum_fusion.2), channel_id=1, source_target_pairs={{0,8},{4,12},{8,0},{12,4},{16,24},{20,28},{24,16},{28,20},{1,9},{5... | collective-permute-start | bytes 98312 | tf_op jit(solution)/shard_map/ppermute | solution.py:440
  12.0 10.4 %collective-permute-start.5 = (f32[1,1,128,512]{3,2,1,0:T(8,128)S(1)}, f32[1,1,128,512]{3,2,1,0:T(8,128)S(1)}, u32[]{:S(2)}, u32[]{:S(2)}) collective-permute-start(f32[1,1,128,512]{3,2,1,0:T(8,128)S(1)} %get-tuple-element.39), channel_id=1, source_target_pairs={{0,2},{1,3},{2,0},{3,1},{4,6},{5,7},{6,4},{7,5},{8,10},{9,11},{10,... | collective-permute-start | bytes 786440 | tf_op jit(solution)/shard_map/ppermute | solution.py:340
  18.2 9.8 %collective-permute-start.4 = (f32[1,2,128,512]{3,2,1,0:T(8,128)S(1)}, f32[1,2,128,512]{3,2,1,0:T(8,128)S(1)}, u32[]{:S(2)}, u32[]{:S(2)}) collective-permute-start(f32[1,2,128,512]{3,2,1,0:T(8,128)S(1)} %collective-permute-done.1.refs_1_.refs_0_), channel_id=1, source_target_pairs={{0,1},{1,0},{2,3},{3,2},{4,5},{5,4},{6,7},{7,6},{8,9},{9,8},{10,11... | collective-permute-start | bytes 1572872 | tf_op jit(solution)/shard_map/ppermute | solution.py:461
  18.3 14.6 %collective-permute-start.9 = (f32[1,2,128,512]{3,2,1,0:T(8,128)S(1)}, f32[1,2,128,512]{3,2,1,0:T(8,128)S(1)}, u32[]{:S(2)}, u32[]{:S(2)}) collective-permute-start(f32[1,2,128,512]{3,2,1,0:T(8,128)S(1)} %send_terms.1), channel_id=1, source_target_pairs={{0,2},{1,3},{2,0},{3,1},{4,6},{5,7},{6,4},{7,5},{8,10},{9,11},{10,... | collective-permute-start | bytes 1572872 | tf_op jit(solution)/shard_map/ppermute | solution.py:456
  19.9 6.6 %collective-permute-start.6 = (f32[4,2,16,128]{3,2,1,0:T(8,128)S(1)}, f32[4,2,16,128]{3,2,1,0:T(8,128)S(1)}, u32[]{:S(2)}, u32[]{:S(2)}) collective-permute-start(f32[4,2,16,128]{3,2,1,0:T(8,128)S(1)} %pad_maximum_fusion.1), channel_id=1, source_target_pairs={{0,16},{4,20},{8,24},{12,28},{16,0},{20,4},{24,8},{28,12},{1,17},{... | collective-permute-start | bytes 196616 | tf_op jit(solution)/shard_map/ppermute | solution.py:440
  26.4 1.5 %collective-permute-start.7 = (f32[1,1,128,512]{3,2,1,0:T(8,128)S(1)}, f32[1,1,128,512]{3,2,1,0:T(8,128)S(1)}, u32[]{:S(2)}, u32[]{:S(2)}) collective-permute-start(f32[1,1,128,512]{3,2,1,0:T(8,128)S(1)} %collective-permute-done.5.refs_2_), channel_id=1, source_target_pairs={{0,1},{1,0},{2,3},{3,2},{4,5},{5,4},{6,7},{7,6},{8,9},{9,8},{10,11... | collective-permute-start | bytes 786440 | tf_op jit(solution)/shard_map/ppermute | solution.py:462
  28.0 1.1 %copy-start = (f32[6,1024]{1,0:T(8,128)S(1)}, f32[6,1024]{1,0:T(8,128)}, u32[]{:S(2)}) copy-start(f32[6,1024]{1,0:T(8,128)} %gop_ref.1) | copy-start | bytes 73732
  28.0 1.1 %copy-start.4 = (s32[8,2]{0,1:T(2,128)S(1)}, s32[8,2]{0,1:T(2,128)}, u32[]{:S(2)}) copy-start(s32[8,2]{0,1:T(2,128)} %param.11) | copy-start | bytes 196
  28.0 1.1 %copy-start.5 = (s32[8,2]{0,1:T(2,128)S(1)}, s32[8,2]{0,1:T(2,128)}, u32[]{:S(2)}) copy-start(s32[8,2]{0,1:T(2,128)} %param.12) | copy-start | bytes 196

commit v4 on v3

--- a/solution.py
+++ b/solution.py
@@ -77,7 +77,7 @@
     wown_ref,
     wnear_ref,
     wdirect_ref,
-    wpassed_ref,
+    wsibling_ref,
     wsend_ref,
     nu_ref,
     columns_ref,
@@ -101,9 +101,11 @@
     for d in range(2):
         source = yop_ref.at[:, column(d, line_pos)]
         copies.append(pltpu.make_async_copy(source, columns_ref.at[d], sems.at[d]))
-    for j, target in enumerate(targets):
+    direct = [lax.rem(line_pos + lines - s, lines) for s in shifts]
+    others = [(target, [line_pos, other]) for target in targets] + [(other, [line_pos] + direct)]
+    for j, (target, sources) in enumerate(others):
         for d in range(2):
-            for i, line in enumerate((line_pos, other)):
+            for i, line in enumerate(sources):
                 source = yop_ref.at[pl.ds(pl.multiple_of(line * rows, 8), rows), column(d, target)]
                 goal = theirs_ref.at[j, d, i * rows : (i + 1) * rows]
                 copies.append(pltpu.make_async_copy(source, goal, sems.at[len(copies)]))
@@ -135,20 +137,21 @@
 
     gather(wown_ref, [line_pos])
     gather(wnear_ref, [other])
-    gather(wdirect_ref, [lax.rem(line_pos + lines - s, lines) for s in shifts])
-    gather(wpassed_ref, [lax.rem(other + lines - s, lines) for s in shifts])
-
-    shape = (rows, rows)
-    ins = [line * rows + lax.broadcasted_iota(jnp.int32, shape, 1) for line in (line_pos, other)]
-    live_in = jnp.concatenate(ins, axis=1) < live_rows
-    for j, target in enumerate(targets):
+    gather(wdirect_ref, direct)
+
+    for j, (target, sources) in enumerate(others):
+        depth = len(sources) * rows
+        shape = (rows, rows)
+        ins = [line * rows + lax.broadcasted_iota(jnp.int32, shape, 1) for line in sources]
+        live_in = jnp.concatenate(ins, axis=1) < live_rows
         live_out = target * rows + lax.broadcasted_iota(jnp.int32, live_in.shape, 0) < live_rows
         offset = pl.multiple_of(lax.rem(target * rows, LANES), 8)
+        goal = wsend_ref.at[j] if j < len(targets) else wsibling_ref
         for d in range(2):
-            turned_ref[d, :, : 2 * rows] = jnp.transpose(theirs_ref[j, d])
-            mine = turned_ref[d, pl.ds(offset, rows), : 2 * rows]
+            turned_ref[d, :, :depth] = jnp.transpose(theirs_ref[j, d, :depth])
+            mine = turned_ref[d, pl.ds(offset, rows), :depth]
             hi, lo = split_bf16(jnp.where(live_in & live_out, SECTION_STEP * mine, 0.0))
-            wsend_ref[j, d * rows : (d + 1) * rows] = jnp.concatenate([hi, lo, hi], axis=1)
+            goal[d * rows : (d + 1) * rows] = jnp.concatenate([hi, lo, hi], axis=1)
 
 
 def own_kernel(
@@ -200,16 +203,20 @@
     rows_ref,
     gop_ref,
     wnear_ref,
+    wdirect_ref,
     nu_ref,
     q_ref,
     base_ref,
-    near_raw_ref,
+    near_ref,
     *refs,
 ):
-    near_sent, refs = refs[0], refs[1:]
-    faces, (out_ref, left_ref, done_ref, sems) = refs[:face_count], refs[face_count:]
-    near = {v: near_sent.at[0, i] for i, v in enumerate(SENT)}
-    near.update({v: near_raw_ref.at[0, i] for i, v in enumerate(RAW)})
+    faces, refs = refs[:face_count], refs[face_count:]
+    *refs, out_ref, left_ref, done_ref, sems = refs
+    count = len(refs) // 2 - 1
+    raw = {}
+    for (low, high), parts in ((FIRST, refs[: count + 1]), (SECOND, refs[count + 1 :])):
+        for v in range(low, high):
+            raw[v] = [ref.at[0, v - low] for ref in parts]
     nvar, rows, x_length = q_ref.shape[1:]
     my_slot = lax.axis_index("blk")
     my_block = find_block(owner_ref, my_slot)
@@ -254,14 +261,18 @@
         stacked = [hi.astype(jnp.float32), lo.astype(jnp.float32), hi.astype(jnp.float32)]
         ghost = jnp.transpose(jnp.concatenate(stacked + [pad], axis=0)).astype(jnp.bfloat16)
         dx = dot(ghost, operator)
-        dy = dot(wnear_ref[...], three_parts([near[v][...]]))
+        if v in SENT:
+            dy = dot(wnear_ref[...], three_parts([near_ref[0, SENT.index(v)]]))
+        else:
+            *direct, from_sibling = raw[v]
+            dy = dot(wdirect_ref[...], three_parts([ref[...] for ref in direct]))
         second = nu_ref[v, 0:1] * (dx[:, x_length:] + dy[rows:])
         value = base_ref[0, v] + second - q_ref[0, 0] * dx[:, :x_length] - q_ref[0, 1] * dy[:rows]
         if v in SENT:
             left_ref[0, SENT.index(v)] = value
             continue
         i = RAW.index(v)
-        done_ref[i] = value
+        done_ref[i] = value + from_sibling[...]
         copies.append(pltpu.make_async_copy(done_ref.at[i], out_ref.at[0, v], sems.at[i]))
         copies[-1].start()
     for copy in copies:
@@ -279,17 +290,13 @@
             out[j][0, i] = nu_ref[v, 0:1] * dy[rows:] - far_v[j][0, 0] * dy[:rows]
 
 
-def raw_kernel(count, wdirect_ref, wpassed_ref, nu_ref, q_ref, base_ref, *refs):
-    out_ref = refs[-1]
+def sibling_kernel(low, high, w_ref, nu_ref, q_ref, near_v_ref, *refs):
+    direct, out_ref = refs[:-1], refs[-1]
     rows = q_ref.shape[2]
-    first, second = [(refs[k : k + count], refs[k + count : k + 2 * count]) for k in (0, 2 * count)]
-    for (low, high), (direct, passed) in ((FIRST, first), (SECOND, second)):
-        for v in range(low, high):
-            dy = dot(wdirect_ref[...], three_parts([piece[0, v - low] for piece in direct]))
-            dy = dy + dot(wpassed_ref[...], three_parts([piece[0, v - low] for piece in passed]))
-            out_ref[0, v] = base_ref[0, v] + nu_ref[v, 0:1] * dy[rows:] - q_ref[0, 1] * dy[:rows]
-    for v in SENT:
-        out_ref[0, v] = base_ref[0, v]
+    for i in range(high - low):
+        v = low + i
+        dy = dot(w_ref[...], three_parts([q_ref[0, v]] + [piece[0, i] for piece in direct]))
+        out_ref[0, i] = nu_ref[v, 0:1] * dy[rows:] - near_v_ref[0, 0] * dy[:rows]
 
 
 def last_kernel(left_ref, *refs):
@@ -365,26 +372,27 @@
     )(block_owner, rows_live, held(part), in_hbm)
     second = flow_state[:, SECOND[0] : SECOND[1]]
     direct_second = across(second)
-    near_sent = lax.ppermute(
+    near = lax.ppermute(
         jnp.concatenate([flow_state[:, v : v + 1] for v in SENT], axis=1), "line", sibling
     )
 
     w_near = jax.ShapeDtypeStruct((2 * rows, 3 * rows), jnp.bfloat16)
     w_far = jax.ShapeDtypeStruct((2 * rows, 3 * len(shifts) * rows), jnp.bfloat16)
+    w_sibling = jax.ShapeDtypeStruct((2 * rows, 3 * (1 + len(shifts)) * rows), jnp.bfloat16)
     w_send = jax.ShapeDtypeStruct((len(shifts), 2 * rows, 6 * rows), jnp.bfloat16)
     nu = jax.ShapeDtypeStruct((nvar, 8, x_length), jnp.float32)
-    w_own, w_near, w_direct, w_passed, w_send, nu = pl.pallas_call(
+    w_own, w_near, w_direct, w_sibling, w_send, nu = pl.pallas_call(
         functools.partial(weights_kernel, lines),
         in_specs=[smem()] * 3 + [pl.BlockSpec(memory_space=pl.ANY)],
         out_specs=[kept()] * 6,
-        out_shape=[w_near, w_near, w_far, w_far, w_send, nu],
+        out_shape=[w_near, w_near, w_far, w_sibling, w_send, nu],
         scratch_shapes=[
             pltpu.VMEM((2, y_length, LANES), jnp.float32),
             pltpu.VMEM((2, LANES, y_length), jnp.float32),
-            pltpu.VMEM((len(shifts), 2, 2 * rows, LANES), jnp.float32),
+            pltpu.VMEM((len(shifts) + 1, 2, max(2, lines // 2) * rows, LANES), jnp.float32),
             pltpu.VMEM((lines, 2 * rows, rows), jnp.bfloat16),
             pltpu.VMEM((lines, 2 * rows, rows), jnp.bfloat16),
-            pltpu.SemaphoreType.DMA((2 + 4 * len(shifts),)),
+            pltpu.SemaphoreType.DMA((2 + 4 * len(shifts) + lines,)),
         ],
         compiler_params=limit,
         cost_estimate=small,
@@ -440,11 +448,11 @@
         there = lax.ppermute(held_faces, "blk", [(i, i ^ step) for i in range(slots)])
         if step == 1:
             there, w_own, own = lax.optimization_barrier((there, w_own, flow_state))
-            near_raw = lax.ppermute(own[:, RAW[0] : RAW[-1] + 1], "line", sibling)
+            near_v = lax.ppermute(own[:, 1:2], "line", sibling)
         elif step == 2:
             state = own_terms(w_own)
             w_send, *_ = lax.optimization_barrier((w_send, state, there))
-            results = send(*map(held, (w_send, nu, flow_state, near_sent, *far_v)))
+            results = send(*map(held, (w_send, nu, flow_state, near, *far_v)))
             direct_first, *_ = lax.optimization_barrier((direct_first, *results))
             direct_second, *_ = lax.optimization_barrier((direct_second, *results))
         arrived.append(there)
@@ -457,24 +465,27 @@
         for s, result in zip(shifts, results)
     ]
 
+    def sibling_terms(part, direct):
+        operands = [*map(held, (w_sibling, nu, flow_state, near_v, *direct))]
+        low, high = part
+        result = pl.pallas_call(
+            functools.partial(sibling_kernel, low, high),
+            in_specs=[kept()] * len(operands),
+            out_specs=kept(),
+            out_shape=jax.ShapeDtypeStruct((1, high - low, rows, x_length), jnp.float32),
+            compiler_params=limit,
+            cost_estimate=small,
+            name="sibling_terms",
+        )(*operands)
+        return [*direct, lax.ppermute(result, "line", sibling)]
+
     direct_second, *_ = lax.optimization_barrier((direct_second, *arrived))
-    passed_first = [lax.ppermute(piece, "line", sibling) for piece in direct_first]
-    passed_second = [lax.ppermute(piece, "line", sibling) for piece in direct_second]
-    pieces = [*direct_first, *passed_first, *direct_second, *passed_second]
-    state = pl.pallas_call(
-        functools.partial(raw_kernel, len(shifts)),
-        in_specs=[kept()] * (5 + len(pieces)),
-        out_specs=kept(),
-        out_shape=state_shape,
-        compiler_params=limit,
-        cost_estimate=small,
-        name="raw_terms",
-    )(*map(held, (w_direct, w_passed, nu, flow_state, state, *pieces)))
+    pieces = sibling_terms(FIRST, direct_first) + sibling_terms(SECOND, direct_second)
 
     anywhere = pl.BlockSpec(memory_space=pl.ANY)
     result, left = pl.pallas_call(
         functools.partial(near_kernel, len(arrived)),
-        in_specs=[smem()] * 4 + [kept()] * (7 + len(arrived)),
+        in_specs=[smem()] * 4 + [kept()] * (7 + len(arrived) + len(pieces)),
         out_specs=[anywhere, kept()],
         out_shape=[state_shape, sent],
         scratch_shapes=[
@@ -489,7 +500,7 @@
         link_block.T,
         link_side.T,
         rows_live,
-        *map(held, (ghost_operator, w_near, nu, flow_state, state, near_raw, near_sent, *arrived)),
+        *map(held, (ghost_operator, w_near, w_direct, nu, flow_state, state, near, *arrived, *pieces)),
     )
 
     operands = [*map(held, (left, *results))]

time: 33.9 us -> 34.5 us (1.018)
    ppermute x1, waiting for transfers between devices: 1.45 us -> 1.81 us  [on_device(): lax.ppermute(result, 'line', [(i, (i + s) % lines) for i in range(lines)])]
    pallas_call x2 -> x3, Pallas kernels: 1.64 us -> 1.63 us  [the longest x2 1.02 us: sibling_terms(): pl.pallas_call(functools.partial(sibling_kernel, low, high), in_specs=[ke...]
where the time goes in v4:
time: 34.5 us; the launch traced here: 34.3 us
  Pallas kernels  15.4 us (45%)
  starting transfers between devices  11.4 us (33%)
  waiting for transfers between devices  7.22 us (21%)
    ppermute x3, starting transfers between devices, on_device(): lax.ppermute(held_faces, 'blk', [(i, i ^ step) for i in range(slots)])  5.81 us
    pallas_call x1, Pallas kernels, own_terms(): pl.pallas_call(own_kernel, grid=(tiles,), in_specs=[smem()] * 3 + [pl.Blo...  5.02 us
    ppermute x3, waiting for transfers between devices, on_device(): lax.ppermute(held_faces, 'blk', [(i, i ^ step) for i in range(slots)])  3.88 us
    ppermute x2, starting transfers between devices, across(): lax.ppermute(array, 'line', [(i, (i + s) % lines) for i in range(lines)])  3.54 us
    pallas_call x1, Pallas kernels, on_device(): pl.pallas_call(functools.partial(weights_kernel, lines), in_specs=[smem()...  2.41 us
    pallas_call x1, Pallas kernels, on_device(): pl.pallas_call(functools.partial(near_kernel, len(arrived)), in_specs=[sm...  2.39 us
    pallas_call x1, Pallas kernels, on_device(): pl.pallas_call(faces_kernel, in_specs=[smem(), smem(), kept(), pl.BlockSp...  2.04 us
    ppermute x1, waiting for transfers between devices, on_device(): lax.ppermute(result, 'line', [(i, (i + s) % lines) for i in range(lines)])  1.81 us
  transfers between devices with their start and end apart: 10, of which 3 were waited for; matrix products, arithmetic and copies ran while one was open for 0% of the time, Pallas kernels for 39%

profile of v4, /device:TPU:0, one launch (start us, length us, event | category | flops | bytes accessed | tf_op | source)
XLA Modules:
  0.0 34.3 jit_solution(13871874025324131621)
XLA Ops:
  0.0 0.0 copy-start.2
  0.0 0.0 copy-start.1
  0.0 1.1 %part.1.part_ref = f32[1,2,128,512]{3,2,1,0:T(8,128)S(1)} custom-call(f32[1,5,128,512]{3,2,1,0:T(8,128)} %q_ref.3), custom_call_target="tpu_custom_call" | custom-call | flops 1 | bytes 1 | tf_op jit(solution)/shard_map/part/pallas_call | solution.py:350
  1.1 3.0 %collective-permute-start.4 = (f32[1,2,128,512]{3,2,1,0:T(8,128)S(1)}, f32[1,2,128,512]{3,2,1,0:T(8,128)S(1)}, u32[]{:S(2)}, u32[]{:S(2)}) collective-permute-start(f32[1,2,128,512]{3,2,1,0:T(8,128)S(1)} %part.1.part_ref), channel_id=1, source_target_pairs={{0,2},{1,3},{2,0},{3,1},{4,6},{5,7},{6,4},{7,5},{8,10},{9,11},{10,... | collective-permute-start | bytes 1572872 | tf_op jit(solution)/shard_map/ppermute | solution.py:347
  4.1 0.0 copy-done.2
  4.1 0.0 copy-done.1
  4.1 2.0 %faces.1 = (f32[1,5,128,512]{3,2,1,0:T(8,128)S(1)}, f32[1,2,16,128]{3,2,1,0:T(8,128)S(1)}) custom-call(s32[8]{0:T(128)S(1)} %copy-done.1, s32[8]{0:T(128)S(1)} %copy-done.2, f32[1,2,128,512]{3,2,1,0:T(8,128)S(1)} %part.1.part_ref, f32[1,5,128,512]{3,2,1,0:T(8,128)} %q_ref.3), custom_call_target="tpu_custom_call" | custom-call | flops 1 | bytes 1 | tf_op jit(solution)/shard_map/faces/pallas_call | solution.py:363
  6.2 0.0 copy-start.3
  6.2 0.1 fusion
  6.3 0.1 collective-permute-start.1
  6.3 1.6 %collective-permute-start = (f32[1,2,16,128]{3,2,1,0:T(8,128)S(1)}, f32[1,2,16,128]{3,2,1,0:T(8,128)S(1)}, u32[]{:S(2)}, u32[]{:S(2)}) collective-permute-start(f32[1,2,16,128]{3,2,1,0:T(8,128)S(1)} %get-tuple-element.26.refs_0_), channel_id=1, source_target_pairs={{0,4},{4,0},{8,12},{12,8},{16,20},{20,16},{24,28},{28,24},{1,5},{5... | collective-permute-start | bytes 49160 | tf_op jit(solution)/shard_map/ppermute | solution.py:448
  7.9 0.0 copy-done.3
  7.9 2.4 %weights.1 = (bf16[256,384]{1,0:T(8,128)(2,1)S(1)}, bf16[256,384]{1,0:T(8,128)(2,1)S(1)}, bf16[256,384]{1,0:T(8,128)(2,1)S(1)}, bf16[256,768]{1,0:T(8,128)(2,1)S...) custom-call(s32[8]{0:T(128)S(1)} %copy-done.1, s32[8]{0:T(128)S(1)} %copy-done.2, f32[7]{0:T(128)S(1)} %copy-done.3, ...), custom_call_target="tpu_custom_call" | custom-call | flops 1 | bytes 1 | tf_op jit(solution)/shard_map/weights/pallas_call | solution.py:384
  10.4 0.0 collective-permute-done.refs_1_
  10.4 0.2 collective-permute-start.5
  10.6 1.6 %collective-permute-start.2 = (f32[2,2,16,128]{3,2,1,0:T(8,128)S(1)}, f32[2,2,16,128]{3,2,1,0:T(8,128)S(1)}, u32[]{:S(2)}, u32[]{:S(2)}) collective-permute-start(f32[2,2,16,128]{3,2,1,0:T(8,128)S(1)} %pad_maximum_fusion.2), channel_id=1, source_target_pairs={{0,8},{4,12},{8,0},{12,4},{16,24},{20,28},{24,16},{28,20},{1,9},{5... | collective-permute-start | bytes 98312 | tf_op jit(solution)/shard_map/ppermute | solution.py:448
  12.2 0.5 %collective-permute-start.7 = (f32[1,1,128,512]{3,2,1,0:T(8,128)S(1)}, f32[1,1,128,512]{3,2,1,0:T(8,128)S(1)}, u32[]{:S(2)}, u32[]{:S(2)}) collective-permute-start(f32[1,1,128,512]{3,2,1,0:T(8,128)S(1)} %get-tuple-element.39), channel_id=1, source_target_pairs={{0,2},{1,3},{2,0},{3,1},{4,6},{5,7},{6,4},{7,5},{8,10},{9,11},{10,... | collective-permute-start | bytes 786440 | tf_op jit(solution)/shard_map/ppermute | solution.py:347
  12.7 5.0 %own_terms.1.base_ref = f32[1,5,128,512]{3,2,1,0:T(8,128)S(1)} custom-call(s32[8]{0:T(128)S(1)} %copy-done.1, s32[8]{0:T(128)S(1)} %copy-done.2, f32[7]{0:T(128)S(1)} %copy-done.3, bf16[256,384]{1,0:T(8,128)(2,1)S(1)} %get-tuple-element.28.wown_ref, f32[1,5,128,512]{3,2,1,0:T(8,128)S(1)} %get-tuple-element.34.q_ref.tile_ref, ...), custom_call_target="tpu_custom_call" | custom-call | flops 1 | bytes 1 | tf_op jit(solution)/shard_map/own_terms/pallas_call | solution.py:404
  17.8 0.0 collective-permute-done.2.refs_2_
  17.8 0.0 collective-permute-done.4.refs_1_.refs_0_.refs_4_
  17.8 0.0 collective-permute-done.1.refs_0_.near_ref
  17.8 0.6 %send_terms.1 = f32[1,2,128,512]{3,2,1,0:T(8,128)S(1)} custom-call(bf16[1,256,768]{2,1,0:T(8,128)(2,1)S(1)} %get-tuple-element.31.wsend_ref, f32[5,8,512]{2,1,0:T(8,128)S(1)} %get-tuple-element.24.nu_ref, f32[1,5,128,512]{3,2,1,0:T(8,128)S(1)} %get-tuple-element.34.q_ref.tile_ref, f32[1,2,128,512]{3,2,1,0:T(8,128)S(1)} %collective-permute-done.1.refs_0_.near_ref, ...), custom_call_target="tpu_custom_call" | custom-call | flops 1 | bytes 1 | tf_op jit(solution)/shard_map/send_terms/pallas_call | solution.py:455
  18.4 0.0 collective-permute-done.5.near_v_ref
  18.4 0.6 %sibling_terms.2 = f32[1,2,128,512]{3,2,1,0:T(8,128)S(1)} custom-call(bf16[256,768]{1,0:T(8,128)(2,1)S(1)} %get-tuple-element.33.w_ref, f32[5,8,512]{2,1,0:T(8,128)S(1)} %get-tuple-element.24.nu_ref, f32[1,5,128,512]{3,2,1,0:T(8,128)S(1)} %get-tuple-element.34.q_ref.tile_ref, f32[1,1,128,512]{3,2,1,0:T(8,128)S(1)} %collective-permute-done.5.near_v_ref, ...), custom_call_target="tpu_custom_call" | custom-call | flops 1 | bytes 1 | tf_op jit(solution)/shard_map/sibling_terms/pallas_call | solution.py:471
  19.1 0.1 collective-permute-start.6
  19.1 1.6 %collective-permute-start.9 = (f32[1,2,128,512]{3,2,1,0:T(8,128)S(1)}, f32[1,2,128,512]{3,2,1,0:T(8,128)S(1)}, u32[]{:S(2)}, u32[]{:S(2)}) collective-permute-start(f32[1,2,128,512]{3,2,1,0:T(8,128)S(1)} %send_terms.1), channel_id=1, source_target_pairs={{0,2},{1,3},{2,0},{3,1},{4,6},{5,7},{6,4},{7,5},{8,10},{9,11},{10,... | collective-permute-start | bytes 1572872 | tf_op jit(solution)/shard_map/ppermute | solution.py:464
  20.7 0.0 copy-start
  20.7 0.0 copy-start.4
  20.7 0.0 copy-start.5
  20.7 2.7 %collective-permute-start.3 = (f32[4,2,16,128]{3,2,1,0:T(8,128)S(1)}, f32[4,2,16,128]{3,2,1,0:T(8,128)S(1)}, u32[]{:S(2)}, u32[]{:S(2)}) collective-permute-start(f32[4,2,16,128]{3,2,1,0:T(8,128)S(1)} %pad_maximum_fusion.1), channel_id=1, source_target_pairs={{0,16},{4,20},{8,24},{12,28},{16,0},{20,4},{24,8},{28,12},{1,17},{... | collective-permute-start | bytes 196616 | tf_op jit(solution)/shard_map/ppermute | solution.py:448
  23.4 0.0 collective-permute-done.7.refs_0_.refs_6_
  23.4 3.9 %collective-permute-done.3.refs_3_ = f32[4,2,16,128]{3,2,1,0:T(8,128)S(1)} collective-permute-done((f32[4,2,16,128]{3,2,1,0:T(8,128)S(1)}, f32[4,2,16,128]{3,2,1,0:T(8,128)S(1)}, u32[]{:S(2)}, u32[]{:S(2)}) %collective-permute-start.3) | collective-permute-done | bytes 65568 | tf_op jit(solution)/shard_map/ppermute | solution.py:448
  27.3 0.4 %sibling_terms.3 = f32[1,1,128,512]{3,2,1,0:T(8,128)S(1)} custom-call(bf16[256,768]{1,0:T(8,128)(2,1)S(1)} %get-tuple-element.33.w_ref, f32[5,8,512]{2,1,0:T(8,128)S(1)} %get-tuple-element.24.nu_ref, f32[1,5,128,512]{3,2,1,0:T(8,128)S(1)} %get-tuple-element.34.q_ref.tile_ref, f32[1,1,128,512]{3,2,1,0:T(8,128)S(1)} %collective-permute-done.5.near_v_ref, ...), custom_call_target="tpu_custom_call" | custom-call | flops 1 | bytes 1 | tf_op jit(solution)/shard_map/sibling_terms/pallas_call | solution.py:471
  27.7 0.1 collective-permute-start.8
  27.7 1.5 %collective-permute-done.8.refs_7_ = f32[1,1,128,512]{3,2,1,0:T(8,128)S(1)} collective-permute-done((f32[1,1,128,512]{3,2,1,0:T(8,128)S(1)}, f32[1,1,128,512]{3,2,1,0:T(8,128)S(1)}, u32[]{:S(2)}, u32[]{:S(2)}) %collective-permute-start.8) | collective-permute-done | bytes 262176 | tf_op jit(solution)/shard_map/ppermute | solution.py:480
  29.3 0.0 collective-permute-done.6.refs_5_
  29.3 0.0 copy-done
  29.3 0.0 copy-done.4
  29.3 0.0 copy-done.5
  29.3 2.4 %near_terms.1 = (f32[1,5,128,512]{3,2,1,0:T(8,128)}, f32[1,2,128,512]{3,2,1,0:T(8,128)S(1)}) custom-call(s32[8]{0:T(128)S(1)} %copy-done.1, s32[2,8]{1,0:T(2,128)S(1)} %bitcast.2, s32[2,8]{1,0:T(2,128)S(1)} %bitcast.3, s32[8]{0:T(128)S(1)} %copy-done.2, f32[6,1024]{1,0:T(8,128)S(1)} %copy-done, bf16[256,384]{1,0:T(8,128)(2,1)S(1)} %get-tuple-element.22.wnear_ref, ...), custom_call_target="tpu_custom_call" | custom-call | flops 1 | bytes 1 | tf_op jit(solution)/shard_map/near_terms/pallas_call | solution.py:486
  31.7 1.8 %collective-permute-done.9.refs_0_ = f32[1,2,128,512]{3,2,1,0:T(8,128)S(1)} collective-permute-done((f32[1,2,128,512]{3,2,1,0:T(8,128)S(1)}, f32[1,2,128,512]{3,2,1,0:T(8,128)S(1)}, u32[]{:S(2)}, u32[]{:S(2)}) %collective-permute-start.9) | collective-permute-done | bytes 524320 | tf_op jit(solution)/shard_map/ppermute | solution.py:464
  33.5 0.8 %last_terms.1 = f32[1,5,128,512]{3,2,1,0:T(8,128)} custom-call(f32[1,2,128,512]{3,2,1,0:T(8,128)S(1)} %get-tuple-element.37.left_ref, f32[1,2,128,512]{3,2,1,0:T(8,128)S(1)} %collective-permute-done.9.refs_0_, f32[1,5,128,512]{3,2,1,0:T(8,128)} %get-tuple-element.38.refs_1_), custom_call_target="tpu_custom_call", output_to_operand_aliasing={{}: (2, {})} | custom-call | flops 1 | bytes 1 | tf_op jit(solution)/shard_map/last_terms/pallas_call | solution.py:507
  (4 shorter events, 0.1 us)
Async XLA Ops:
  0.0 4.1 %copy-start.2 = (s32[8]{0:T(128)S(1)}, s32[8]{0:T(128)}, u32[]{:S(2)}) copy-start(s32[8]{0:T(128)} %rows_ref.7) | copy-start | bytes 100
  0.0 4.1 %copy-start.1 = (s32[8]{0:T(128)S(1)}, s32[8]{0:T(128)}, u32[]{:S(2)}) copy-start(s32[8]{0:T(128)} %owner_ref.7) | copy-start | bytes 100
  1.1 16.7 %collective-permute-start.4 = (f32[1,2,128,512]{3,2,1,0:T(8,128)S(1)}, f32[1,2,128,512]{3,2,1,0:T(8,128)S(1)}, u32[]{:S(2)}, u32[]{:S(2)}) collective-permute-start(f32[1,2,128,512]{3,2,1,0:T(8,128)S(1)} %part.1.part_ref), channel_id=1, source_target_pairs={{0,2},{1,3},{2,0},{3,1},{4,6},{5,7},{6,4},{7,5},{8,10},{9,11},{10,... | collective-permute-start | bytes 1572872 | tf_op jit(solution)/shard_map/ppermute | solution.py:347
  6.2 1.8 %copy-start.3 = (f32[7]{0:T(128)S(1)}, f32[7]{0:T(128)}, u32[]{:S(2)}) copy-start(f32[7]{0:T(128)} %coef_ref.3) | copy-start | bytes 88
  6.3 11.5 %collective-permute-start.1 = (f32[1,2,128,512]{3,2,1,0:T(8,128)S(1)}, f32[1,2,128,512]{3,2,1,0:T(8,128)S(1)}, u32[]{:S(2)}, u32[]{:S(2)}) collective-permute-start(f32[1,2,128,512]{3,2,1,0:T(8,128)S(1)} %pad_maximum_fusion), channel_id=1, source_target_pairs={{0,1},{1,0},{2,3},{3,2},{4,5},{5,4},{6,7},{7,6},{8,9},{9,8},{10,11... | collective-permute-start | bytes 1572872 | tf_op jit(solution)/shard_map/ppermute | solution.py:375
  6.3 4.0 %collective-permute-start = (f32[1,2,16,128]{3,2,1,0:T(8,128)S(1)}, f32[1,2,16,128]{3,2,1,0:T(8,128)S(1)}, u32[]{:S(2)}, u32[]{:S(2)}) collective-permute-start(f32[1,2,16,128]{3,2,1,0:T(8,128)S(1)} %get-tuple-element.26.refs_0_), channel_id=1, source_target_pairs={{0,4},{4,0},{8,12},{12,8},{16,20},{20,16},{24,28},{28,24},{1,5},{5... | collective-permute-start | bytes 49160 | tf_op jit(solution)/shard_map/ppermute | solution.py:448
  10.4 8.0 %collective-permute-start.5 = (f32[1,1,128,512]{3,2,1,0:T(8,128)S(1)}, f32[1,1,128,512]{3,2,1,0:T(8,128)S(1)}, u32[]{:S(2)}, u32[]{:S(2)}) collective-permute-start(f32[1,1,128,512]{3,2,1,0:T(8,128)S(1)} %slice.14), channel_id=1, source_target_pairs={{0,1},{1,0},{2,3},{3,2},{4,5},{5,4},{6,7},{7,6},{8,9},{9,8},{10,11... | collective-permute-start | bytes 786440 | tf_op jit(solution)/shard_map/ppermute | solution.py:451
  10.6 7.1 %collective-permute-start.2 = (f32[2,2,16,128]{3,2,1,0:T(8,128)S(1)}, f32[2,2,16,128]{3,2,1,0:T(8,128)S(1)}, u32[]{:S(2)}, u32[]{:S(2)}) collective-permute-start(f32[2,2,16,128]{3,2,1,0:T(8,128)S(1)} %pad_maximum_fusion.2), channel_id=1, source_target_pairs={{0,8},{4,12},{8,0},{12,4},{16,24},{20,28},{24,16},{28,20},{1,9},{5... | collective-permute-start | bytes 98312 | tf_op jit(solution)/shard_map/ppermute | solution.py:448
  12.2 11.2 %collective-permute-start.7 = (f32[1,1,128,512]{3,2,1,0:T(8,128)S(1)}, f32[1,1,128,512]{3,2,1,0:T(8,128)S(1)}, u32[]{:S(2)}, u32[]{:S(2)}) collective-permute-start(f32[1,1,128,512]{3,2,1,0:T(8,128)S(1)} %get-tuple-element.39), channel_id=1, source_target_pairs={{0,2},{1,3},{2,0},{3,1},{4,6},{5,7},{6,4},{7,5},{8,10},{9,11},{10,... | collective-permute-start | bytes 786440 | tf_op jit(solution)/shard_map/ppermute | solution.py:347
  19.1 10.2 %collective-permute-start.6 = (f32[1,2,128,512]{3,2,1,0:T(8,128)S(1)}, f32[1,2,128,512]{3,2,1,0:T(8,128)S(1)}, u32[]{:S(2)}, u32[]{:S(2)}) collective-permute-start(f32[1,2,128,512]{3,2,1,0:T(8,128)S(1)} %sibling_terms.2), channel_id=1, source_target_pairs={{0,1},{1,0},{2,3},{3,2},{4,5},{5,4},{6,7},{7,6},{8,9},{9,8},{10,11... | collective-permute-start | bytes 1572872 | tf_op jit(solution)/shard_map/ppermute | solution.py:480
  19.1 14.3 %collective-permute-start.9 = (f32[1,2,128,512]{3,2,1,0:T(8,128)S(1)}, f32[1,2,128,512]{3,2,1,0:T(8,128)S(1)}, u32[]{:S(2)}, u32[]{:S(2)}) collective-permute-start(f32[1,2,128,512]{3,2,1,0:T(8,128)S(1)} %send_terms.1), channel_id=1, source_target_pairs={{0,2},{1,3},{2,0},{3,1},{4,6},{5,7},{6,4},{7,5},{8,10},{9,11},{10,... | collective-permute-start | bytes 1572872 | tf_op jit(solution)/shard_map/ppermute | solution.py:464
  20.7 8.6 %copy-start = (f32[6,1024]{1,0:T(8,128)S(1)}, f32[6,1024]{1,0:T(8,128)}, u32[]{:S(2)}) copy-start(f32[6,1024]{1,0:T(8,128)} %gop_ref.1) | copy-start | bytes 73732
  20.7 8.6 %copy-start.4 = (s32[8,2]{0,1:T(2,128)S(1)}, s32[8,2]{0,1:T(2,128)}, u32[]{:S(2)}) copy-start(s32[8,2]{0,1:T(2,128)} %param.11) | copy-start | bytes 196
  20.7 8.6 %copy-start.5 = (s32[8,2]{0,1:T(2,128)S(1)}, s32[8,2]{0,1:T(2,128)}, u32[]{:S(2)}) copy-start(s32[8,2]{0,1:T(2,128)} %param.12) | copy-start | bytes 196
  20.7 6.5 %collective-permute-start.3 = (f32[4,2,16,128]{3,2,1,0:T(8,128)S(1)}, f32[4,2,16,128]{3,2,1,0:T(8,128)S(1)}, u32[]{:S(2)}, u32[]{:S(2)}) collective-permute-start(f32[4,2,16,128]{3,2,1,0:T(8,128)S(1)} %pad_maximum_fusion.1), channel_id=1, source_target_pairs={{0,16},{4,20},{8,24},{12,28},{16,0},{20,4},{24,8},{28,12},{1,17},{... | collective-permute-start | bytes 196616 | tf_op jit(solution)/shard_map/ppermute | solution.py:448
  27.7 1.6 %collective-permute-start.8 = (f32[1,1,128,512]{3,2,1,0:T(8,128)S(1)}, f32[1,1,128,512]{3,2,1,0:T(8,128)S(1)}, u32[]{:S(2)}, u32[]{:S(2)}) collective-permute-start(f32[1,1,128,512]{3,2,1,0:T(8,128)S(1)} %sibling_terms.3), channel_id=1, source_target_pairs={{0,1},{1,0},{2,3},{3,2},{4,5},{5,4},{6,7},{7,6},{8,9},{9,8},{10,11... | collective-permute-start | bytes 786440 | tf_op jit(solution)/shard_map/ppermute | solution.py:480

commit v5 on v3

--- a/solution.py
+++ b/solution.py
@@ -207,7 +207,7 @@
     *refs,
 ):
     near_sent, refs = refs[0], refs[1:]
-    faces, (out_ref, left_ref, done_ref, sems) = refs[:face_count], refs[face_count:]
+    faces, (out_ref,) = refs[:face_count], refs[face_count:]
     near = {v: near_sent.at[0, i] for i, v in enumerate(SENT)}
     near.update({v: near_raw_ref.at[0, i] for i, v in enumerate(RAW)})
     nvar, rows, x_length = q_ref.shape[1:]
@@ -242,8 +242,7 @@
 
     operator = ghost_rows(gop_ref[...])
     pad = jnp.zeros((LANES - 6 * GHOST, rows), jnp.float32)
-    copies = []
-    for v in RAW + SENT:
+    for v in range(nvar):
         parts = []
         for m in range(2):
             part = planes[m][GHOST * v : GHOST * (v + 1)]
@@ -256,22 +255,12 @@
         dx = dot(ghost, operator)
         dy = dot(wnear_ref[...], three_parts([near[v][...]]))
         second = nu_ref[v, 0:1] * (dx[:, x_length:] + dy[rows:])
-        value = base_ref[0, v] + second - q_ref[0, 0] * dx[:, :x_length] - q_ref[0, 1] * dy[:rows]
-        if v in SENT:
-            left_ref[0, SENT.index(v)] = value
-            continue
-        i = RAW.index(v)
-        done_ref[i] = value
-        copies.append(pltpu.make_async_copy(done_ref.at[i], out_ref.at[0, v], sems.at[i]))
-        copies[-1].start()
-    for copy in copies:
-        copy.wait()
+        out_ref[0, v] = base_ref[0, v] + second - q_ref[0, 0] * dx[:, :x_length] - q_ref[0, 1] * dy[:rows]
 
 
 def send_kernel(wsend_ref, nu_ref, q_ref, *refs):
     count = wsend_ref.shape[0]
-    near, refs = refs[0], refs[1:]
-    far_v, out = refs[:count], refs[count:]
+    far_v, near, out = refs[:count], refs[count], refs[count + 1 :]
     rows = q_ref.shape[2]
     for j in range(count):
         for i, v in enumerate(SENT):
@@ -280,23 +269,28 @@
 
 
 def raw_kernel(count, wdirect_ref, wpassed_ref, nu_ref, q_ref, base_ref, *refs):
-    out_ref = refs[-1]
+    *refs, out_ref, done_ref, sems = refs
     rows = q_ref.shape[2]
-    first, second = [(refs[k : k + count], refs[k + count : k + 2 * count]) for k in (0, 2 * count)]
-    for (low, high), (direct, passed) in ((FIRST, first), (SECOND, second)):
+    copies = []
+    for low, high in (FIRST, SECOND):
+        direct, refs = refs[:count], refs[count:]
         for v in range(low, high):
+            i = v - RAW[0]
+            passed, refs = refs[:count], refs[count:]
             dy = dot(wdirect_ref[...], three_parts([piece[0, v - low] for piece in direct]))
-            dy = dy + dot(wpassed_ref[...], three_parts([piece[0, v - low] for piece in passed]))
-            out_ref[0, v] = base_ref[0, v] + nu_ref[v, 0:1] * dy[rows:] - q_ref[0, 1] * dy[:rows]
-    for v in SENT:
-        out_ref[0, v] = base_ref[0, v]
-
-
-def last_kernel(left_ref, *refs):
+            dy = dy + dot(wpassed_ref[...], three_parts([piece[0, 0] for piece in passed]))
+            done_ref[i] = base_ref[0, v] + nu_ref[v, 0:1] * dy[rows:] - q_ref[0, 1] * dy[:rows]
+            copies.append(pltpu.make_async_copy(done_ref.at[i], out_ref.at[0, v], sems.at[i]))
+            copies[-1].start()
+    for copy in copies:
+        copy.wait()
+
+
+def last_kernel(base_ref, *refs):
     results, (_, out_ref, done_ref, sems) = refs[:-4], refs[-4:]
     copies = []
     for i, v in enumerate(SENT):
-        done_ref[i] = left_ref[0, i] + sum(piece[0, i] for piece in results)
+        done_ref[i] = base_ref[0, v] + sum(piece[0, i] for piece in results)
         copies.append(pltpu.make_async_copy(done_ref.at[i], out_ref.at[0, v], sems.at[i]))
         copies[-1].start()
     for copy in copies:
@@ -442,11 +436,11 @@
             there, w_own, own = lax.optimization_barrier((there, w_own, flow_state))
             near_raw = lax.ppermute(own[:, RAW[0] : RAW[-1] + 1], "line", sibling)
         elif step == 2:
+            w_send, *_ = lax.optimization_barrier((w_send, there))
+            results = send(*map(held, (w_send, nu, flow_state, *far_v, near_sent)))
+            direct_first, *_ = lax.optimization_barrier((direct_first, *results))
+            w_own, *_ = lax.optimization_barrier((w_own, *results))
             state = own_terms(w_own)
-            w_send, *_ = lax.optimization_barrier((w_send, state, there))
-            results = send(*map(held, (w_send, nu, flow_state, near_sent, *far_v)))
-            direct_first, *_ = lax.optimization_barrier((direct_first, *results))
-            direct_second, *_ = lax.optimization_barrier((direct_second, *results))
         arrived.append(there)
         step *= 2
         if step < slots:
@@ -457,30 +451,20 @@
         for s, result in zip(shifts, results)
     ]
 
-    direct_second, *_ = lax.optimization_barrier((direct_second, *arrived))
-    passed_first = [lax.ppermute(piece, "line", sibling) for piece in direct_first]
+    passed_first = [
+        lax.ppermute(piece[:, i : i + 1], "line", sibling)
+        for i in range(FIRST[1] - FIRST[0])
+        for piece in direct_first
+    ]
+    direct_second, *_ = lax.optimization_barrier((direct_second, state, *arrived))
     passed_second = [lax.ppermute(piece, "line", sibling) for piece in direct_second]
     pieces = [*direct_first, *passed_first, *direct_second, *passed_second]
+
     state = pl.pallas_call(
-        functools.partial(raw_kernel, len(shifts)),
-        in_specs=[kept()] * (5 + len(pieces)),
+        functools.partial(near_kernel, len(arrived)),
+        in_specs=[smem()] * 4 + [kept()] * (7 + len(arrived)),
         out_specs=kept(),
         out_shape=state_shape,
-        compiler_params=limit,
-        cost_estimate=small,
-        name="raw_terms",
-    )(*map(held, (w_direct, w_passed, nu, flow_state, state, *pieces)))
-
-    anywhere = pl.BlockSpec(memory_space=pl.ANY)
-    result, left = pl.pallas_call(
-        functools.partial(near_kernel, len(arrived)),
-        in_specs=[smem()] * 4 + [kept()] * (7 + len(arrived)),
-        out_specs=[anywhere, kept()],
-        out_shape=[state_shape, sent],
-        scratch_shapes=[
-            pltpu.VMEM((len(RAW), rows, x_length), jnp.float32),
-            pltpu.SemaphoreType.DMA((len(RAW),)),
-        ],
         compiler_params=limit,
         cost_estimate=small,
         name="near_terms",
@@ -492,7 +476,22 @@
         *map(held, (ghost_operator, w_near, nu, flow_state, state, near_raw, near_sent, *arrived)),
     )
 
-    operands = [*map(held, (left, *results))]
+    anywhere = pl.BlockSpec(memory_space=pl.ANY)
+    result = pl.pallas_call(
+        functools.partial(raw_kernel, len(shifts)),
+        in_specs=[kept()] * (5 + len(pieces)),
+        out_specs=anywhere,
+        out_shape=state_shape,
+        scratch_shapes=[
+            pltpu.VMEM((len(RAW), rows, x_length), jnp.float32),
+            pltpu.SemaphoreType.DMA((len(RAW),)),
+        ],
+        compiler_params=limit,
+        cost_estimate=small,
+        name="raw_terms",
+    )(*map(held, (w_direct, w_passed, nu, flow_state, state, *pieces)))
+
+    operands = [*map(held, (state, *results))]
     return pl.pallas_call(
         last_kernel,
         in_specs=[kept()] * len(operands) + [anywhere],

time: 33.9 us -> 33.9 us (level)
  waiting for transfers between devices: 6.99 us -> 5.23 us
  starting transfers between devices: 11.2 us -> 12.4 us
  Pallas kernels: 15.1 us -> 15.7 us
    ppermute x2, waiting for transfers between devices: 0.01 us -> 2.49 us  [across(): lax.ppermute(array, 'line', [(i, (i + s) % lines) for i in range(lines)])]
    ppermute x3, waiting for transfers between devices: 4 us -> 1.82 us  [on_device(): lax.ppermute(held_faces, 'blk', [(i, i ^ step) for i in range(slots)])]
    ppermute x2 -> x1, waiting for transfers between devices: 1.54 us -> 0.01 us  [on_device(): lax.ppermute(piece, 'line', sibling)]
    pallas_call x1, Pallas kernels: 1.03 us -> 1.74 us  [on_device(): pl.pallas_call(functools.partial(raw_kernel, len(shifts)), in_specs=[kept...]
    ppermute x0 -> x2, starting transfers between devices: none -> 0.6 us  [on_device(): lax.ppermute(piece[:, i:i + 1], 'line', sibling)]
    ppermute x1, starting transfers between devices: 1.56 us -> 2.12 us  [on_device(): lax.ppermute(result, 'line', [(i, (i + s) % lines) for i in range(lines)])]
    ppermute x1, waiting for transfers between devices: 1.45 us -> 0.91 us  [on_device(): lax.ppermute(result, 'line', [(i, (i + s) % lines) for i in range(lines)])]
  transfers between devices with their start and end apart: 10 -> 11, of which waited for: 3 -> 3; matrix products, arithmetic and copies ran while one was open for 0% -> 1% of each run, Pallas kernels for 39% -> 41%
where the time goes in v5:
time: 33.9 us; the launch traced here: 33.7 us
  Pallas kernels  15.7 us (46%)
  starting transfers between devices  12.4 us (37%)
  waiting for transfers between devices  5.23 us (15%)
    ppermute x3, starting transfers between devices, on_device(): lax.ppermute(held_faces, 'blk', [(i, i ^ step) for i in range(slots)])  5.75 us
    pallas_call x1, Pallas kernels, own_terms(): pl.pallas_call(own_kernel, grid=(tiles,), in_specs=[smem()] * 3 + [pl.Blo...  5.02 us
    ppermute x2, starting transfers between devices, across(): lax.ppermute(array, 'line', [(i, (i + s) % lines) for i in range(lines)])  3.54 us
    ppermute x2, waiting for transfers between devices, across(): lax.ppermute(array, 'line', [(i, (i + s) % lines) for i in range(lines)])  2.49 us
    pallas_call x1, Pallas kernels, on_device(): pl.pallas_call(functools.partial(weights_kernel, lines), in_specs=[smem()...  2.19 us
    pallas_call x1, Pallas kernels, on_device(): pl.pallas_call(functools.partial(near_kernel, len(arrived)), in_specs=[sm...  2.14 us
    ppermute x1, starting transfers between devices, on_device(): lax.ppermute(result, 'line', [(i, (i + s) % lines) for i in range(lines)])  2.12 us
    pallas_call x1, Pallas kernels, on_device(): pl.pallas_call(faces_kernel, in_specs=[smem(), smem(), kept(), pl.BlockSp...  2.04 us
  transfers between devices with their start and end apart: 11, of which 3 were waited for; matrix products, arithmetic and copies ran while one was open for 1% of the time, Pallas kernels for 41%

profile of v5, /device:TPU:0, one launch (start us, length us, event | category | flops | bytes accessed | tf_op | source)
XLA Modules:
  0.0 33.7 jit_solution(9409146414527286405)
XLA Ops:
  0.0 0.0 copy-start.1
  0.0 0.0 copy-start.2
  0.0 1.1 %part.1.part_ref = f32[1,2,128,512]{3,2,1,0:T(8,128)S(1)} custom-call(f32[1,5,128,512]{3,2,1,0:T(8,128)} %q_ref.3), custom_call_target="tpu_custom_call" | custom-call | flops 1 | bytes 1 | tf_op jit(solution)/shard_map/part/pallas_call | solution.py:337
  1.1 3.0 %collective-permute-start.2 = (f32[1,2,128,512]{3,2,1,0:T(8,128)S(1)}, f32[1,2,128,512]{3,2,1,0:T(8,128)S(1)}, u32[]{:S(2)}, u32[]{:S(2)}) collective-permute-start(f32[1,2,128,512]{3,2,1,0:T(8,128)S(1)} %part.1.part_ref), channel_id=1, source_target_pairs={{0,2},{1,3},{2,0},{3,1},{4,6},{5,7},{6,4},{7,5},{8,10},{9,11},{10,... | collective-permute-start | bytes 1572872 | tf_op jit(solution)/shard_map/ppermute | solution.py:334
  4.1 0.0 copy-done.1
  4.1 0.0 copy-done.2
  4.1 2.0 %faces.1 = (f32[1,5,128,512]{3,2,1,0:T(8,128)S(1)}, f32[1,2,16,128]{3,2,1,0:T(8,128)S(1)}) custom-call(s32[8]{0:T(128)S(1)} %copy-done.1, s32[8]{0:T(128)S(1)} %copy-done.2, f32[1,2,128,512]{3,2,1,0:T(8,128)S(1)} %part.1.part_ref, f32[1,5,128,512]{3,2,1,0:T(8,128)} %q_ref.3), custom_call_target="tpu_custom_call" | custom-call | flops 1 | bytes 1 | tf_op jit(solution)/shard_map/faces/pallas_call | solution.py:350
  6.2 0.0 copy-start.3
  6.2 0.1 fusion
  6.3 0.1 collective-permute-start.3
  6.3 1.6 %collective-permute-start = (f32[1,2,16,128]{3,2,1,0:T(8,128)S(1)}, f32[1,2,16,128]{3,2,1,0:T(8,128)S(1)}, u32[]{:S(2)}, u32[]{:S(2)}) collective-permute-start(f32[1,2,16,128]{3,2,1,0:T(8,128)S(1)} %get-tuple-element.23.refs_1_), channel_id=1, source_target_pairs={{0,4},{4,0},{8,12},{12,8},{16,20},{20,16},{24,28},{28,24},{1,5},{5... | collective-permute-start | bytes 49160 | tf_op jit(solution)/shard_map/ppermute | solution.py:434
  7.9 0.0 copy-done.3
  7.9 2.2 %weights.1 = (bf16[256,384]{1,0:T(8,128)(2,1)S(1)}, bf16[256,384]{1,0:T(8,128)(2,1)S(1)}, bf16[256,384]{1,0:T(8,128)(2,1)S(1)}, bf16[256,384]{1,0:T(8,128)(2,1)S...) custom-call(s32[8]{0:T(128)S(1)} %copy-done.1, s32[8]{0:T(128)S(1)} %copy-done.2, f32[7]{0:T(128)S(1)} %copy-done.3, ...), custom_call_target="tpu_custom_call" | custom-call | flops 1 | bytes 1 | tf_op jit(solution)/shard_map/weights/pallas_call | solution.py:370
  10.1 0.0 collective-permute-done.refs_2_
  10.2 0.1 slice.20
  10.2 0.2 collective-permute-start.4
  10.4 1.6 %collective-permute-start.1 = (f32[2,2,16,128]{3,2,1,0:T(8,128)S(1)}, f32[2,2,16,128]{3,2,1,0:T(8,128)S(1)}, u32[]{:S(2)}, u32[]{:S(2)}) collective-permute-start(f32[2,2,16,128]{3,2,1,0:T(8,128)S(1)} %pad_maximum_fusion.2), channel_id=1, source_target_pairs={{0,8},{4,12},{8,0},{12,4},{16,24},{20,28},{24,16},{28,20},{1,9},{5... | collective-permute-start | bytes 98312 | tf_op jit(solution)/shard_map/ppermute | solution.py:434
  12.0 0.5 %collective-permute-start.9 = (f32[1,1,128,512]{3,2,1,0:T(8,128)S(1)}, f32[1,1,128,512]{3,2,1,0:T(8,128)S(1)}, u32[]{:S(2)}, u32[]{:S(2)}) collective-permute-start(f32[1,1,128,512]{3,2,1,0:T(8,128)S(1)} %get-tuple-element.35), channel_id=1, source_target_pairs={{0,2},{1,3},{2,0},{3,1},{4,6},{5,7},{6,4},{7,5},{8,10},{9,11},{10,... | collective-permute-start | bytes 786440 | tf_op jit(solution)/shard_map/ppermute | solution.py:334
  12.6 1.8 %collective-permute-done.1.refs_3_ = f32[2,2,16,128]{3,2,1,0:T(8,128)S(1)} collective-permute-done((f32[2,2,16,128]{3,2,1,0:T(8,128)S(1)}, f32[2,2,16,128]{3,2,1,0:T(8,128)S(1)}, u32[]{:S(2)}, u32[]{:S(2)}) %collective-permute-start.1) | collective-permute-done | bytes 32800 | tf_op jit(solution)/shard_map/ppermute | solution.py:434
  14.4 2.5 %collective-permute-done.2.refs_0_ = f32[1,2,128,512]{3,2,1,0:T(8,128)S(1)} collective-permute-done((f32[1,2,128,512]{3,2,1,0:T(8,128)S(1)}, f32[1,2,128,512]{3,2,1,0:T(8,128)S(1)}, u32[]{:S(2)}, u32[]{:S(2)}) %collective-permute-start.2) | collective-permute-done | bytes 524320 | tf_op jit(solution)/shard_map/ppermute | solution.py:334
  16.8 0.0 collective-permute-done.3.refs_1_.refs_0_
  16.8 0.6 %send_terms.1 = f32[1,2,128,512]{3,2,1,0:T(8,128)S(1)} custom-call(bf16[1,256,768]{2,1,0:T(8,128)(2,1)S(1)} %get-tuple-element.28.wsend_ref, f32[5,8,512]{2,1,0:T(8,128)S(1)} %get-tuple-element.21.nu_ref, f32[1,5,128,512]{3,2,1,0:T(8,128)S(1)} %get-tuple-element.30.q_ref.tile_ref, f32[1,2,128,512]{3,2,1,0:T(8,128)S(1)} %collective-permute-done.2.refs_0_, ...), custom_call_target="tpu_custom_call" | custom-call | flops 1 | bytes 1 | tf_op jit(solution)/shard_map/send_terms/pallas_call | solution.py:440
  17.5 2.1 %collective-permute-start.6 = (f32[1,2,128,512]{3,2,1,0:T(8,128)S(1)}, f32[1,2,128,512]{3,2,1,0:T(8,128)S(1)}, u32[]{:S(2)}, u32[]{:S(2)}) collective-permute-start(f32[1,2,128,512]{3,2,1,0:T(8,128)S(1)} %send_terms.1), channel_id=1, source_target_pairs={{0,2},{1,3},{2,0},{3,1},{4,6},{5,7},{6,4},{7,5},{8,10},{9,11},{10,... | collective-permute-start | bytes 1572872 | tf_op jit(solution)/shard_map/ppermute | solution.py:450
  19.6 2.6 %collective-permute-start.5 = (f32[4,2,16,128]{3,2,1,0:T(8,128)S(1)}, f32[4,2,16,128]{3,2,1,0:T(8,128)S(1)}, u32[]{:S(2)}, u32[]{:S(2)}) collective-permute-start(f32[4,2,16,128]{3,2,1,0:T(8,128)S(1)} %pad_maximum_fusion.1), channel_id=1, source_target_pairs={{0,16},{4,20},{8,24},{12,28},{16,0},{20,4},{24,8},{28,12},{1,17},{... | collective-permute-start | bytes 196616 | tf_op jit(solution)/shard_map/ppermute | solution.py:434
  22.2 0.0 copy-start
  22.3 0.0 copy-start.4
  22.3 0.0 copy-start.5
  22.3 0.1 collective-permute-start.7
  22.4 5.0 %own_terms.1.base_ref = f32[1,5,128,512]{3,2,1,0:T(8,128)S(1)} custom-call(s32[8]{0:T(128)S(1)} %copy-done.1, s32[8]{0:T(128)S(1)} %copy-done.2, f32[7]{0:T(128)S(1)} %copy-done.3, bf16[256,384]{1,0:T(8,128)(2,1)S(1)} %get-tuple-element.29.wown_ref, f32[1,5,128,512]{3,2,1,0:T(8,128)S(1)} %get-tuple-element.30.q_ref.tile_ref, ...), custom_call_target="tpu_custom_call" | custom-call | flops 1 | bytes 1 | tf_op jit(solution)/shard_map/own_terms/pallas_call | solution.py:390
  27.4 0.0 collective-permute-done.5.refs_4_
  27.4 0.5 %collective-permute-start.8 = (f32[1,1,128,512]{3,2,1,0:T(8,128)S(1)}, f32[1,1,128,512]{3,2,1,0:T(8,128)S(1)}, u32[]{:S(2)}, u32[]{:S(2)}) collective-permute-start(f32[1,1,128,512]{3,2,1,0:T(8,128)S(1)} %get-tuple-element.38), channel_id=1, source_target_pairs={{0,1},{1,0},{2,3},{3,2},{4,5},{5,4},{6,7},{7,6},{8,9},{9,8},{10,11... | collective-permute-start | bytes 786440 | tf_op jit(solution)/shard_map/ppermute | solution.py:455
  27.9 0.0 collective-permute-done.9.refs_3_
  27.9 0.1 collective-permute-start.10
  28.0 0.0 collective-permute-done.4.near_raw_ref
  28.0 0.0 copy-done
  28.0 0.0 copy-done.4
  28.0 0.0 copy-done.5
  28.0 2.1 %near_terms.1.base_ref = f32[1,5,128,512]{3,2,1,0:T(8,128)S(1)} custom-call(s32[8]{0:T(128)S(1)} %copy-done.1, s32[2,8]{1,0:T(2,128)S(1)} %bitcast.2, s32[2,8]{1,0:T(2,128)S(1)} %bitcast.3, s32[8]{0:T(128)S(1)} %copy-done.2, f32[6,1024]{1,0:T(8,128)S(1)} %copy-done, bf16[256,384]{1,0:T(8,128)(2,1)S(1)} %get-tuple-element.20.wnear_ref, ...), custom_call_target="tpu_custom_call" | custom-call | flops 1 | bytes 1 | tf_op jit(solution)/shard_map/near_terms/pallas_call | solution.py:463
  30.2 0.0 collective-permute-done.7.refs_1_
  30.2 0.0 collective-permute-done.8.refs_2_
  30.2 0.0 collective-permute-done.10.refs_4_
  30.2 1.7 %raw_terms.1.refs_1_ = f32[1,5,128,512]{3,2,1,0:T(8,128)} custom-call(bf16[256,384]{1,0:T(8,128)(2,1)S(1)} %get-tuple-element.31.wdirect_ref, bf16[256,384]{1,0:T(8,128)(2,1)S(1)} %get-tuple-element.32.wpassed_ref, f32[5,8,512]{2,1,0:T(8,128)S(1)} %get-tuple-element.21.nu_ref, f32[1,5,128,512]{3,2,1,0:T(8,128)S(1)} %get-tuple-element.30.q_ref.tile_ref, ...), custom_call_target="tpu_custom_call" | custom-call | flops 1 | bytes 1 | tf_op jit(solution)/shard_map/raw_terms/pallas_call | solution.py:480
  32.0 0.9 %collective-permute-done.6.refs_0_ = f32[1,2,128,512]{3,2,1,0:T(8,128)S(1)} collective-permute-done((f32[1,2,128,512]{3,2,1,0:T(8,128)S(1)}, f32[1,2,128,512]{3,2,1,0:T(8,128)S(1)}, u32[]{:S(2)}, u32[]{:S(2)}) %collective-permute-start.6) | collective-permute-done | bytes 524320 | tf_op jit(solution)/shard_map/ppermute | solution.py:450
  32.9 0.8 %last_terms.1 = f32[1,5,128,512]{3,2,1,0:T(8,128)} custom-call(f32[1,5,128,512]{3,2,1,0:T(8,128)S(1)} %near_terms.1.base_ref, f32[1,2,128,512]{3,2,1,0:T(8,128)S(1)} %collective-permute-done.6.refs_0_, f32[1,5,128,512]{3,2,1,0:T(8,128)} %raw_terms.1.refs_1_), custom_call_target="tpu_custom_call", output_to_operand_aliasing={{}: (2, {})} | custom-call | flops 1 | bytes 1 | tf_op jit(solution)/shard_map/last_terms/pallas_call | solution.py:495
  (4 shorter events, 0.1 us)
Async XLA Ops:
  0.0 4.1 %copy-start.1 = (s32[8]{0:T(128)S(1)}, s32[8]{0:T(128)}, u32[]{:S(2)}) copy-start(s32[8]{0:T(128)} %owner_ref.7) | copy-start | bytes 100
  0.0 4.1 %copy-start.2 = (s32[8]{0:T(128)S(1)}, s32[8]{0:T(128)}, u32[]{:S(2)}) copy-start(s32[8]{0:T(128)} %rows_ref.7) | copy-start | bytes 100
  1.1 15.8 %collective-permute-start.2 = (f32[1,2,128,512]{3,2,1,0:T(8,128)S(1)}, f32[1,2,128,512]{3,2,1,0:T(8,128)S(1)}, u32[]{:S(2)}, u32[]{:S(2)}) collective-permute-start(f32[1,2,128,512]{3,2,1,0:T(8,128)S(1)} %part.1.part_ref), channel_id=1, source_target_pairs={{0,2},{1,3},{2,0},{3,1},{4,6},{5,7},{6,4},{7,5},{8,10},{9,11},{10,... | collective-permute-start | bytes 1572872 | tf_op jit(solution)/shard_map/ppermute | solution.py:334
  6.2 1.8 %copy-start.3 = (f32[7]{0:T(128)S(1)}, f32[7]{0:T(128)}, u32[]{:S(2)}) copy-start(f32[7]{0:T(128)} %coef_ref.3) | copy-start | bytes 88
  6.3 10.6 %collective-permute-start.3 = (f32[1,2,128,512]{3,2,1,0:T(8,128)S(1)}, f32[1,2,128,512]{3,2,1,0:T(8,128)S(1)}, u32[]{:S(2)}, u32[]{:S(2)}) collective-permute-start(f32[1,2,128,512]{3,2,1,0:T(8,128)S(1)} %pad_maximum_fusion), channel_id=1, source_target_pairs={{0,1},{1,0},{2,3},{3,2},{4,5},{5,4},{6,7},{7,6},{8,9},{9,8},{10,11... | collective-permute-start | bytes 1572872 | tf_op jit(solution)/shard_map/ppermute | solution.py:362
  6.3 3.8 %collective-permute-start = (f32[1,2,16,128]{3,2,1,0:T(8,128)S(1)}, f32[1,2,16,128]{3,2,1,0:T(8,128)S(1)}, u32[]{:S(2)}, u32[]{:S(2)}) collective-permute-start(f32[1,2,16,128]{3,2,1,0:T(8,128)S(1)} %get-tuple-element.23.refs_1_), channel_id=1, source_target_pairs={{0,4},{4,0},{8,12},{12,8},{16,20},{20,16},{24,28},{28,24},{1,5},{5... | collective-permute-start | bytes 49160 | tf_op jit(solution)/shard_map/ppermute | solution.py:434
  10.2 17.8 %collective-permute-start.4 = (f32[1,3,128,512]{3,2,1,0:T(8,128)S(1)}, f32[1,3,128,512]{3,2,1,0:T(8,128)S(1)}, u32[]{:S(2)}, u32[]{:S(2)}) collective-permute-start(f32[1,3,128,512]{3,2,1,0:T(8,128)S(1)} %slice.20), channel_id=1, source_target_pairs={{0,1},{1,0},{2,3},{3,2},{4,5},{5,4},{6,7},{7,6},{8,9},{9,8},{10,11... | collective-permute-start | bytes 2359304 | tf_op jit(solution)/shard_map/ppermute | solution.py:437
  10.4 3.9 %collective-permute-start.1 = (f32[2,2,16,128]{3,2,1,0:T(8,128)S(1)}, f32[2,2,16,128]{3,2,1,0:T(8,128)S(1)}, u32[]{:S(2)}, u32[]{:S(2)}) collective-permute-start(f32[2,2,16,128]{3,2,1,0:T(8,128)S(1)} %pad_maximum_fusion.2), channel_id=1, source_target_pairs={{0,8},{4,12},{8,0},{12,4},{16,24},{20,28},{24,16},{28,20},{1,9},{5... | collective-permute-start | bytes 98312 | tf_op jit(solution)/shard_map/ppermute | solution.py:434
  12.0 15.9 %collective-permute-start.9 = (f32[1,1,128,512]{3,2,1,0:T(8,128)S(1)}, f32[1,1,128,512]{3,2,1,0:T(8,128)S(1)}, u32[]{:S(2)}, u32[]{:S(2)}) collective-permute-start(f32[1,1,128,512]{3,2,1,0:T(8,128)S(1)} %get-tuple-element.35), channel_id=1, source_target_pairs={{0,2},{1,3},{2,0},{3,1},{4,6},{5,7},{6,4},{7,5},{8,10},{9,11},{10,... | collective-permute-start | bytes 786440 | tf_op jit(solution)/shard_map/ppermute | solution.py:334
  17.5 15.4 %collective-permute-start.6 = (f32[1,2,128,512]{3,2,1,0:T(8,128)S(1)}, f32[1,2,128,512]{3,2,1,0:T(8,128)S(1)}, u32[]{:S(2)}, u32[]{:S(2)}) collective-permute-start(f32[1,2,128,512]{3,2,1,0:T(8,128)S(1)} %send_terms.1), channel_id=1, source_target_pairs={{0,2},{1,3},{2,0},{3,1},{4,6},{5,7},{6,4},{7,5},{8,10},{9,11},{10,... | collective-permute-start | bytes 1572872 | tf_op jit(solution)/shard_map/ppermute | solution.py:450
  19.6 7.8 %collective-permute-start.5 = (f32[4,2,16,128]{3,2,1,0:T(8,128)S(1)}, f32[4,2,16,128]{3,2,1,0:T(8,128)S(1)}, u32[]{:S(2)}, u32[]{:S(2)}) collective-permute-start(f32[4,2,16,128]{3,2,1,0:T(8,128)S(1)} %pad_maximum_fusion.1), channel_id=1, source_target_pairs={{0,16},{4,20},{8,24},{12,28},{16,0},{20,4},{24,8},{28,12},{1,17},{... | collective-permute-start | bytes 196616 | tf_op jit(solution)/shard_map/ppermute | solution.py:434
  22.2 5.8 %copy-start = (f32[6,1024]{1,0:T(8,128)S(1)}, f32[6,1024]{1,0:T(8,128)}, u32[]{:S(2)}) copy-start(f32[6,1024]{1,0:T(8,128)} %gop_ref.1) | copy-start | bytes 73732
  22.3 5.8 %copy-start.4 = (s32[8,2]{0,1:T(2,128)S(1)}, s32[8,2]{0,1:T(2,128)}, u32[]{:S(2)}) copy-start(s32[8,2]{0,1:T(2,128)} %param.11) | copy-start | bytes 196
  22.3 5.8 %copy-start.5 = (s32[8,2]{0,1:T(2,128)S(1)}, s32[8,2]{0,1:T(2,128)}, u32[]{:S(2)}) copy-start(s32[8,2]{0,1:T(2,128)} %param.12) | copy-start | bytes 196
  22.3 7.9 %collective-permute-start.7 = (f32[1,1,128,512]{3,2,1,0:T(8,128)S(1)}, f32[1,1,128,512]{3,2,1,0:T(8,128)S(1)}, u32[]{:S(2)}, u32[]{:S(2)}) collective-permute-start(f32[1,1,128,512]{3,2,1,0:T(8,128)S(1)} %get-tuple-element.39), channel_id=1, source_target_pairs={{0,1},{1,0},{2,3},{3,2},{4,5},{5,4},{6,7},{7,6},{8,9},{9,8},{10,11... | collective-permute-start | bytes 786440 | tf_op jit(solution)/shard_map/ppermute | solution.py:455
  27.4 2.8 %collective-permute-start.8 = (f32[1,1,128,512]{3,2,1,0:T(8,128)S(1)}, f32[1,1,128,512]{3,2,1,0:T(8,128)S(1)}, u32[]{:S(2)}, u32[]{:S(2)}) collective-permute-start(f32[1,1,128,512]{3,2,1,0:T(8,128)S(1)} %get-tuple-element.38), channel_id=1, source_target_pairs={{0,1},{1,0},{2,3},{3,2},{4,5},{5,4},{6,7},{7,6},{8,9},{9,8},{10,11... | collective-permute-start | bytes 786440 | tf_op jit(solution)/shard_map/ppermute | solution.py:455
  27.9 2.3 %collective-permute-start.10 = (f32[1,1,128,512]{3,2,1,0:T(8,128)S(1)}, f32[1,1,128,512]{3,2,1,0:T(8,128)S(1)}, u32[]{:S(2)}, u32[]{:S(2)}) collective-permute-start(f32[1,1,128,512]{3,2,1,0:T(8,128)S(1)} %collective-permute-done.9.refs_3_), channel_id=1, source_target_pairs={{0,1},{1,0},{2,3},{3,2},{4,5},{5,4},{6,7},{7,6},{8,9},{9,8},{10,11... | collective-permute-start | bytes 786440 | tf_op jit(solution)/shard_map/ppermute | solution.py:460

commit v6 on v4

--- a/solution.py
+++ b/solution.py
@@ -212,11 +212,13 @@
 ):
     faces, refs = refs[:face_count], refs[face_count:]
     *refs, out_ref, left_ref, done_ref, sems = refs
-    count = len(refs) // 2 - 1
+    count = (len(refs) - len(RAW)) // 2
     raw = {}
-    for (low, high), parts in ((FIRST, refs[: count + 1]), (SECOND, refs[count + 1 :])):
+    for low, high in (FIRST, SECOND):
+        direct, refs = refs[:count], refs[count:]
         for v in range(low, high):
-            raw[v] = [ref.at[0, v - low] for ref in parts]
+            raw[v] = [ref.at[0, v - low] for ref in direct] + [refs[v - low].at[0, 0]]
+        refs = refs[high - low :]
     nvar, rows, x_length = q_ref.shape[1:]
     my_slot = lax.axis_index("blk")
     my_block = find_block(owner_ref, my_slot)
@@ -281,8 +283,7 @@
 
 def send_kernel(wsend_ref, nu_ref, q_ref, *refs):
     count = wsend_ref.shape[0]
-    near, refs = refs[0], refs[1:]
-    far_v, out = refs[:count], refs[count:]
+    far_v, near, out = refs[:count], refs[count], refs[count + 1 :]
     rows = q_ref.shape[2]
     for j in range(count):
         for i, v in enumerate(SENT):
@@ -291,12 +292,12 @@
 
 
 def sibling_kernel(low, high, w_ref, nu_ref, q_ref, near_v_ref, *refs):
-    direct, out_ref = refs[:-1], refs[-1]
+    direct, out = refs[: low - high], refs[low - high :]
     rows = q_ref.shape[2]
     for i in range(high - low):
         v = low + i
         dy = dot(w_ref[...], three_parts([q_ref[0, v]] + [piece[0, i] for piece in direct]))
-        out_ref[0, i] = nu_ref[v, 0:1] * dy[rows:] - near_v_ref[0, 0] * dy[:rows]
+        out[i][0, 0] = nu_ref[v, 0:1] * dy[rows:] - near_v_ref[0, 0] * dy[:rows]
 
 
 def last_kernel(left_ref, *refs):
@@ -452,7 +453,7 @@
         elif step == 2:
             state = own_terms(w_own)
             w_send, *_ = lax.optimization_barrier((w_send, state, there))
-            results = send(*map(held, (w_send, nu, flow_state, near, *far_v)))
+            results = send(*map(held, (w_send, nu, flow_state, *far_v, near)))
             direct_first, *_ = lax.optimization_barrier((direct_first, *results))
             direct_second, *_ = lax.optimization_barrier((direct_second, *results))
         arrived.append(there)
@@ -468,16 +469,16 @@
     def sibling_terms(part, direct):
         operands = [*map(held, (w_sibling, nu, flow_state, near_v, *direct))]
         low, high = part
-        result = pl.pallas_call(
+        results = pl.pallas_call(
             functools.partial(sibling_kernel, low, high),
             in_specs=[kept()] * len(operands),
-            out_specs=kept(),
-            out_shape=jax.ShapeDtypeStruct((1, high - low, rows, x_length), jnp.float32),
+            out_specs=[kept()] * (high - low),
+            out_shape=[jax.ShapeDtypeStruct((1, 1, rows, x_length), jnp.float32)] * (high - low),
             compiler_params=limit,
             cost_estimate=small,
             name="sibling_terms",
         )(*operands)
-        return [*direct, lax.ppermute(result, "line", sibling)]
+        return [*direct, *(lax.ppermute(result, "line", sibling) for result in results)]
 
     direct_second, *_ = lax.optimization_barrier((direct_second, *arrived))
     pieces = sibling_terms(FIRST, direct_first) + sibling_terms(SECOND, direct_second)

time: 34.5 us -> 33.9 us (0.983)
  waiting for transfers between devices: 7.22 us -> 6.28 us
    ppermute x3, waiting for transfers between devices: 3.88 us -> 2.79 us  [on_device(): lax.ppermute(held_faces, 'blk', [(i, i ^ step) for i in range(slots)])]
    ppermute x2 -> x3, starting transfers between devices: 0.14 us -> 0.58 us  [sibling_terms(): lax.ppermute(result, 'line', sibling)]
    ppermute x2 -> x3, waiting for transfers between devices: 1.52 us -> 1.52 us  [sibling_terms(): lax.ppermute(result, 'line', sibling)]
  transfers between devices with their start and end apart: 10 -> 11, of which waited for: 3 -> 5; matrix products, arithmetic and copies ran while one was open for 0% -> 0% of each run, Pallas kernels for 39% -> 40%
where the time goes in v6:
time: 33.9 us; the launch traced here: 33.7 us
  Pallas kernels  15.4 us (45%)
  starting transfers between devices  11.7 us (35%)
  waiting for transfers between devices  6.28 us (19%)
    ppermute x3, starting transfers between devices, on_device(): lax.ppermute(held_faces, 'blk', [(i, i ^ step) for i in range(slots)])  5.82 us
    pallas_call x1, Pallas kernels, own_terms(): pl.pallas_call(own_kernel, grid=(tiles,), in_specs=[smem()] * 3 + [pl.Blo...  5.02 us
    ppermute x2, starting transfers between devices, across(): lax.ppermute(array, 'line', [(i, (i + s) % lines) for i in range(lines)])  3.6 us
    ppermute x3, waiting for transfers between devices, on_device(): lax.ppermute(held_faces, 'blk', [(i, i ^ step) for i in range(slots)])  2.79 us
    pallas_call x1, Pallas kernels, on_device(): pl.pallas_call(functools.partial(weights_kernel, lines), in_specs=[smem()...  2.41 us
    pallas_call x1, Pallas kernels, on_device(): pl.pallas_call(functools.partial(near_kernel, len(arrived)), in_specs=[sm...  2.36 us
    pallas_call x1, Pallas kernels, on_device(): pl.pallas_call(faces_kernel, in_specs=[smem(), smem(), kept(), pl.BlockSp...  2.04 us
    ppermute x1, waiting for transfers between devices, on_device(): lax.ppermute(result, 'line', [(i, (i + s) % lines) for i in range(lines)])  1.96 us
  transfers between devices with their start and end apart: 11, of which 5 were waited for; matrix products, arithmetic and copies ran while one was open for 0% of the time, Pallas kernels for 40%

profile of v6, /device:TPU:0, one launch (start us, length us, event | category | flops | bytes accessed | tf_op | source)
XLA Modules:
  0.0 33.7 jit_solution(7103750374012860233)
XLA Ops:
  0.0 0.0 copy-start.2
  0.0 0.0 copy-start.1
  0.0 1.1 %part.1.part_ref = f32[1,2,128,512]{3,2,1,0:T(8,128)S(1)} custom-call(f32[1,5,128,512]{3,2,1,0:T(8,128)} %q_ref.3), custom_call_target="tpu_custom_call" | custom-call | flops 1 | bytes 1 | tf_op jit(solution)/shard_map/part/pallas_call | solution.py:351
  1.1 3.0 %collective-permute-start.4 = (f32[1,2,128,512]{3,2,1,0:T(8,128)S(1)}, f32[1,2,128,512]{3,2,1,0:T(8,128)S(1)}, u32[]{:S(2)}, u32[]{:S(2)}) collective-permute-start(f32[1,2,128,512]{3,2,1,0:T(8,128)S(1)} %part.1.part_ref), channel_id=1, source_target_pairs={{0,2},{1,3},{2,0},{3,1},{4,6},{5,7},{6,4},{7,5},{8,10},{9,11},{10,... | collective-permute-start | bytes 1572872 | tf_op jit(solution)/shard_map/ppermute | solution.py:348
  4.1 0.0 copy-done.2
  4.1 0.0 copy-done.1
  4.1 2.0 %faces.1 = (f32[1,5,128,512]{3,2,1,0:T(8,128)S(1)}, f32[1,2,16,128]{3,2,1,0:T(8,128)S(1)}) custom-call(s32[8]{0:T(128)S(1)} %copy-done.1, s32[8]{0:T(128)S(1)} %copy-done.2, f32[1,2,128,512]{3,2,1,0:T(8,128)S(1)} %part.1.part_ref, f32[1,5,128,512]{3,2,1,0:T(8,128)} %q_ref.3), custom_call_target="tpu_custom_call" | custom-call | flops 1 | bytes 1 | tf_op jit(solution)/shard_map/faces/pallas_call | solution.py:364
  6.2 0.0 copy-start.3
  6.2 0.1 fusion
  6.3 0.1 collective-permute-start.1
  6.3 1.6 %collective-permute-start = (f32[1,2,16,128]{3,2,1,0:T(8,128)S(1)}, f32[1,2,16,128]{3,2,1,0:T(8,128)S(1)}, u32[]{:S(2)}, u32[]{:S(2)}) collective-permute-start(f32[1,2,16,128]{3,2,1,0:T(8,128)S(1)} %get-tuple-element.28.refs_0_), channel_id=1, source_target_pairs={{0,4},{4,0},{8,12},{12,8},{16,20},{20,16},{24,28},{28,24},{1,5},{5... | collective-permute-start | bytes 49160 | tf_op jit(solution)/shard_map/ppermute | solution.py:449
  7.9 0.0 copy-done.3
  7.9 2.4 %weights.1 = (bf16[256,384]{1,0:T(8,128)(2,1)S(1)}, bf16[256,384]{1,0:T(8,128)(2,1)S(1)}, bf16[256,384]{1,0:T(8,128)(2,1)S(1)}, bf16[256,768]{1,0:T(8,128)(2,1)S...) custom-call(s32[8]{0:T(128)S(1)} %copy-done.1, s32[8]{0:T(128)S(1)} %copy-done.2, f32[7]{0:T(128)S(1)} %copy-done.3, ...), custom_call_target="tpu_custom_call" | custom-call | flops 1 | bytes 1 | tf_op jit(solution)/shard_map/weights/pallas_call | solution.py:385
  10.4 0.0 collective-permute-done.refs_1_
  10.4 1.6 %collective-permute-start.2 = (f32[2,2,16,128]{3,2,1,0:T(8,128)S(1)}, f32[2,2,16,128]{3,2,1,0:T(8,128)S(1)}, u32[]{:S(2)}, u32[]{:S(2)}) collective-permute-start(f32[2,2,16,128]{3,2,1,0:T(8,128)S(1)} %pad_maximum_fusion.2), channel_id=1, source_target_pairs={{0,8},{4,12},{8,0},{12,4},{16,24},{20,28},{24,16},{28,20},{1,9},{5... | collective-permute-start | bytes 98312 | tf_op jit(solution)/shard_map/ppermute | solution.py:449
  12.0 0.1 collective-permute-start.5
  12.1 0.6 %collective-permute-start.8 = (f32[1,1,128,512]{3,2,1,0:T(8,128)S(1)}, f32[1,1,128,512]{3,2,1,0:T(8,128)S(1)}, u32[]{:S(2)}, u32[]{:S(2)}) collective-permute-start(f32[1,1,128,512]{3,2,1,0:T(8,128)S(1)} %get-tuple-element.43), channel_id=1, source_target_pairs={{0,2},{1,3},{2,0},{3,1},{4,6},{5,7},{6,4},{7,5},{8,10},{9,11},{10,... | collective-permute-start | bytes 786440 | tf_op jit(solution)/shard_map/ppermute | solution.py:348
  12.7 5.0 %own_terms.1.base_ref = f32[1,5,128,512]{3,2,1,0:T(8,128)S(1)} custom-call(s32[8]{0:T(128)S(1)} %copy-done.1, s32[8]{0:T(128)S(1)} %copy-done.2, f32[7]{0:T(128)S(1)} %copy-done.3, bf16[256,384]{1,0:T(8,128)(2,1)S(1)} %get-tuple-element.30.wown_ref, f32[1,5,128,512]{3,2,1,0:T(8,128)S(1)} %get-tuple-element.36.q_ref.tile_ref, ...), custom_call_target="tpu_custom_call" | custom-call | flops 1 | bytes 1 | tf_op jit(solution)/shard_map/own_terms/pallas_call | solution.py:405
  17.7 0.0 collective-permute-done.2.refs_2_
  17.8 0.0 collective-permute-done.4.refs_0_.refs_4_
  17.8 0.0 collective-permute-done.1.refs_1_.near_ref
  17.8 0.6 %send_terms.1 = f32[1,2,128,512]{3,2,1,0:T(8,128)S(1)} custom-call(bf16[1,256,768]{2,1,0:T(8,128)(2,1)S(1)} %get-tuple-element.33.wsend_ref, f32[5,8,512]{2,1,0:T(8,128)S(1)} %get-tuple-element.26.nu_ref, f32[1,5,128,512]{3,2,1,0:T(8,128)S(1)} %get-tuple-element.36.q_ref.tile_ref, f32[1,2,128,512]{3,2,1,0:T(8,128)S(1)} %collective-permute-done.4.refs_0_.refs_4_, ...), custom_call_target="tpu_custom_call" | custom-call | flops 1 | bytes 1 | tf_op jit(solution)/shard_map/send_terms/pallas_call | solution.py:456
  18.4 1.6 %collective-permute-start.10 = (f32[1,2,128,512]{3,2,1,0:T(8,128)S(1)}, f32[1,2,128,512]{3,2,1,0:T(8,128)S(1)}, u32[]{:S(2)}, u32[]{:S(2)}) collective-permute-start(f32[1,2,128,512]{3,2,1,0:T(8,128)S(1)} %send_terms.1), channel_id=1, source_target_pairs={{0,2},{1,3},{2,0},{3,1},{4,6},{5,7},{6,4},{7,5},{8,10},{9,11},{10,... | collective-permute-start | bytes 1572872 | tf_op jit(solution)/shard_map/ppermute | solution.py:465
  20.0 2.6 %collective-permute-start.3 = (f32[4,2,16,128]{3,2,1,0:T(8,128)S(1)}, f32[4,2,16,128]{3,2,1,0:T(8,128)S(1)}, u32[]{:S(2)}, u32[]{:S(2)}) collective-permute-start(f32[4,2,16,128]{3,2,1,0:T(8,128)S(1)} %pad_maximum_fusion.1), channel_id=1, source_target_pairs={{0,16},{4,20},{8,24},{12,28},{16,0},{20,4},{24,8},{28,12},{1,17},{... | collective-permute-start | bytes 196616 | tf_op jit(solution)/shard_map/ppermute | solution.py:449
  22.5 0.0 collective-permute-done.5.near_v_ref
  22.5 0.6 %sibling_terms.2 = (f32[1,1,128,512]{3,2,1,0:T(8,128)S(1)}, f32[1,1,128,512]{3,2,1,0:T(8,128)S(1)}) custom-call(bf16[256,768]{1,0:T(8,128)(2,1)S(1)} %get-tuple-element.35.w_ref, f32[5,8,512]{2,1,0:T(8,128)S(1)} %get-tuple-element.26.nu_ref, f32[1,5,128,512]{3,2,1,0:T(8,128)S(1)} %get-tuple-element.36.q_ref.tile_ref, ...), custom_call_target="tpu_custom_call" | custom-call | flops 1 | bytes 1 | tf_op jit(solution)/shard_map/sibling_terms/pallas_call | solution.py:472
  23.2 0.0 copy-start
  23.2 0.0 copy-start.4
  23.2 0.0 copy-start.5
  23.2 0.0 collective-permute-done.8.refs_0_.refs_7_
  23.2 2.8 %collective-permute-done.3.refs_3_ = f32[4,2,16,128]{3,2,1,0:T(8,128)S(1)} collective-permute-done((f32[4,2,16,128]{3,2,1,0:T(8,128)S(1)}, f32[4,2,16,128]{3,2,1,0:T(8,128)S(1)}, u32[]{:S(2)}, u32[]{:S(2)}) %collective-permute-start.3) | collective-permute-done | bytes 65568 | tf_op jit(solution)/shard_map/ppermute | solution.py:449
  26.0 0.0 collective-permute-start.6
  26.0 0.5 %collective-permute-start.7 = (f32[1,1,128,512]{3,2,1,0:T(8,128)S(1)}, f32[1,1,128,512]{3,2,1,0:T(8,128)S(1)}, u32[]{:S(2)}, u32[]{:S(2)}) collective-permute-start(f32[1,1,128,512]{3,2,1,0:T(8,128)S(1)} %get-tuple-element.38), channel_id=1, source_target_pairs={{0,1},{1,0},{2,3},{3,2},{4,5},{5,4},{6,7},{7,6},{8,9},{9,8},{10,11... | collective-permute-start | bytes 786440 | tf_op jit(solution)/shard_map/ppermute | solution.py:481
  26.5 0.4 %sibling_terms.3 = f32[1,1,128,512]{3,2,1,0:T(8,128)S(1)} custom-call(bf16[256,768]{1,0:T(8,128)(2,1)S(1)} %get-tuple-element.35.w_ref, f32[5,8,512]{2,1,0:T(8,128)S(1)} %get-tuple-element.26.nu_ref, f32[1,5,128,512]{3,2,1,0:T(8,128)S(1)} %get-tuple-element.36.q_ref.tile_ref, f32[1,1,128,512]{3,2,1,0:T(8,128)S(1)} %collective-permute-done.5.near_v_ref, ...), custom_call_target="tpu_custom_call" | custom-call | flops 1 | bytes 1 | tf_op jit(solution)/shard_map/sibling_terms/pallas_call | solution.py:472
  26.9 0.1 collective-permute-start.9
  27.0 0.6 %collective-permute-done.6.refs_5_ = f32[1,1,128,512]{3,2,1,0:T(8,128)S(1)} collective-permute-done((f32[1,1,128,512]{3,2,1,0:T(8,128)S(1)}, f32[1,1,128,512]{3,2,1,0:T(8,128)S(1)}, u32[]{:S(2)}, u32[]{:S(2)}) %collective-permute-start.6) | collective-permute-done | bytes 262176 | tf_op jit(solution)/shard_map/ppermute | solution.py:481
  27.6 0.4 %collective-permute-done.7.refs_6_ = f32[1,1,128,512]{3,2,1,0:T(8,128)S(1)} collective-permute-done((f32[1,1,128,512]{3,2,1,0:T(8,128)S(1)}, f32[1,1,128,512]{3,2,1,0:T(8,128)S(1)}, u32[]{:S(2)}, u32[]{:S(2)}) %collective-permute-start.7) | collective-permute-done | bytes 262176 | tf_op jit(solution)/shard_map/ppermute | solution.py:481
  27.9 0.6 %collective-permute-done.9.refs_8_ = f32[1,1,128,512]{3,2,1,0:T(8,128)S(1)} collective-permute-done((f32[1,1,128,512]{3,2,1,0:T(8,128)S(1)}, f32[1,1,128,512]{3,2,1,0:T(8,128)S(1)}, u32[]{:S(2)}, u32[]{:S(2)}) %collective-permute-start.9) | collective-permute-done | bytes 262176 | tf_op jit(solution)/shard_map/ppermute | solution.py:481
  28.5 0.0 copy-done
  28.5 0.0 copy-done.4
  28.5 0.0 copy-done.5
  28.5 2.4 %near_terms.1 = (f32[1,5,128,512]{3,2,1,0:T(8,128)}, f32[1,2,128,512]{3,2,1,0:T(8,128)S(1)}) custom-call(s32[8]{0:T(128)S(1)} %copy-done.1, s32[2,8]{1,0:T(2,128)S(1)} %bitcast.2, s32[2,8]{1,0:T(2,128)S(1)} %bitcast.3, s32[8]{0:T(128)S(1)} %copy-done.2, f32[6,1024]{1,0:T(8,128)S(1)} %copy-done, bf16[256,384]{1,0:T(8,128)(2,1)S(1)} %get-tuple-element.24.wnear_ref, ...), custom_call_target="tpu_custom_call" | custom-call | flops 1 | bytes 1 | tf_op jit(solution)/shard_map/near_terms/pallas_call | solution.py:487
  30.9 2.0 %collective-permute-done.10.refs_0_ = f32[1,2,128,512]{3,2,1,0:T(8,128)S(1)} collective-permute-done((f32[1,2,128,512]{3,2,1,0:T(8,128)S(1)}, f32[1,2,128,512]{3,2,1,0:T(8,128)S(1)}, u32[]{:S(2)}, u32[]{:S(2)}) %collective-permute-start.10) | collective-permute-done | bytes 524320 | tf_op jit(solution)/shard_map/ppermute | solution.py:465
  32.9 0.8 %last_terms.1 = f32[1,5,128,512]{3,2,1,0:T(8,128)} custom-call(f32[1,2,128,512]{3,2,1,0:T(8,128)S(1)} %get-tuple-element.41.left_ref, f32[1,2,128,512]{3,2,1,0:T(8,128)S(1)} %collective-permute-done.10.refs_0_, f32[1,5,128,512]{3,2,1,0:T(8,128)} %get-tuple-element.42.refs_1_), custom_call_target="tpu_custom_call", output_to_operand_aliasing={{}: (2, {})} | custom-call | flops 1 | bytes 1 | tf_op jit(solution)/shard_map/last_terms/pallas_call | solution.py:508
  (4 shorter events, 0.1 us)
Async XLA Ops:
  0.0 4.1 %copy-start.2 = (s32[8]{0:T(128)S(1)}, s32[8]{0:T(128)}, u32[]{:S(2)}) copy-start(s32[8]{0:T(128)} %rows_ref.7) | copy-start | bytes 100
  0.0 4.1 %copy-start.1 = (s32[8]{0:T(128)S(1)}, s32[8]{0:T(128)}, u32[]{:S(2)}) copy-start(s32[8]{0:T(128)} %owner_ref.7) | copy-start | bytes 100
  1.1 16.7 %collective-permute-start.4 = (f32[1,2,128,512]{3,2,1,0:T(8,128)S(1)}, f32[1,2,128,512]{3,2,1,0:T(8,128)S(1)}, u32[]{:S(2)}, u32[]{:S(2)}) collective-permute-start(f32[1,2,128,512]{3,2,1,0:T(8,128)S(1)} %part.1.part_ref), channel_id=1, source_target_pairs={{0,2},{1,3},{2,0},{3,1},{4,6},{5,7},{6,4},{7,5},{8,10},{9,11},{10,... | collective-permute-start | bytes 1572872 | tf_op jit(solution)/shard_map/ppermute | solution.py:348
  6.2 1.8 %copy-start.3 = (f32[7]{0:T(128)S(1)}, f32[7]{0:T(128)}, u32[]{:S(2)}) copy-start(f32[7]{0:T(128)} %coef_ref.3) | copy-start | bytes 88
  6.3 11.5 %collective-permute-start.1 = (f32[1,2,128,512]{3,2,1,0:T(8,128)S(1)}, f32[1,2,128,512]{3,2,1,0:T(8,128)S(1)}, u32[]{:S(2)}, u32[]{:S(2)}) collective-permute-start(f32[1,2,128,512]{3,2,1,0:T(8,128)S(1)} %pad_maximum_fusion), channel_id=1, source_target_pairs={{0,1},{1,0},{2,3},{3,2},{4,5},{5,4},{6,7},{7,6},{8,9},{9,8},{10,11... | collective-permute-start | bytes 1572872 | tf_op jit(solution)/shard_map/ppermute | solution.py:376
  6.3 4.0 %collective-permute-start = (f32[1,2,16,128]{3,2,1,0:T(8,128)S(1)}, f32[1,2,16,128]{3,2,1,0:T(8,128)S(1)}, u32[]{:S(2)}, u32[]{:S(2)}) collective-permute-start(f32[1,2,16,128]{3,2,1,0:T(8,128)S(1)} %get-tuple-element.28.refs_0_), channel_id=1, source_target_pairs={{0,4},{4,0},{8,12},{12,8},{16,20},{20,16},{24,28},{28,24},{1,5},{5... | collective-permute-start | bytes 49160 | tf_op jit(solution)/shard_map/ppermute | solution.py:449
  10.4 7.4 %collective-permute-start.2 = (f32[2,2,16,128]{3,2,1,0:T(8,128)S(1)}, f32[2,2,16,128]{3,2,1,0:T(8,128)S(1)}, u32[]{:S(2)}, u32[]{:S(2)}) collective-permute-start(f32[2,2,16,128]{3,2,1,0:T(8,128)S(1)} %pad_maximum_fusion.2), channel_id=1, source_target_pairs={{0,8},{4,12},{8,0},{12,4},{16,24},{20,28},{24,16},{28,20},{1,9},{5... | collective-permute-start | bytes 98312 | tf_op jit(solution)/shard_map/ppermute | solution.py:449
  12.0 10.5 %collective-permute-start.5 = (f32[1,1,128,512]{3,2,1,0:T(8,128)S(1)}, f32[1,1,128,512]{3,2,1,0:T(8,128)S(1)}, u32[]{:S(2)}, u32[]{:S(2)}) collective-permute-start(f32[1,1,128,512]{3,2,1,0:T(8,128)S(1)} %slice.14), channel_id=1, source_target_pairs={{0,1},{1,0},{2,3},{3,2},{4,5},{5,4},{6,7},{7,6},{8,9},{9,8},{10,11... | collective-permute-start | bytes 786440 | tf_op jit(solution)/shard_map/ppermute | solution.py:452
  12.1 11.1 %collective-permute-start.8 = (f32[1,1,128,512]{3,2,1,0:T(8,128)S(1)}, f32[1,1,128,512]{3,2,1,0:T(8,128)S(1)}, u32[]{:S(2)}, u32[]{:S(2)}) collective-permute-start(f32[1,1,128,512]{3,2,1,0:T(8,128)S(1)} %get-tuple-element.43), channel_id=1, source_target_pairs={{0,2},{1,3},{2,0},{3,1},{4,6},{5,7},{6,4},{7,5},{8,10},{9,11},{10,... | collective-permute-start | bytes 786440 | tf_op jit(solution)/shard_map/ppermute | solution.py:348
  18.4 14.5 %collective-permute-start.10 = (f32[1,2,128,512]{3,2,1,0:T(8,128)S(1)}, f32[1,2,128,512]{3,2,1,0:T(8,128)S(1)}, u32[]{:S(2)}, u32[]{:S(2)}) collective-permute-start(f32[1,2,128,512]{3,2,1,0:T(8,128)S(1)} %send_terms.1), channel_id=1, source_target_pairs={{0,2},{1,3},{2,0},{3,1},{4,6},{5,7},{6,4},{7,5},{8,10},{9,11},{10,... | collective-permute-start | bytes 1572872 | tf_op jit(solution)/shard_map/ppermute | solution.py:465
  20.0 6.1 %collective-permute-start.3 = (f32[4,2,16,128]{3,2,1,0:T(8,128)S(1)}, f32[4,2,16,128]{3,2,1,0:T(8,128)S(1)}, u32[]{:S(2)}, u32[]{:S(2)}) collective-permute-start(f32[4,2,16,128]{3,2,1,0:T(8,128)S(1)} %pad_maximum_fusion.1), channel_id=1, source_target_pairs={{0,16},{4,20},{8,24},{12,28},{16,0},{20,4},{24,8},{28,12},{1,17},{... | collective-permute-start | bytes 196616 | tf_op jit(solution)/shard_map/ppermute | solution.py:449
  23.2 5.3 %copy-start = (f32[6,1024]{1,0:T(8,128)S(1)}, f32[6,1024]{1,0:T(8,128)}, u32[]{:S(2)}) copy-start(f32[6,1024]{1,0:T(8,128)} %gop_ref.1) | copy-start | bytes 73732
  23.2 5.3 %copy-start.4 = (s32[8,2]{0,1:T(2,128)S(1)}, s32[8,2]{0,1:T(2,128)}, u32[]{:S(2)}) copy-start(s32[8,2]{0,1:T(2,128)} %param.11) | copy-start | bytes 196
  23.2 5.3 %copy-start.5 = (s32[8,2]{0,1:T(2,128)S(1)}, s32[8,2]{0,1:T(2,128)}, u32[]{:S(2)}) copy-start(s32[8,2]{0,1:T(2,128)} %param.12) | copy-start | bytes 196
  26.0 1.5 %collective-permute-start.6 = (f32[1,1,128,512]{3,2,1,0:T(8,128)S(1)}, f32[1,1,128,512]{3,2,1,0:T(8,128)S(1)}, u32[]{:S(2)}, u32[]{:S(2)}) collective-permute-start(f32[1,1,128,512]{3,2,1,0:T(8,128)S(1)} %get-tuple-element.37), channel_id=1, source_target_pairs={{0,1},{1,0},{2,3},{3,2},{4,5},{5,4},{6,7},{7,6},{8,9},{9,8},{10,11... | collective-permute-start | bytes 786440 | tf_op jit(solution)/shard_map/ppermute | solution.py:481
  26.0 1.9 %collective-permute-start.7 = (f32[1,1,128,512]{3,2,1,0:T(8,128)S(1)}, f32[1,1,128,512]{3,2,1,0:T(8,128)S(1)}, u32[]{:S(2)}, u32[]{:S(2)}) collective-permute-start(f32[1,1,128,512]{3,2,1,0:T(8,128)S(1)} %get-tuple-element.38), channel_id=1, source_target_pairs={{0,1},{1,0},{2,3},{3,2},{4,5},{5,4},{6,7},{7,6},{8,9},{9,8},{10,11... | collective-permute-start | bytes 786440 | tf_op jit(solution)/shard_map/ppermute | solution.py:481
  26.9 1.6 %collective-permute-start.9 = (f32[1,1,128,512]{3,2,1,0:T(8,128)S(1)}, f32[1,1,128,512]{3,2,1,0:T(8,128)S(1)}, u32[]{:S(2)}, u32[]{:S(2)}) collective-permute-start(f32[1,1,128,512]{3,2,1,0:T(8,128)S(1)} %sibling_terms.3), channel_id=1, source_target_pairs={{0,1},{1,0},{2,3},{3,2},{4,5},{5,4},{6,7},{7,6},{8,9},{9,8},{10,11... | collective-permute-start | bytes 786440 | tf_op jit(solution)/shard_map/ppermute | solution.py:481

commit v7 on v6

--- a/solution.py
+++ b/solution.py
@@ -12,7 +12,7 @@
 FACE_ROWS = 16
 TILE = 256
 LANES = 128
-FIRST, SECOND = (1, 3), (3, 4)
+FIRST, SECOND = (1, 2), (2, 4)
 RAW = tuple(range(FIRST[0], SECOND[1]))
 SENT = (0, 4)
 
@@ -207,9 +207,9 @@
     nu_ref,
     q_ref,
     base_ref,
-    near_ref,
     *refs,
 ):
+    near, refs = refs[: len(SENT)], refs[len(SENT) :]
     faces, refs = refs[:face_count], refs[face_count:]
     *refs, out_ref, left_ref, done_ref, sems = refs
     count = (len(refs) - len(RAW)) // 2
@@ -264,7 +264,7 @@
         ghost = jnp.transpose(jnp.concatenate(stacked + [pad], axis=0)).astype(jnp.bfloat16)
         dx = dot(ghost, operator)
         if v in SENT:
-            dy = dot(wnear_ref[...], three_parts([near_ref[0, SENT.index(v)]]))
+            dy = dot(wnear_ref[...], three_parts([near[SENT.index(v)][0, 0]]))
         else:
             *direct, from_sibling = raw[v]
             dy = dot(wdirect_ref[...], three_parts([ref[...] for ref in direct]))
@@ -283,11 +283,11 @@
 
 def send_kernel(wsend_ref, nu_ref, q_ref, *refs):
     count = wsend_ref.shape[0]
-    far_v, near, out = refs[:count], refs[count], refs[count + 1 :]
+    far_v, near, out = refs[:count], refs[count : count + len(SENT)], refs[count + len(SENT) :]
     rows = q_ref.shape[2]
     for j in range(count):
         for i, v in enumerate(SENT):
-            dy = dot(wsend_ref[j], three_parts([q_ref[0, v], near[0, i]]))
+            dy = dot(wsend_ref[j], three_parts([q_ref[0, v], near[i][0, 0]]))
             out[j][0, i] = nu_ref[v, 0:1] * dy[rows:] - far_v[j][0, 0] * dy[:rows]
 
 
@@ -373,9 +373,7 @@
     )(block_owner, rows_live, held(part), in_hbm)
     second = flow_state[:, SECOND[0] : SECOND[1]]
     direct_second = across(second)
-    near = lax.ppermute(
-        jnp.concatenate([flow_state[:, v : v + 1] for v in SENT], axis=1), "line", sibling
-    )
+    near = [lax.ppermute(flow_state[:, v : v + 1], "line", sibling) for v in SENT]
 
     w_near = jax.ShapeDtypeStruct((2 * rows, 3 * rows), jnp.bfloat16)
     w_far = jax.ShapeDtypeStruct((2 * rows, 3 * len(shifts) * rows), jnp.bfloat16)
@@ -436,7 +434,7 @@
     sent = jax.ShapeDtypeStruct((1, len(SENT), rows, x_length), jnp.float32)
     send = pl.pallas_call(
         send_kernel,
-        in_specs=[kept()] * (4 + len(shifts)),
+        in_specs=[kept()] * (3 + len(SENT) + len(shifts)),
         out_specs=[kept()] * len(shifts),
         out_shape=[sent] * len(shifts),
         compiler_params=limit,
@@ -451,11 +449,12 @@
             there, w_own, own = lax.optimization_barrier((there, w_own, flow_state))
             near_v = lax.ppermute(own[:, 1:2], "line", sibling)
         elif step == 2:
-            state = own_terms(w_own)
-            w_send, *_ = lax.optimization_barrier((w_send, state, there))
-            results = send(*map(held, (w_send, nu, flow_state, *far_v, near)))
+            w_send, *_ = lax.optimization_barrier((w_send, there))
+            results = send(*map(held, (w_send, nu, flow_state, *far_v, *near)))
             direct_first, *_ = lax.optimization_barrier((direct_first, *results))
             direct_second, *_ = lax.optimization_barrier((direct_second, *results))
+            w_own, *_ = lax.optimization_barrier((w_own, *results))
+            state = own_terms(w_own)
         arrived.append(there)
         step *= 2
         if step < slots:
@@ -480,13 +479,13 @@
         )(*operands)
         return [*direct, *(lax.ppermute(result, "line", sibling) for result in results)]
 
-    direct_second, *_ = lax.optimization_barrier((direct_second, *arrived))
+    direct_second, *_ = lax.optimization_barrier((direct_second, state, *arrived))
     pieces = sibling_terms(FIRST, direct_first) + sibling_terms(SECOND, direct_second)
 
     anywhere = pl.BlockSpec(memory_space=pl.ANY)
     result, left = pl.pallas_call(
         functools.partial(near_kernel, len(arrived)),
-        in_specs=[smem()] * 4 + [kept()] * (7 + len(arrived) + len(pieces)),
+        in_specs=[smem()] * 4 + [kept()] * (6 + len(SENT) + len(arrived) + len(pieces)),
         out_specs=[anywhere, kept()],
         out_shape=[state_shape, sent],
         scratch_shapes=[
@@ -501,7 +500,7 @@
         link_block.T,
         link_side.T,
         rows_live,
-        *map(held, (ghost_operator, w_near, w_direct, nu, flow_state, state, near, *arrived, *pieces)),
+        *map(held, (ghost_operator, w_near, w_direct, nu, flow_state, state, *near, *arrived, *pieces)),
     )
 
     operands = [*map(held, (left, *results))]

time: 33.9 us -> 33.8 us (level)
  waiting for transfers between devices: 6.28 us -> 5.74 us
  starting transfers between devices: 11.7 us -> 12.2 us
    ppermute x2, starting transfers between devices: 3.6 us -> 3.1 us  [across(): lax.ppermute(array, 'line', [(i, (i + s) % lines) for i in range(lines)])]
    ppermute x1 -> x2, starting transfers between devices: 0.07 us -> 0.57 us  [on_device(): near = [lax.ppermute(flow_state[:, v:v + 1], 'line', sibling) for v in SENT]]
    ppermute x3, waiting for transfers between devices: 2.79 us -> 2.32 us  [on_device(): lax.ppermute(held_faces, 'blk', [(i, i ^ step) for i in range(slots)])]
    ppermute x3, starting transfers between devices: 5.82 us -> 6.26 us  [on_device(): lax.ppermute(held_faces, 'blk', [(i, i ^ step) for i in range(slots)])]
  transfers between devices with their start and end apart: 11 -> 12, of which waited for: 5 -> 5; matrix products, arithmetic and copies ran while one was open for 0% -> 0% of each run, Pallas kernels for 40% -> 40%
where the time goes in v7:
time: 33.8 us; the launch traced here: 33.6 us
  Pallas kernels  15.4 us (46%)
  starting transfers between devices  12.2 us (36%)
  waiting for transfers between devices  5.74 us (17%)
    ppermute x3, starting transfers between devices, on_device(): lax.ppermute(held_faces, 'blk', [(i, i ^ step) for i in range(slots)])  6.26 us
    pallas_call x1, Pallas kernels, own_terms(): pl.pallas_call(own_kernel, grid=(tiles,), in_specs=[smem()] * 3 + [pl.Blo...  5.02 us
    ppermute x2, starting transfers between devices, across(): lax.ppermute(array, 'line', [(i, (i + s) % lines) for i in range(lines)])  3.1 us
    pallas_call x1, Pallas kernels, on_device(): pl.pallas_call(functools.partial(near_kernel, len(arrived)), in_specs=[sm...  2.42 us
    pallas_call x1, Pallas kernels, on_device(): pl.pallas_call(functools.partial(weights_kernel, lines), in_specs=[smem()...  2.41 us
    ppermute x3, waiting for transfers between devices, on_device(): lax.ppermute(held_faces, 'blk', [(i, i ^ step) for i in range(slots)])  2.32 us
    pallas_call x1, Pallas kernels, on_device(): pl.pallas_call(faces_kernel, in_specs=[smem(), smem(), kept(), pl.BlockSp...  2.04 us
    ppermute x1, waiting for transfers between devices, on_device(): lax.ppermute(result, 'line', [(i, (i + s) % lines) for i in range(lines)])  1.95 us
  transfers between devices with their start and end apart: 12, of which 5 were waited for; matrix products, arithmetic and copies ran while one was open for 0% of the time, Pallas kernels for 40%

profile of v7, /device:TPU:0, one launch (start us, length us, event | category | flops | bytes accessed | tf_op | source)
XLA Modules:
  0.0 33.6 jit_solution(14516451167699480057)
XLA Ops:
  0.0 0.0 copy-start.2
  0.0 0.0 copy-start.1
  0.0 1.0 %part.1.part_ref = f32[1,1,128,512]{3,2,1,0:T(8,128)S(1)} custom-call(f32[1,5,128,512]{3,2,1,0:T(8,128)} %q_ref.3), custom_call_target="tpu_custom_call" | custom-call | flops 1 | bytes 1 | tf_op jit(solution)/shard_map/part/pallas_call | solution.py:351
  1.0 3.0 %collective-permute-start.2 = (f32[1,1,128,512]{3,2,1,0:T(8,128)S(1)}, f32[1,1,128,512]{3,2,1,0:T(8,128)S(1)}, u32[]{:S(2)}, u32[]{:S(2)}) collective-permute-start(f32[1,1,128,512]{3,2,1,0:T(8,128)S(1)} %part.1.part_ref), channel_id=1, source_target_pairs={{0,2},{1,3},{2,0},{3,1},{4,6},{5,7},{6,4},{7,5},{8,10},{9,11},{10,... | collective-permute-start | bytes 786440 | tf_op jit(solution)/shard_map/ppermute | solution.py:348
  4.0 0.0 copy-done.2
  4.0 0.0 copy-done.1
  4.0 2.0 %faces.1 = (f32[1,5,128,512]{3,2,1,0:T(8,128)S(1)}, f32[1,2,16,128]{3,2,1,0:T(8,128)S(1)}) custom-call(s32[8]{0:T(128)S(1)} %copy-done.1, s32[8]{0:T(128)S(1)} %copy-done.2, f32[1,1,128,512]{3,2,1,0:T(8,128)S(1)} %part.1.part_ref, f32[1,5,128,512]{3,2,1,0:T(8,128)} %q_ref.3), custom_call_target="tpu_custom_call" | custom-call | flops 1 | bytes 1 | tf_op jit(solution)/shard_map/faces/pallas_call | solution.py:364
  6.1 0.0 copy-start.3
  6.1 0.1 collective-permute-start.8
  6.2 0.1 collective-permute-start.4
  6.3 0.5 %collective-permute-start.3 = (f32[1,1,128,512]{3,2,1,0:T(8,128)S(1)}, f32[1,1,128,512]{3,2,1,0:T(8,128)S(1)}, u32[]{:S(2)}, u32[]{:S(2)}) collective-permute-start(f32[1,1,128,512]{3,2,1,0:T(8,128)S(1)} %get-tuple-element.46), channel_id=1, source_target_pairs={{0,1},{1,0},{2,3},{3,2},{4,5},{5,4},{6,7},{7,6},{8,9},{9,8},{10,11... | collective-permute-start | bytes 786440 | tf_op jit(solution)/shard_map/ppermute | solution.py:376
  6.8 2.0 %collective-permute-start = (f32[1,2,16,128]{3,2,1,0:T(8,128)S(1)}, f32[1,2,16,128]{3,2,1,0:T(8,128)S(1)}, u32[]{:S(2)}, u32[]{:S(2)}) collective-permute-start(f32[1,2,16,128]{3,2,1,0:T(8,128)S(1)} %get-tuple-element.29.refs_2_), channel_id=1, source_target_pairs={{0,4},{4,0},{8,12},{12,8},{16,20},{20,16},{24,28},{28,24},{1,5},{5... | collective-permute-start | bytes 49160 | tf_op jit(solution)/shard_map/ppermute | solution.py:447
  8.8 0.0 copy-done.3
  8.9 2.4 %weights.1 = (bf16[256,384]{1,0:T(8,128)(2,1)S(1)}, bf16[256,384]{1,0:T(8,128)(2,1)S(1)}, bf16[256,384]{1,0:T(8,128)(2,1)S(1)}, bf16[256,768]{1,0:T(8,128)(2,1)S...) custom-call(s32[8]{0:T(128)S(1)} %copy-done.1, s32[8]{0:T(128)S(1)} %copy-done.2, f32[7]{0:T(128)S(1)} %copy-done.3, ...), custom_call_target="tpu_custom_call" | custom-call | flops 1 | bytes 1 | tf_op jit(solution)/shard_map/weights/pallas_call | solution.py:383
  11.3 0.0 collective-permute-done.refs_3_
  11.3 1.6 %collective-permute-start.1 = (f32[2,2,16,128]{3,2,1,0:T(8,128)S(1)}, f32[2,2,16,128]{3,2,1,0:T(8,128)S(1)}, u32[]{:S(2)}, u32[]{:S(2)}) collective-permute-start(f32[2,2,16,128]{3,2,1,0:T(8,128)S(1)} %pad_maximum_fusion.1), channel_id=1, source_target_pairs={{0,8},{4,12},{8,0},{12,4},{16,24},{20,28},{24,16},{28,20},{1,9},{5... | collective-permute-start | bytes 98312 | tf_op jit(solution)/shard_map/ppermute | solution.py:447
  13.0 2.3 %collective-permute-done.1.refs_4_ = f32[2,2,16,128]{3,2,1,0:T(8,128)S(1)} collective-permute-done((f32[2,2,16,128]{3,2,1,0:T(8,128)S(1)}, f32[2,2,16,128]{3,2,1,0:T(8,128)S(1)}, u32[]{:S(2)}, u32[]{:S(2)}) %collective-permute-start.1) | collective-permute-done | bytes 32800 | tf_op jit(solution)/shard_map/ppermute | solution.py:447
  15.3 0.0 collective-permute-start.6
  15.3 0.0 collective-permute-done.2.refs_0_.refs_6_
  15.3 0.0 collective-permute-done.4.refs_2_.refs_1_
  15.3 0.0 collective-permute-done.3.refs_1_.refs_0_
  15.3 0.6 %send_terms.1 = f32[1,2,128,512]{3,2,1,0:T(8,128)S(1)} custom-call(bf16[1,256,768]{2,1,0:T(8,128)(2,1)S(1)} %get-tuple-element.34.wsend_ref, f32[5,8,512]{2,1,0:T(8,128)S(1)} %get-tuple-element.27.nu_ref, f32[1,5,128,512]{3,2,1,0:T(8,128)S(1)} %get-tuple-element.38.q_ref.tile_ref, f32[1,1,128,512]{3,2,1,0:T(8,128)S(1)} %collective-permute-done.2.refs_0_.refs_6_, ...), custom_call_target="tpu_custom_call" | custom-call | flops 1 | bytes 1 | tf_op jit(solution)/shard_map/send_terms/pallas_call | solution.py:453
  15.9 1.6 %collective-permute-start.11 = (f32[1,2,128,512]{3,2,1,0:T(8,128)S(1)}, f32[1,2,128,512]{3,2,1,0:T(8,128)S(1)}, u32[]{:S(2)}, u32[]{:S(2)}) collective-permute-start(f32[1,2,128,512]{3,2,1,0:T(8,128)S(1)} %send_terms.1), channel_id=1, source_target_pairs={{0,2},{1,3},{2,0},{3,1},{4,6},{5,7},{6,4},{7,5},{8,10},{9,11},{10,... | collective-permute-start | bytes 1572872 | tf_op jit(solution)/shard_map/ppermute | solution.py:464
  17.5 2.6 %collective-permute-start.5 = (f32[4,2,16,128]{3,2,1,0:T(8,128)S(1)}, f32[4,2,16,128]{3,2,1,0:T(8,128)S(1)}, u32[]{:S(2)}, u32[]{:S(2)}) collective-permute-start(f32[4,2,16,128]{3,2,1,0:T(8,128)S(1)} %pad_maximum_fusion), channel_id=1, source_target_pairs={{0,16},{4,20},{8,24},{12,28},{16,0},{20,4},{24,8},{28,12},{1,17},{... | collective-permute-start | bytes 196616 | tf_op jit(solution)/shard_map/ppermute | solution.py:447
  20.1 5.0 %own_terms.1.base_ref = f32[1,5,128,512]{3,2,1,0:T(8,128)S(1)} custom-call(s32[8]{0:T(128)S(1)} %copy-done.1, s32[8]{0:T(128)S(1)} %copy-done.2, f32[7]{0:T(128)S(1)} %copy-done.3, bf16[256,384]{1,0:T(8,128)(2,1)S(1)} %get-tuple-element.35.wown_ref, f32[1,5,128,512]{3,2,1,0:T(8,128)S(1)} %get-tuple-element.38.q_ref.tile_ref, ...), custom_call_target="tpu_custom_call" | custom-call | flops 1 | bytes 1 | tf_op jit(solution)/shard_map/own_terms/pallas_call | solution.py:403
  25.1 0.0 collective-permute-done.6.near_v_ref
  25.1 0.4 %sibling_terms.2 = f32[1,1,128,512]{3,2,1,0:T(8,128)S(1)} custom-call(bf16[256,768]{1,0:T(8,128)(2,1)S(1)} %get-tuple-element.37.w_ref, f32[5,8,512]{2,1,0:T(8,128)S(1)} %get-tuple-element.27.nu_ref, f32[1,5,128,512]{3,2,1,0:T(8,128)S(1)} %get-tuple-element.38.q_ref.tile_ref, f32[1,1,128,512]{3,2,1,0:T(8,128)S(1)} %collective-permute-done.6.near_v_ref, ...), custom_call_target="tpu_custom_call" | custom-call | flops 1 | bytes 1 | tf_op jit(solution)/shard_map/sibling_terms/pallas_call | solution.py:471
  25.5 0.0 copy-start
  25.5 0.0 copy-start.4
  25.6 0.0 copy-start.5
  25.6 0.1 collective-permute-start.7
  25.6 0.0 collective-permute-done.8.refs_0_.refs_8_
  25.7 0.0 collective-permute-done.5.refs_5_
  25.7 0.6 %sibling_terms.3 = (f32[1,1,128,512]{3,2,1,0:T(8,128)S(1)}, f32[1,1,128,512]{3,2,1,0:T(8,128)S(1)}) custom-call(bf16[256,768]{1,0:T(8,128)(2,1)S(1)} %get-tuple-element.37.w_ref, f32[5,8,512]{2,1,0:T(8,128)S(1)} %get-tuple-element.27.nu_ref, f32[1,5,128,512]{3,2,1,0:T(8,128)S(1)} %get-tuple-element.38.q_ref.tile_ref, ...), custom_call_target="tpu_custom_call" | custom-call | flops 1 | bytes 1 | tf_op jit(solution)/shard_map/sibling_terms/pallas_call | solution.py:471
  26.3 0.5 %collective-permute-start.9 = (f32[1,1,128,512]{3,2,1,0:T(8,128)S(1)}, f32[1,1,128,512]{3,2,1,0:T(8,128)S(1)}, u32[]{:S(2)}, u32[]{:S(2)}) collective-permute-start(f32[1,1,128,512]{3,2,1,0:T(8,128)S(1)} %get-tuple-element.41), channel_id=1, source_target_pairs={{0,1},{1,0},{2,3},{3,2},{4,5},{5,4},{6,7},{7,6},{8,9},{9,8},{10,11... | collective-permute-start | bytes 786440 | tf_op jit(solution)/shard_map/ppermute | solution.py:480
  26.9 0.1 collective-permute-start.10
  26.9 0.2 collective-permute-done.7.refs_7_
  27.2 0.9 %collective-permute-done.9.refs_9_ = f32[1,1,128,512]{3,2,1,0:T(8,128)S(1)} collective-permute-done((f32[1,1,128,512]{3,2,1,0:T(8,128)S(1)}, f32[1,1,128,512]{3,2,1,0:T(8,128)S(1)}, u32[]{:S(2)}, u32[]{:S(2)}) %collective-permute-start.9) | collective-permute-done | bytes 262176 | tf_op jit(solution)/shard_map/ppermute | solution.py:480
  28.0 0.4 %collective-permute-done.10.refs_10_ = f32[1,1,128,512]{3,2,1,0:T(8,128)S(1)} collective-permute-done((f32[1,1,128,512]{3,2,1,0:T(8,128)S(1)}, f32[1,1,128,512]{3,2,1,0:T(8,128)S(1)}, u32[]{:S(2)}, u32[]{:S(2)}) %collective-permute-start.10) | collective-permute-done | bytes 262176 | tf_op jit(solution)/shard_map/ppermute | solution.py:480
  28.4 0.0 copy-done
  28.4 0.0 copy-done.4
  28.4 0.0 copy-done.5
  28.4 2.4 %near_terms.1 = (f32[1,5,128,512]{3,2,1,0:T(8,128)}, f32[1,2,128,512]{3,2,1,0:T(8,128)S(1)}) custom-call(s32[8]{0:T(128)S(1)} %copy-done.1, s32[2,8]{1,0:T(2,128)S(1)} %bitcast.2, s32[2,8]{1,0:T(2,128)S(1)} %bitcast.3, s32[8]{0:T(128)S(1)} %copy-done.2, f32[6,1024]{1,0:T(8,128)S(1)} %copy-done, bf16[256,384]{1,0:T(8,128)(2,1)S(1)} %get-tuple-element.25.wnear_ref, ...), custom_call_target="tpu_custom_call" | custom-call | flops 1 | bytes 1 | tf_op jit(solution)/shard_map/near_terms/pallas_call | solution.py:486
  30.8 2.0 %collective-permute-done.11.refs_0_ = f32[1,2,128,512]{3,2,1,0:T(8,128)S(1)} collective-permute-done((f32[1,2,128,512]{3,2,1,0:T(8,128)S(1)}, f32[1,2,128,512]{3,2,1,0:T(8,128)S(1)}, u32[]{:S(2)}, u32[]{:S(2)}) %collective-permute-start.11) | collective-permute-done | bytes 524320 | tf_op jit(solution)/shard_map/ppermute | solution.py:464
  32.8 0.8 %last_terms.1 = f32[1,5,128,512]{3,2,1,0:T(8,128)} custom-call(f32[1,2,128,512]{3,2,1,0:T(8,128)S(1)} %get-tuple-element.43.left_ref, f32[1,2,128,512]{3,2,1,0:T(8,128)S(1)} %collective-permute-done.11.refs_0_, f32[1,5,128,512]{3,2,1,0:T(8,128)} %get-tuple-element.44.refs_1_), custom_call_target="tpu_custom_call", output_to_operand_aliasing={{}: (2, {})} | custom-call | flops 1 | bytes 1 | tf_op jit(solution)/shard_map/last_terms/pallas_call | solution.py:507
  (5 shorter events, 0.1 us)
Async XLA Ops:
  0.0 4.0 %copy-start.2 = (s32[8]{0:T(128)S(1)}, s32[8]{0:T(128)}, u32[]{:S(2)}) copy-start(s32[8]{0:T(128)} %rows_ref.7) | copy-start | bytes 100
  0.0 4.0 %copy-start.1 = (s32[8]{0:T(128)S(1)}, s32[8]{0:T(128)}, u32[]{:S(2)}) copy-start(s32[8]{0:T(128)} %owner_ref.7) | copy-start | bytes 100
  1.0 14.3 %collective-permute-start.2 = (f32[1,1,128,512]{3,2,1,0:T(8,128)S(1)}, f32[1,1,128,512]{3,2,1,0:T(8,128)S(1)}, u32[]{:S(2)}, u32[]{:S(2)}) collective-permute-start(f32[1,1,128,512]{3,2,1,0:T(8,128)S(1)} %part.1.part_ref), channel_id=1, source_target_pairs={{0,2},{1,3},{2,0},{3,1},{4,6},{5,7},{6,4},{7,5},{8,10},{9,11},{10,... | collective-permute-start | bytes 786440 | tf_op jit(solution)/shard_map/ppermute | solution.py:348
  6.1 2.8 %copy-start.3 = (f32[7]{0:T(128)S(1)}, f32[7]{0:T(128)}, u32[]{:S(2)}) copy-start(f32[7]{0:T(128)} %coef_ref.3) | copy-start | bytes 88
  6.1 19.5 %collective-permute-start.8 = (f32[1,2,128,512]{3,2,1,0:T(8,128)S(1)}, f32[1,2,128,512]{3,2,1,0:T(8,128)S(1)}, u32[]{:S(2)}, u32[]{:S(2)}) collective-permute-start(f32[1,2,128,512]{3,2,1,0:T(8,128)S(1)} %slice.15), channel_id=1, source_target_pairs={{0,2},{1,3},{2,0},{3,1},{4,6},{5,7},{6,4},{7,5},{8,10},{9,11},{10,... | collective-permute-start | bytes 1572872 | tf_op jit(solution)/shard_map/ppermute | solution.py:348
  6.2 9.0 %collective-permute-start.4 = (f32[1,1,128,512]{3,2,1,0:T(8,128)S(1)}, f32[1,1,128,512]{3,2,1,0:T(8,128)S(1)}, u32[]{:S(2)}, u32[]{:S(2)}) collective-permute-start(f32[1,1,128,512]{3,2,1,0:T(8,128)S(1)} %get-tuple-element.45), channel_id=1, source_target_pairs={{0,1},{1,0},{2,3},{3,2},{4,5},{5,4},{6,7},{7,6},{8,9},{9,8},{10,11... | collective-permute-start | bytes 786440 | tf_op jit(solution)/shard_map/ppermute | solution.py:376
  6.3 9.0 %collective-permute-start.3 = (f32[1,1,128,512]{3,2,1,0:T(8,128)S(1)}, f32[1,1,128,512]{3,2,1,0:T(8,128)S(1)}, u32[]{:S(2)}, u32[]{:S(2)}) collective-permute-start(f32[1,1,128,512]{3,2,1,0:T(8,128)S(1)} %get-tuple-element.46), channel_id=1, source_target_pairs={{0,1},{1,0},{2,3},{3,2},{4,5},{5,4},{6,7},{7,6},{8,9},{9,8},{10,11... | collective-permute-start | bytes 786440 | tf_op jit(solution)/shard_map/ppermute | solution.py:376
  6.8 4.4 %collective-permute-start = (f32[1,2,16,128]{3,2,1,0:T(8,128)S(1)}, f32[1,2,16,128]{3,2,1,0:T(8,128)S(1)}, u32[]{:S(2)}, u32[]{:S(2)}) collective-permute-start(f32[1,2,16,128]{3,2,1,0:T(8,128)S(1)} %get-tuple-element.29.refs_2_), channel_id=1, source_target_pairs={{0,4},{4,0},{8,12},{12,8},{16,20},{20,16},{24,28},{28,24},{1,5},{5... | collective-permute-start | bytes 49160 | tf_op jit(solution)/shard_map/ppermute | solution.py:447
  11.3 4.0 %collective-permute-start.1 = (f32[2,2,16,128]{3,2,1,0:T(8,128)S(1)}, f32[2,2,16,128]{3,2,1,0:T(8,128)S(1)}, u32[]{:S(2)}, u32[]{:S(2)}) collective-permute-start(f32[2,2,16,128]{3,2,1,0:T(8,128)S(1)} %pad_maximum_fusion.1), channel_id=1, source_target_pairs={{0,8},{4,12},{8,0},{12,4},{16,24},{20,28},{24,16},{28,20},{1,9},{5... | collective-permute-start | bytes 98312 | tf_op jit(solution)/shard_map/ppermute | solution.py:447
  15.3 9.8 %collective-permute-start.6 = (f32[1,1,128,512]{3,2,1,0:T(8,128)S(1)}, f32[1,1,128,512]{3,2,1,0:T(8,128)S(1)}, u32[]{:S(2)}, u32[]{:S(2)}) collective-permute-start(f32[1,1,128,512]{3,2,1,0:T(8,128)S(1)} %slice.14), channel_id=1, source_target_pairs={{0,1},{1,0},{2,3},{3,2},{4,5},{5,4},{6,7},{7,6},{8,9},{9,8},{10,11... | collective-permute-start | bytes 786440 | tf_op jit(solution)/shard_map/ppermute | solution.py:450
  15.9 16.8 %collective-permute-start.11 = (f32[1,2,128,512]{3,2,1,0:T(8,128)S(1)}, f32[1,2,128,512]{3,2,1,0:T(8,128)S(1)}, u32[]{:S(2)}, u32[]{:S(2)}) collective-permute-start(f32[1,2,128,512]{3,2,1,0:T(8,128)S(1)} %send_terms.1), channel_id=1, source_target_pairs={{0,2},{1,3},{2,0},{3,1},{4,6},{5,7},{6,4},{7,5},{8,10},{9,11},{10,... | collective-permute-start | bytes 1572872 | tf_op jit(solution)/shard_map/ppermute | solution.py:464
  17.5 8.2 %collective-permute-start.5 = (f32[4,2,16,128]{3,2,1,0:T(8,128)S(1)}, f32[4,2,16,128]{3,2,1,0:T(8,128)S(1)}, u32[]{:S(2)}, u32[]{:S(2)}) collective-permute-start(f32[4,2,16,128]{3,2,1,0:T(8,128)S(1)} %pad_maximum_fusion), channel_id=1, source_target_pairs={{0,16},{4,20},{8,24},{12,28},{16,0},{20,4},{24,8},{28,12},{1,17},{... | collective-permute-start | bytes 196616 | tf_op jit(solution)/shard_map/ppermute | solution.py:447
  25.5 2.9 %copy-start = (f32[6,1024]{1,0:T(8,128)S(1)}, f32[6,1024]{1,0:T(8,128)}, u32[]{:S(2)}) copy-start(f32[6,1024]{1,0:T(8,128)} %gop_ref.1) | copy-start | bytes 73732
  25.5 2.9 %copy-start.4 = (s32[8,2]{0,1:T(2,128)S(1)}, s32[8,2]{0,1:T(2,128)}, u32[]{:S(2)}) copy-start(s32[8,2]{0,1:T(2,128)} %param.11) | copy-start | bytes 196
  25.6 2.8 %copy-start.5 = (s32[8,2]{0,1:T(2,128)S(1)}, s32[8,2]{0,1:T(2,128)}, u32[]{:S(2)}) copy-start(s32[8,2]{0,1:T(2,128)} %param.12) | copy-start | bytes 196
  25.6 1.6 %collective-permute-start.7 = (f32[1,1,128,512]{3,2,1,0:T(8,128)S(1)}, f32[1,1,128,512]{3,2,1,0:T(8,128)S(1)}, u32[]{:S(2)}, u32[]{:S(2)}) collective-permute-start(f32[1,1,128,512]{3,2,1,0:T(8,128)S(1)} %sibling_terms.2), channel_id=1, source_target_pairs={{0,1},{1,0},{2,3},{3,2},{4,5},{5,4},{6,7},{7,6},{8,9},{9,8},{10,11... | collective-permute-start | bytes 786440 | tf_op jit(solution)/shard_map/ppermute | solution.py:480
  26.3 1.7 %collective-permute-start.9 = (f32[1,1,128,512]{3,2,1,0:T(8,128)S(1)}, f32[1,1,128,512]{3,2,1,0:T(8,128)S(1)}, u32[]{:S(2)}, u32[]{:S(2)}) collective-permute-start(f32[1,1,128,512]{3,2,1,0:T(8,128)S(1)} %get-tuple-element.41), channel_id=1, source_target_pairs={{0,1},{1,0},{2,3},{3,2},{4,5},{5,4},{6,7},{7,6},{8,9},{9,8},{10,11... | collective-permute-start | bytes 786440 | tf_op jit(solution)/shard_map/ppermute | solution.py:480
  26.9 1.5 %collective-permute-start.10 = (f32[1,1,128,512]{3,2,1,0:T(8,128)S(1)}, f32[1,1,128,512]{3,2,1,0:T(8,128)S(1)}, u32[]{:S(2)}, u32[]{:S(2)}) collective-permute-start(f32[1,1,128,512]{3,2,1,0:T(8,128)S(1)} %get-tuple-element.42), channel_id=1, source_target_pairs={{0,1},{1,0},{2,3},{3,2},{4,5},{5,4},{6,7},{7,6},{8,9},{9,8},{10,11... | collective-permute-start | bytes 786440 | tf_op jit(solution)/shard_map/ppermute | solution.py:480

commit v8 on v7

--- a/solution.py
+++ b/solution.py
@@ -479,7 +479,7 @@
         )(*operands)
         return [*direct, *(lax.ppermute(result, "line", sibling) for result in results)]
 
-    direct_second, *_ = lax.optimization_barrier((direct_second, state, *arrived))
+    direct_second, *_ = lax.optimization_barrier((direct_second, *arrived))
     pieces = sibling_terms(FIRST, direct_first) + sibling_terms(SECOND, direct_second)
 
     anywhere = pl.BlockSpec(memory_space=pl.ANY)

time: 33.8 us -> 33.8 us (level)
    ppermute x1, waiting for transfers between devices: 1.95 us -> 0.02 us  [on_device(): lax.ppermute(result, 'line', [(i, (i + s) % lines) for i in range(lines)])]
    ppermute x2, waiting for transfers between devices: 0.01 us -> 1.84 us  [across(): lax.ppermute(array, 'line', [(i, (i + s) % lines) for i in range(lines)])]
    ppermute x3, waiting for transfers between devices: 2.32 us -> 3.99 us  [on_device(): lax.ppermute(held_faces, 'blk', [(i, i ^ step) for i in range(slots)])]
    ppermute x3, waiting for transfers between devices: 1.46 us -> 0.01 us  [sibling_terms(): lax.ppermute(result, 'line', sibling)]
  transfers between devices with their start and end apart: 12 -> 12, of which waited for: 5 -> 3; matrix products, arithmetic and copies ran while one was open for 0% -> 0% of each run, Pallas kernels for 40% -> 40%
where the time goes in v8:
time: 33.8 us; the launch traced here: 33.6 us
  Pallas kernels  15.3 us (45%)
  starting transfers between devices  12.1 us (36%)
  waiting for transfers between devices  5.87 us (17%)
    ppermute x3, starting transfers between devices, on_device(): lax.ppermute(held_faces, 'blk', [(i, i ^ step) for i in range(slots)])  6.25 us
    pallas_call x1, Pallas kernels, own_terms(): pl.pallas_call(own_kernel, grid=(tiles,), in_specs=[smem()] * 3 + [pl.Blo...  5.02 us
    ppermute x3, waiting for transfers between devices, on_device(): lax.ppermute(held_faces, 'blk', [(i, i ^ step) for i in range(slots)])  3.99 us
    ppermute x2, starting transfers between devices, across(): lax.ppermute(array, 'line', [(i, (i + s) % lines) for i in range(lines)])  3.1 us
    pallas_call x1, Pallas kernels, on_device(): pl.pallas_call(functools.partial(weights_kernel, lines), in_specs=[smem()...  2.41 us
    pallas_call x1, Pallas kernels, on_device(): pl.pallas_call(functools.partial(near_kernel, len(arrived)), in_specs=[sm...  2.39 us
    pallas_call x1, Pallas kernels, on_device(): pl.pallas_call(faces_kernel, in_specs=[smem(), smem(), kept(), pl.BlockSp...  2.04 us
    ppermute x2, waiting for transfers between devices, across(): lax.ppermute(array, 'line', [(i, (i + s) % lines) for i in range(lines)])  1.84 us
  transfers between devices with their start and end apart: 12, of which 3 were waited for; matrix products, arithmetic and copies ran while one was open for 0% of the time, Pallas kernels for 40%

profile of v8, /device:TPU:0, one launch (start us, length us, event | category | flops | bytes accessed | tf_op | source)
XLA Modules:
  0.0 33.6 jit_solution(9994552184464873784)
XLA Ops:
  0.0 0.0 copy-start.2
  0.0 0.0 copy-start.1
  0.0 1.0 %part.1.part_ref = f32[1,1,128,512]{3,2,1,0:T(8,128)S(1)} custom-call(f32[1,5,128,512]{3,2,1,0:T(8,128)} %q_ref.3), custom_call_target="tpu_custom_call" | custom-call | flops 1 | bytes 1 | tf_op jit(solution)/shard_map/part/pallas_call | solution.py:351
  1.0 3.0 %collective-permute-start.2 = (f32[1,1,128,512]{3,2,1,0:T(8,128)S(1)}, f32[1,1,128,512]{3,2,1,0:T(8,128)S(1)}, u32[]{:S(2)}, u32[]{:S(2)}) collective-permute-start(f32[1,1,128,512]{3,2,1,0:T(8,128)S(1)} %part.1.part_ref), channel_id=1, source_target_pairs={{0,2},{1,3},{2,0},{3,1},{4,6},{5,7},{6,4},{7,5},{8,10},{9,11},{10,... | collective-permute-start | bytes 786440 | tf_op jit(solution)/shard_map/ppermute | solution.py:348
  4.0 0.0 copy-done.2
  4.0 0.0 copy-done.1
  4.0 2.0 %faces.1 = (f32[1,5,128,512]{3,2,1,0:T(8,128)S(1)}, f32[1,2,16,128]{3,2,1,0:T(8,128)S(1)}) custom-call(s32[8]{0:T(128)S(1)} %copy-done.1, s32[8]{0:T(128)S(1)} %copy-done.2, f32[1,1,128,512]{3,2,1,0:T(8,128)S(1)} %part.1.part_ref, f32[1,5,128,512]{3,2,1,0:T(8,128)} %q_ref.3), custom_call_target="tpu_custom_call" | custom-call | flops 1 | bytes 1 | tf_op jit(solution)/shard_map/faces/pallas_call | solution.py:364
  6.1 0.0 copy-start.3
  6.1 0.1 collective-permute-start.8
  6.2 0.1 collective-permute-start.4
  6.3 0.5 %collective-permute-start.3 = (f32[1,1,128,512]{3,2,1,0:T(8,128)S(1)}, f32[1,1,128,512]{3,2,1,0:T(8,128)S(1)}, u32[]{:S(2)}, u32[]{:S(2)}) collective-permute-start(f32[1,1,128,512]{3,2,1,0:T(8,128)S(1)} %get-tuple-element.46), channel_id=1, source_target_pairs={{0,1},{1,0},{2,3},{3,2},{4,5},{5,4},{6,7},{7,6},{8,9},{9,8},{10,11... | collective-permute-start | bytes 786440 | tf_op jit(solution)/shard_map/ppermute | solution.py:376
  6.8 2.0 %collective-permute-start = (f32[1,2,16,128]{3,2,1,0:T(8,128)S(1)}, f32[1,2,16,128]{3,2,1,0:T(8,128)S(1)}, u32[]{:S(2)}, u32[]{:S(2)}) collective-permute-start(f32[1,2,16,128]{3,2,1,0:T(8,128)S(1)} %get-tuple-element.29.refs_2_), channel_id=1, source_target_pairs={{0,4},{4,0},{8,12},{12,8},{16,20},{20,16},{24,28},{28,24},{1,5},{5... | collective-permute-start | bytes 49160 | tf_op jit(solution)/shard_map/ppermute | solution.py:447
  8.8 0.0 copy-done.3
  8.9 2.4 %weights.1 = (bf16[256,384]{1,0:T(8,128)(2,1)S(1)}, bf16[256,384]{1,0:T(8,128)(2,1)S(1)}, bf16[256,384]{1,0:T(8,128)(2,1)S(1)}, bf16[256,768]{1,0:T(8,128)(2,1)S...) custom-call(s32[8]{0:T(128)S(1)} %copy-done.1, s32[8]{0:T(128)S(1)} %copy-done.2, f32[7]{0:T(128)S(1)} %copy-done.3, ...), custom_call_target="tpu_custom_call" | custom-call | flops 1 | bytes 1 | tf_op jit(solution)/shard_map/weights/pallas_call | solution.py:383
  11.3 0.0 collective-permute-done.refs_3_
  11.3 1.6 %collective-permute-start.1 = (f32[2,2,16,128]{3,2,1,0:T(8,128)S(1)}, f32[2,2,16,128]{3,2,1,0:T(8,128)S(1)}, u32[]{:S(2)}, u32[]{:S(2)}) collective-permute-start(f32[2,2,16,128]{3,2,1,0:T(8,128)S(1)} %pad_maximum_fusion.1), channel_id=1, source_target_pairs={{0,8},{4,12},{8,0},{12,4},{16,24},{20,28},{24,16},{28,20},{1,9},{5... | collective-permute-start | bytes 98312 | tf_op jit(solution)/shard_map/ppermute | solution.py:447
  13.0 2.3 %collective-permute-done.1.refs_4_ = f32[2,2,16,128]{3,2,1,0:T(8,128)S(1)} collective-permute-done((f32[2,2,16,128]{3,2,1,0:T(8,128)S(1)}, f32[2,2,16,128]{3,2,1,0:T(8,128)S(1)}, u32[]{:S(2)}, u32[]{:S(2)}) %collective-permute-start.1) | collective-permute-done | bytes 32800 | tf_op jit(solution)/shard_map/ppermute | solution.py:447
  15.3 0.0 collective-permute-start.6
  15.3 0.0 collective-permute-done.2.refs_0_.refs_6_
  15.3 0.0 collective-permute-done.4.refs_2_.refs_1_
  15.3 0.0 collective-permute-done.3.refs_1_.refs_0_
  15.3 0.6 %send_terms.1 = f32[1,2,128,512]{3,2,1,0:T(8,128)S(1)} custom-call(bf16[1,256,768]{2,1,0:T(8,128)(2,1)S(1)} %get-tuple-element.34.wsend_ref, f32[5,8,512]{2,1,0:T(8,128)S(1)} %get-tuple-element.27.nu_ref, f32[1,5,128,512]{3,2,1,0:T(8,128)S(1)} %get-tuple-element.38.q_ref.tile_ref, f32[1,1,128,512]{3,2,1,0:T(8,128)S(1)} %collective-permute-done.2.refs_0_.refs_6_, ...), custom_call_target="tpu_custom_call" | custom-call | flops 1 | bytes 1 | tf_op jit(solution)/shard_map/send_terms/pallas_call | solution.py:453
  15.9 1.6 %collective-permute-start.11 = (f32[1,2,128,512]{3,2,1,0:T(8,128)S(1)}, f32[1,2,128,512]{3,2,1,0:T(8,128)S(1)}, u32[]{:S(2)}, u32[]{:S(2)}) collective-permute-start(f32[1,2,128,512]{3,2,1,0:T(8,128)S(1)} %send_terms.1), channel_id=1, source_target_pairs={{0,2},{1,3},{2,0},{3,1},{4,6},{5,7},{6,4},{7,5},{8,10},{9,11},{10,... | collective-permute-start | bytes 1572872 | tf_op jit(solution)/shard_map/ppermute | solution.py:464
  17.5 2.6 %collective-permute-start.5 = (f32[4,2,16,128]{3,2,1,0:T(8,128)S(1)}, f32[4,2,16,128]{3,2,1,0:T(8,128)S(1)}, u32[]{:S(2)}, u32[]{:S(2)}) collective-permute-start(f32[4,2,16,128]{3,2,1,0:T(8,128)S(1)} %pad_maximum_fusion), channel_id=1, source_target_pairs={{0,16},{4,20},{8,24},{12,28},{16,0},{20,4},{24,8},{28,12},{1,17},{... | collective-permute-start | bytes 196616 | tf_op jit(solution)/shard_map/ppermute | solution.py:447
  20.1 0.0 collective-permute-done.6.near_v_ref
  20.1 0.4 %sibling_terms.2 = f32[1,1,128,512]{3,2,1,0:T(8,128)S(1)} custom-call(bf16[256,768]{1,0:T(8,128)(2,1)S(1)} %get-tuple-element.37.w_ref, f32[5,8,512]{2,1,0:T(8,128)S(1)} %get-tuple-element.27.nu_ref, f32[1,5,128,512]{3,2,1,0:T(8,128)S(1)} %get-tuple-element.38.q_ref.tile_ref, f32[1,1,128,512]{3,2,1,0:T(8,128)S(1)} %collective-permute-done.6.near_v_ref, ...), custom_call_target="tpu_custom_call" | custom-call | flops 1 | bytes 1 | tf_op jit(solution)/shard_map/sibling_terms/pallas_call | solution.py:471
  20.5 0.1 collective-permute-start.7
  20.5 1.8 %collective-permute-done.8.refs_0_.refs_8_ = f32[1,2,128,512]{3,2,1,0:T(8,128)S(1)} collective-permute-done((f32[1,2,128,512]{3,2,1,0:T(8,128)S(1)}, f32[1,2,128,512]{3,2,1,0:T(8,128)S(1)}, u32[]{:S(2)}, u32[]{:S(2)}) %collective-permute-start.8) | collective-permute-done | bytes 524320 | tf_op jit(solution)/shard_map/ppermute | solution.py:348
  22.4 1.7 %collective-permute-done.5.refs_5_ = f32[4,2,16,128]{3,2,1,0:T(8,128)S(1)} collective-permute-done((f32[4,2,16,128]{3,2,1,0:T(8,128)S(1)}, f32[4,2,16,128]{3,2,1,0:T(8,128)S(1)}, u32[]{:S(2)}, u32[]{:S(2)}) %collective-permute-start.5) | collective-permute-done | bytes 65568 | tf_op jit(solution)/shard_map/ppermute | solution.py:447
  24.0 0.6 %sibling_terms.3 = (f32[1,1,128,512]{3,2,1,0:T(8,128)S(1)}, f32[1,1,128,512]{3,2,1,0:T(8,128)S(1)}) custom-call(bf16[256,768]{1,0:T(8,128)(2,1)S(1)} %get-tuple-element.37.w_ref, f32[5,8,512]{2,1,0:T(8,128)S(1)} %get-tuple-element.27.nu_ref, f32[1,5,128,512]{3,2,1,0:T(8,128)S(1)} %get-tuple-element.38.q_ref.tile_ref, ...), custom_call_target="tpu_custom_call" | custom-call | flops 1 | bytes 1 | tf_op jit(solution)/shard_map/sibling_terms/pallas_call | solution.py:471
  24.7 0.1 collective-permute-start.9
  24.8 0.0 copy-start
  24.8 0.0 copy-start.4
  24.8 0.0 copy-start.5
  24.8 0.5 %collective-permute-start.10 = (f32[1,1,128,512]{3,2,1,0:T(8,128)S(1)}, f32[1,1,128,512]{3,2,1,0:T(8,128)S(1)}, u32[]{:S(2)}, u32[]{:S(2)}) collective-permute-start(f32[1,1,128,512]{3,2,1,0:T(8,128)S(1)} %get-tuple-element.42), channel_id=1, source_target_pairs={{0,1},{1,0},{2,3},{3,2},{4,5},{5,4},{6,7},{7,6},{8,9},{9,8},{10,11... | collective-permute-start | bytes 786440 | tf_op jit(solution)/shard_map/ppermute | solution.py:480
  25.3 5.0 %own_terms.1.base_ref = f32[1,5,128,512]{3,2,1,0:T(8,128)S(1)} custom-call(s32[8]{0:T(128)S(1)} %copy-done.1, s32[8]{0:T(128)S(1)} %copy-done.2, f32[7]{0:T(128)S(1)} %copy-done.3, bf16[256,384]{1,0:T(8,128)(2,1)S(1)} %get-tuple-element.35.wown_ref, f32[1,5,128,512]{3,2,1,0:T(8,128)S(1)} %get-tuple-element.38.q_ref.tile_ref, ...), custom_call_target="tpu_custom_call" | custom-call | flops 1 | bytes 1 | tf_op jit(solution)/shard_map/own_terms/pallas_call | solution.py:403
  30.3 0.0 collective-permute-done.7.refs_7_
  30.3 0.0 collective-permute-done.9.refs_9_
  30.3 0.0 collective-permute-done.10.refs_10_
  30.3 0.0 copy-done
  30.3 0.0 copy-done.4
  30.3 0.0 copy-done.5
  30.4 2.4 %near_terms.1 = (f32[1,5,128,512]{3,2,1,0:T(8,128)}, f32[1,2,128,512]{3,2,1,0:T(8,128)S(1)}) custom-call(s32[8]{0:T(128)S(1)} %copy-done.1, s32[2,8]{1,0:T(2,128)S(1)} %bitcast.2, s32[2,8]{1,0:T(2,128)S(1)} %bitcast.3, s32[8]{0:T(128)S(1)} %copy-done.2, f32[6,1024]{1,0:T(8,128)S(1)} %copy-done, bf16[256,384]{1,0:T(8,128)(2,1)S(1)} %get-tuple-element.25.wnear_ref, ...), custom_call_target="tpu_custom_call" | custom-call | flops 1 | bytes 1 | tf_op jit(solution)/shard_map/near_terms/pallas_call | solution.py:486
  32.8 0.0 collective-permute-done.11.refs_0_
  32.8 0.8 %last_terms.1 = f32[1,5,128,512]{3,2,1,0:T(8,128)} custom-call(f32[1,2,128,512]{3,2,1,0:T(8,128)S(1)} %get-tuple-element.43.left_ref, f32[1,2,128,512]{3,2,1,0:T(8,128)S(1)} %collective-permute-done.11.refs_0_, f32[1,5,128,512]{3,2,1,0:T(8,128)} %get-tuple-element.44.refs_1_), custom_call_target="tpu_custom_call", output_to_operand_aliasing={{}: (2, {})} | custom-call | flops 1 | bytes 1 | tf_op jit(solution)/shard_map/last_terms/pallas_call | solution.py:507
  (5 shorter events, 0.1 us)
Async XLA Ops:
  0.0 4.0 %copy-start.2 = (s32[8]{0:T(128)S(1)}, s32[8]{0:T(128)}, u32[]{:S(2)}) copy-start(s32[8]{0:T(128)} %rows_ref.7) | copy-start | bytes 100
  0.0 4.0 %copy-start.1 = (s32[8]{0:T(128)S(1)}, s32[8]{0:T(128)}, u32[]{:S(2)}) copy-start(s32[8]{0:T(128)} %owner_ref.7) | copy-start | bytes 100
  1.0 14.3 %collective-permute-start.2 = (f32[1,1,128,512]{3,2,1,0:T(8,128)S(1)}, f32[1,1,128,512]{3,2,1,0:T(8,128)S(1)}, u32[]{:S(2)}, u32[]{:S(2)}) collective-permute-start(f32[1,1,128,512]{3,2,1,0:T(8,128)S(1)} %part.1.part_ref), channel_id=1, source_target_pairs={{0,2},{1,3},{2,0},{3,1},{4,6},{5,7},{6,4},{7,5},{8,10},{9,11},{10,... | collective-permute-start | bytes 786440 | tf_op jit(solution)/shard_map/ppermute | solution.py:348
  6.1 2.8 %copy-start.3 = (f32[7]{0:T(128)S(1)}, f32[7]{0:T(128)}, u32[]{:S(2)}) copy-start(f32[7]{0:T(128)} %coef_ref.3) | copy-start | bytes 88
  6.1 16.3 %collective-permute-start.8 = (f32[1,2,128,512]{3,2,1,0:T(8,128)S(1)}, f32[1,2,128,512]{3,2,1,0:T(8,128)S(1)}, u32[]{:S(2)}, u32[]{:S(2)}) collective-permute-start(f32[1,2,128,512]{3,2,1,0:T(8,128)S(1)} %slice.15), channel_id=1, source_target_pairs={{0,2},{1,3},{2,0},{3,1},{4,6},{5,7},{6,4},{7,5},{8,10},{9,11},{10,... | collective-permute-start | bytes 1572872 | tf_op jit(solution)/shard_map/ppermute | solution.py:348
  6.2 9.0 %collective-permute-start.4 = (f32[1,1,128,512]{3,2,1,0:T(8,128)S(1)}, f32[1,1,128,512]{3,2,1,0:T(8,128)S(1)}, u32[]{:S(2)}, u32[]{:S(2)}) collective-permute-start(f32[1,1,128,512]{3,2,1,0:T(8,128)S(1)} %get-tuple-element.45), channel_id=1, source_target_pairs={{0,1},{1,0},{2,3},{3,2},{4,5},{5,4},{6,7},{7,6},{8,9},{9,8},{10,11... | collective-permute-start | bytes 786440 | tf_op jit(solution)/shard_map/ppermute | solution.py:376
  6.3 9.0 %collective-permute-start.3 = (f32[1,1,128,512]{3,2,1,0:T(8,128)S(1)}, f32[1,1,128,512]{3,2,1,0:T(8,128)S(1)}, u32[]{:S(2)}, u32[]{:S(2)}) collective-permute-start(f32[1,1,128,512]{3,2,1,0:T(8,128)S(1)} %get-tuple-element.46), channel_id=1, source_target_pairs={{0,1},{1,0},{2,3},{3,2},{4,5},{5,4},{6,7},{7,6},{8,9},{9,8},{10,11... | collective-permute-start | bytes 786440 | tf_op jit(solution)/shard_map/ppermute | solution.py:376
  6.8 4.4 %collective-permute-start = (f32[1,2,16,128]{3,2,1,0:T(8,128)S(1)}, f32[1,2,16,128]{3,2,1,0:T(8,128)S(1)}, u32[]{:S(2)}, u32[]{:S(2)}) collective-permute-start(f32[1,2,16,128]{3,2,1,0:T(8,128)S(1)} %get-tuple-element.29.refs_2_), channel_id=1, source_target_pairs={{0,4},{4,0},{8,12},{12,8},{16,20},{20,16},{24,28},{28,24},{1,5},{5... | collective-permute-start | bytes 49160 | tf_op jit(solution)/shard_map/ppermute | solution.py:447
  11.3 4.0 %collective-permute-start.1 = (f32[2,2,16,128]{3,2,1,0:T(8,128)S(1)}, f32[2,2,16,128]{3,2,1,0:T(8,128)S(1)}, u32[]{:S(2)}, u32[]{:S(2)}) collective-permute-start(f32[2,2,16,128]{3,2,1,0:T(8,128)S(1)} %pad_maximum_fusion.1), channel_id=1, source_target_pairs={{0,8},{4,12},{8,0},{12,4},{16,24},{20,28},{24,16},{28,20},{1,9},{5... | collective-permute-start | bytes 98312 | tf_op jit(solution)/shard_map/ppermute | solution.py:447
  15.3 4.8 %collective-permute-start.6 = (f32[1,1,128,512]{3,2,1,0:T(8,128)S(1)}, f32[1,1,128,512]{3,2,1,0:T(8,128)S(1)}, u32[]{:S(2)}, u32[]{:S(2)}) collective-permute-start(f32[1,1,128,512]{3,2,1,0:T(8,128)S(1)} %slice.14), channel_id=1, source_target_pairs={{0,1},{1,0},{2,3},{3,2},{4,5},{5,4},{6,7},{7,6},{8,9},{9,8},{10,11... | collective-permute-start | bytes 786440 | tf_op jit(solution)/shard_map/ppermute | solution.py:450
  15.9 16.9 %collective-permute-start.11 = (f32[1,2,128,512]{3,2,1,0:T(8,128)S(1)}, f32[1,2,128,512]{3,2,1,0:T(8,128)S(1)}, u32[]{:S(2)}, u32[]{:S(2)}) collective-permute-start(f32[1,2,128,512]{3,2,1,0:T(8,128)S(1)} %send_terms.1), channel_id=1, source_target_pairs={{0,2},{1,3},{2,0},{3,1},{4,6},{5,7},{6,4},{7,5},{8,10},{9,11},{10,... | collective-permute-start | bytes 1572872 | tf_op jit(solution)/shard_map/ppermute | solution.py:464
  17.5 6.6 %collective-permute-start.5 = (f32[4,2,16,128]{3,2,1,0:T(8,128)S(1)}, f32[4,2,16,128]{3,2,1,0:T(8,128)S(1)}, u32[]{:S(2)}, u32[]{:S(2)}) collective-permute-start(f32[4,2,16,128]{3,2,1,0:T(8,128)S(1)} %pad_maximum_fusion), channel_id=1, source_target_pairs={{0,16},{4,20},{8,24},{12,28},{16,0},{20,4},{24,8},{28,12},{1,17},{... | collective-permute-start | bytes 196616 | tf_op jit(solution)/shard_map/ppermute | solution.py:447
  20.5 9.8 %collective-permute-start.7 = (f32[1,1,128,512]{3,2,1,0:T(8,128)S(1)}, f32[1,1,128,512]{3,2,1,0:T(8,128)S(1)}, u32[]{:S(2)}, u32[]{:S(2)}) collective-permute-start(f32[1,1,128,512]{3,2,1,0:T(8,128)S(1)} %sibling_terms.2), channel_id=1, source_target_pairs={{0,1},{1,0},{2,3},{3,2},{4,5},{5,4},{6,7},{7,6},{8,9},{9,8},{10,11... | collective-permute-start | bytes 786440 | tf_op jit(solution)/shard_map/ppermute | solution.py:480
  24.7 5.6 %collective-permute-start.9 = (f32[1,1,128,512]{3,2,1,0:T(8,128)S(1)}, f32[1,1,128,512]{3,2,1,0:T(8,128)S(1)}, u32[]{:S(2)}, u32[]{:S(2)}) collective-permute-start(f32[1,1,128,512]{3,2,1,0:T(8,128)S(1)} %get-tuple-element.41), channel_id=1, source_target_pairs={{0,1},{1,0},{2,3},{3,2},{4,5},{5,4},{6,7},{7,6},{8,9},{9,8},{10,11... | collective-permute-start | bytes 786440 | tf_op jit(solution)/shard_map/ppermute | solution.py:480
  24.8 5.6 %copy-start = (f32[6,1024]{1,0:T(8,128)S(1)}, f32[6,1024]{1,0:T(8,128)}, u32[]{:S(2)}) copy-start(f32[6,1024]{1,0:T(8,128)} %gop_ref.1) | copy-start | bytes 73732
  24.8 5.6 %copy-start.4 = (s32[8,2]{0,1:T(2,128)S(1)}, s32[8,2]{0,1:T(2,128)}, u32[]{:S(2)}) copy-start(s32[8,2]{0,1:T(2,128)} %param.11) | copy-start | bytes 196
  24.8 5.6 %copy-start.5 = (s32[8,2]{0,1:T(2,128)S(1)}, s32[8,2]{0,1:T(2,128)}, u32[]{:S(2)}) copy-start(s32[8,2]{0,1:T(2,128)} %param.12) | copy-start | bytes 196
  24.8 5.5 %collective-permute-start.10 = (f32[1,1,128,512]{3,2,1,0:T(8,128)S(1)}, f32[1,1,128,512]{3,2,1,0:T(8,128)S(1)}, u32[]{:S(2)}, u32[]{:S(2)}) collective-permute-start(f32[1,1,128,512]{3,2,1,0:T(8,128)S(1)} %get-tuple-element.42), channel_id=1, source_target_pairs={{0,1},{1,0},{2,3},{3,2},{4,5},{5,4},{6,7},{7,6},{8,9},{9,8},{10,11... | collective-permute-start | bytes 786440 | tf_op jit(solution)/shard_map/ppermute | solution.py:480
